TPU v7x, 512 devices: a whole 4x4x16 slice. The times are simulated.
512 devices in a mesh: patch: 128 (over z, y_hi, x), batch: 4 (over y_lo, core).
Axes of the slice: x: 4, y: 4 (y_hi: 2, y_lo: 2; y = y_hi * 2 + y_lo), z: 16, core: 2. Of those that a mesh axis runs over, the one named last changes fastest.
Arguments:
- block_input: bfloat16 [128, 128, 640], P('patch', 'batch'), parts along dimension 1, may hold values from -6 to 6
- stale_input: bfloat16 [128, 128, 640], P('patch', 'batch'), parts along dimension 1, may hold values from -6 to 6
- query_weight: bfloat16 [640, 640], replicated, may hold values from -5 to 5
- key_weight: bfloat16 [640, 640], replicated, may hold values from -0.25 to 0.25
- value_weight: bfloat16 [640, 640], replicated, may hold values from -0.25 to 0.25
- out_weight: bfloat16 [640, 640], replicated, may hold values from -0.25 to 0.25
- conv_weight: bfloat16 [9, 640, 320], P(None, 'patch'), may hold values from -0.078125 to 0.078125
Outputs:
- attended: bfloat16 [128, 128, 640], P('patch', 'batch'), parts along dimension 1
- convolved: bfloat16 [128, 128, 320], P('patch', 'batch'), parts along dimension 1
There are 4 independent parts, one for each index of `batch`. A program takes and returns all parts, laid end to end along the dimension named above; an argument that names none is the same for every part. Nothing has to cross between parts.
All inputs are finite; a program needn't handle non-finite values.
Results may differ from a plain program's by a relative error of at most 0.009.
The roundings to bfloat16 on the way count: a program that leaves them out, or rounds other values in their place, can miss the bound.
Values may be sent and summed in bfloat16 or wider, within the bound.
No kernel may reach another device: no remote copies, remote signals or barrier semaphores. Data moves between devices by JAX's collectives and lax.ppermute only.
A program may use at most 64 MiB of HBM per device.

v0:
```python
import jax
import jax.numpy as jnp
from jax import lax
from jax.sharding import PartitionSpec as P

HEADS = 10
HEAD_DIM = 64


def padded_2(block, sides, width):
    for axis, dim in sides:
        count = lax.axis_size(axis)
        forward = [(i, i + 1) for i in range(count - 1)]
        backward = [(target, source) for source, target in forward]
        low = lax.ppermute(
            lax.slice_in_dim(block, block.shape[dim] - width, None, axis=dim), axis, forward
        )
        high = lax.ppermute(lax.slice_in_dim(block, 0, width, axis=dim), axis, backward)
        block = jnp.concatenate([low, block, high], axis=dim)
    return block


def layer_norm(values_in):
    mean = jnp.mean(values_in, axis=-1, keepdims=True)
    centered = values_in - mean
    variance = jnp.mean(centered * centered, axis=-1, keepdims=True)
    return centered * lax.rsqrt(variance + 1e-05)


def accumulate(state_now, query_heads, key_rows, value_rows, masked):
    row_max_old, row_sum_old, weighted_old = state_now
    key_count = key_rows.shape[0]
    head_count = query_heads.shape[1]
    head_size = query_heads.shape[2]
    keys_three = key_rows.reshape(key_count, head_count, head_size)
    values_three = value_rows.reshape(key_count, head_count, head_size)
    scores = jnp.einsum(
        "qhd,khd->hqk", query_heads, keys_three, preferred_element_type=jnp.float32
    ) * head_size ** (-0.5)
    if masked is not None:
        scores = jnp.where(masked[None, None, :], -1e30, scores)
    row_max = jnp.maximum(row_max_old, jnp.max(scores, axis=-1))
    exp_scores = jnp.exp(scores - row_max[:, :, None])
    if masked is not None:
        exp_scores = jnp.where(masked[None, None, :], 0.0, exp_scores)
    factor = jnp.exp(row_max_old - row_max)
    row_sum = row_sum_old * factor + jnp.sum(exp_scores, axis=-1)
    weighted = weighted_old * factor[:, :, None] + jnp.einsum(
        "hqk,khd->hqd",
        exp_scores.astype(jnp.bfloat16),
        values_three,
        preferred_element_type=jnp.float32,
    )
    return (row_max, row_sum, weighted)


def local(
    block_input, stale_input, query_weight, key_weight, value_weight, out_weight, conv_weight
):
    columns = block_input.shape[1]
    channels = block_input.shape[2]
    tokens_flat = block_input.reshape(columns, channels)
    stale_flat = stale_input.reshape(columns, channels)
    normed = layer_norm(tokens_flat.astype(jnp.float32)).astype(jnp.bfloat16)
    stale_normed = layer_norm(stale_flat.astype(jnp.float32)).astype(jnp.bfloat16)
    query = jnp.dot(normed, query_weight, preferred_element_type=jnp.float32).astype(jnp.bfloat16)
    key_fresh = jnp.dot(normed, key_weight, preferred_element_type=jnp.float32).astype(jnp.bfloat16)
    value_fresh = jnp.dot(normed, value_weight, preferred_element_type=jnp.float32).astype(
        jnp.bfloat16
    )
    query_heads = query.reshape(columns, HEADS, HEAD_DIM)
    own_start = lax.axis_index("patch") * columns
    empty_state = (
        jnp.full((HEADS, columns), -1e30, jnp.float32),
        jnp.zeros((HEADS, columns), jnp.float32),
        jnp.zeros((HEADS, columns, HEAD_DIM), jnp.float32),
    )
    initial = accumulate(empty_state, query_heads, key_fresh, value_fresh, None)
    key_stale = jnp.dot(stale_normed, key_weight, preferred_element_type=jnp.float32).astype(
        jnp.bfloat16
    )
    value_stale = jnp.dot(stale_normed, value_weight, preferred_element_type=jnp.float32).astype(
        jnp.bfloat16
    )
    pieces = (
        lax.all_gather(key_stale, "patch", axis=0, tiled=True),
        lax.all_gather(value_stale, "patch", axis=0, tiled=True),
    )
    position = jnp.arange(pieces[0].shape[0], dtype=jnp.int32)
    final_state = accumulate(
        initial,
        query_heads,
        pieces[0],
        pieces[1],
        (position >= own_start) & (position < own_start + columns),
    )
    weighted = final_state[2] / final_state[1][:, :, None]
    mixed = (
        jnp.transpose(weighted, (1, 0, 2)).reshape(columns, HEADS * HEAD_DIM).astype(jnp.bfloat16)
    )
    attended = jnp.dot(mixed, out_weight, preferred_element_type=jnp.float32).astype(jnp.bfloat16)
    activated = jax.nn.silu(block_input.astype(jnp.float32)).astype(jnp.bfloat16)
    stale_activated = jax.nn.silu(stale_input.astype(jnp.float32)).astype(jnp.bfloat16)
    rim_rows = padded_2(stale_activated, (("patch", 0),), 1)
    padded = jnp.concatenate([rim_rows[0:1], activated, rim_rows[2:3]], axis=0)
    padded = jnp.pad(padded, ((0, 0), (1, 1), (0, 0)))
    patches = jnp.concatenate(
        [
            padded[row_off, col_off : col_off + columns, :]
            for row_off in range(3)
            for col_off in range(3)
        ],
        axis=-1,
    )
    all_taps = lax.all_gather(conv_weight, "patch", axis=1, tiled=True)
    out_channels = all_taps.shape[2]
    convolved = jnp.dot(
        patches, all_taps.reshape(9 * channels, out_channels), preferred_element_type=jnp.float32
    ).astype(jnp.bfloat16)
    return (attended.reshape(1, columns, channels), convolved.reshape(1, columns, out_channels))


def solution(mesh):
    placed = (
        P("patch", "batch", None),
        P("patch", "batch", None),
        P(),
        P(),
        P(),
        P(),
        P(None, "patch", None),
    )
    return jax.shard_map(
        local,
        mesh=mesh,
        in_specs=placed,
        out_specs=(P("patch", "batch", None), P("patch", "batch", None)),
        check_vma=False,
    )
```

profile of v0, /device:TPU:1, one launch (start us, length us, event | category | flops | bytes accessed | tf_op | source)
XLA Modules:
  0.0 724.3 jit_solution(404078362208709745)
XLA Ops:
  7.2 1.5 copy.41
  8.8 0.9 fusion.43
  9.7 1.0 fusion.38
  10.7 1.7 convolution_convert_fusion.2
  12.5 2.1 convolution_convert_fusion.1
  14.6 1.3 collective-permute-start.1
  15.9 4.6 collective-permute-start
  20.5 0.9 fusion.34
  21.4 1.0 fusion.29
  22.4 1.5 convolution_convert_fusion.5
  24.1 1.1 convolution_convert_fusion.4
  25.5 1.5 convolution_convert_fusion.3
  27.4 222.0 %all-gather.8.cloned.1.call-done = bf16[9,640,320]{2,0,1:T(8,128)(2,1)} async-done(((bf16[9,5,320]{2,0,1:T(8,128)(2,1)}), bf16[9,640,320]{2,0,1:T(8,128)(2,1)}) %all-gather.8.cloned.1.call-update) | async-done | bytes 3686416 | tf_op jit(solution)/shard_map/all_gather | solution.py:115
  249.4 4.3 copy.42
  253.6 1.4 fusion.17
  255.0 220.5 %all-gather.4.cloned.1.call-done = bf16[4096,640]{1,0:T(8,128)(2,1)} async-done(((bf16[32,640]{1,0:T(8,128)(2,1)}), bf16[4096,640]{1,0:T(8,128)(2,1)}) %all-gather.4.cloned.1.call-update) | async-done | bytes 5242896 | tf_op jit(solution)/shard_map/all_gather | solution.py:86
  475.5 8.0 %copy.37 = bf16[4096,640]{0,1:T(8,128)(2,1)} copy(bf16[4096,640]{1,0:T(8,128)(2,1)} %all-gather.4.cloned.1.call-done) | data formatting | bytes 10485760 | tf_op jit(solution)/shard_map/all_gather | solution.py:86
  483.5 3.7 fusion.70
  487.2 2.2 copy-done.1
  489.4 1.1 fusion.1
  490.5 212.1 %all-gather.6.cloned.1.call-done = bf16[4096,640]{1,0:T(8,128)(2,1)} async-done(((bf16[32,640]{1,0:T(8,128)(2,1)}), bf16[4096,640]{1,0:T(8,128)(2,1)}) %all-gather.6.cloned.1.call-update) | async-done | bytes 5242896 | tf_op jit(solution)/shard_map/all_gather | solution.py:87
  702.7 8.0 %copy.39 = bf16[4096,640]{0,1:T(8,128)(2,1)} copy(bf16[4096,640]{1,0:T(8,128)(2,1)} %all-gather.6.cloned.1.call-done) | data formatting | bytes 10485760 | tf_op jit(solution)/shard_map/all_gather | solution.py:87
  710.6 5.7 fusion.12
  716.9 0.9 fusion.16
  (40 shorter events, 1.6 us)
Async XLA Ops:
  7.2 3.6 copy-start
  7.2 20.1 %copy-start.2 = (bf16[1,32,640]{2,1,0:T(8,128)(2,1)S(1)}, bf16[1,32,640]{2,1,0:T(8,128)(2,1)}, u32[]{:S(2)}) copy-start(bf16[1,32,640]{2,1,0:T(8,128)(2,1)} %param.7) | copy-start | bytes 122884
  7.2 242.2 %all-gather.8.cloned.1.call-start = ((), (), s32[]{:S(2)}) async-start(), calls=%async_computation.2 | async-start | bytes 7925760 | tf_op jit(solution)/shard_map/all_gather | solution.py:115
  8.8 466.7 %all-gather.4.cloned.1.call-start = ((), (), s32[]{:S(2)}) async-start(), calls=%async_computation | async-start | bytes 5283840 | tf_op jit(solution)/shard_map/all_gather | solution.py:86
  12.5 690.2 %all-gather.6.cloned.1.call-start = ((), (), s32[]{:S(2)}) async-start(), calls=%async_computation.1 | async-start | bytes 5283840 | tf_op jit(solution)/shard_map/all_gather | solution.py:87
  14.6 12.5 %collective-permute-start.1 = (bf16[1,32,640]{2,1,0:T(8,128)(2,1)S(1)}, bf16[1,32,640]{2,1,0:T(8,128)(2,1)S(1)}, u32[]{:S(2)}, u32[]{:S(2)}) collective-permute-start(bf16[1,32,640]{2,1,0:T(8,128)(2,1)S(1)} %get-tuple-element.6), channel_id=1, source_target_pairs={{4,0},{8,4},{12,8},{16,12},{20,16},{24,20},{28,24},{32,28},{36,32}... | collective-permute-start | bytes 122888 | tf_op jit(solution)/shard_map/ppermute | solution.py:18
  15.9 11.2 %collective-permute-start = (bf16[1,32,640]{2,1,0:T(8,128)(2,1)S(1)}, bf16[1,32,640]{2,1,0:T(8,128)(2,1)S(1)}, u32[]{:S(2)}, u32[]{:S(2)}) collective-permute-start(bf16[1,32,640]{2,1,0:T(8,128)(2,1)S(1)} %get-tuple-element.6), channel_id=1, source_target_pairs={{0,4},{4,8},{8,12},{12,16},{16,20},{20,24},{24,28},{28,32},{32,36}... | collective-permute-start | bytes 122888 | tf_op jit(solution)/shard_map/ppermute | solution.py:15
  487.2 2.3 copy-start.1
  710.6 6.3 copy-start.3
Sparse Core Ops, SparseCore 0:
  12.6 236.7 all-gather.7
  253.9 221.5 all-gather.3
  480.6 222.0 all-gather.5
where the time goes:
time: 733 us; the launch traced here: 724 us
  waiting for transfers between devices  655 us (89%)
  local copies, waits for them, and re-layouts  24.7 us (3%)
  matrix products  19.9 us (3%)
  between operations  14 us (2%)
    all_gather x1, waiting for transfers between devices, local(): all_taps = lax.all_gather(conv_weight, 'patch', axis=1, tiled=True)  222 us
    all_gather x1, waiting for transfers between devices, local(): lax.all_gather(key_stale, 'patch', axis=0, tiled=True)  220 us
    all_gather x1, waiting for transfers between devices, local(): lax.all_gather(value_stale, 'patch', axis=0, tiled=True)  212 us
  transfers between devices with their start and end apart: 5, of which 3 were waited for; matrix products, arithmetic and copies ran while one was open for 4% of the time, Pallas kernels for 0%

commit v1 on v0

v1 whole, which is shorter than its diff:
```python
import jax
import jax.numpy as jnp
import ml_dtypes
import numpy as np
from jax import lax
from jax.experimental import pallas as pl
from jax.experimental.pallas import tpu as pltpu
from jax.sharding import Mesh, PartitionSpec as P

HEADS = 10
HEAD_DIM = 64
D = 640
CO = 320
COLS = 32
Z = 16
GROUP = 8
OWN = 5
LANES = 128
PAIRS = HEADS // 2
QUERIES = GROUP * COLS
KEYS = Z * COLS
SEND = D + 3 * LANES
BACK = D + LANES + 3 * LANES
VMEM = 24 * 1024 * 1024
F32 = jnp.float32
BF16 = jnp.bfloat16


def slice_matrix():
    out = np.zeros((D, GROUP * LANES), np.float32)
    for j in range(GROUP):
        for z in range(Z):
            for c in range(OWN):
                out[(z * GROUP + j) * OWN + c, LANES * j + 8 * z + c] = 1.0
    return out.astype(ml_dtypes.bfloat16)


def tap_matrix():
    out = np.zeros((3 * LANES, 2 * LANES), np.float32)
    for dx in range(3):
        for z in range(Z):
            for c in range(OWN):
                out[LANES * dx + 8 * z + c, 16 * z + OWN * dx + c] = 1.0
    return out.astype(ml_dtypes.bfloat16)


def layer_norm(values_in):
    mean = jnp.mean(values_in, axis=-1, keepdims=True)
    centered = values_in - mean
    variance = jnp.mean(centered * centered, axis=-1, keepdims=True)
    return (centered * lax.rsqrt(variance + 1e-05)).astype(BF16)


def silu(values_in):
    return (values_in * jax.nn.sigmoid(values_in)).astype(BF16)


def dot(a, b):
    return jnp.dot(a, b, preferred_element_type=F32)


def dot_t(a, b):
    return lax.dot_general(a, b, (((1,), (1,)), ((), ())), preferred_element_type=F32)


def lane_ids(rows):
    return lax.broadcasted_iota(jnp.int32, (rows, LANES), 1)


def prepare_kernel(ids, block, stale, halo, taps, wq, slices, send, query_out, gather, rows):
    query = dot(layer_norm(block[...].astype(F32)), wq[...]).astype(BF16)
    query = query * jnp.array(HEAD_DIM**-0.5, BF16)
    query_out[...] = query
    three = jnp.concatenate(
        [silu(block[...].astype(F32)), silu(stale[...].astype(F32)), silu(halo[...].astype(F32))],
        axis=0,
    )
    cut = dot(three, slices[...]).astype(BF16)
    for j in range(GROUP):
        send[j, :, :D] = query
        for part in range(3):
            send[j, :, D + part * LANES : D + (part + 1) * LANES] = cut[
                part * COLS : (part + 1) * COLS, j * LANES : (j + 1) * LANES
            ]
    gather[:COLS, :] = stale[...]
    core = ids[2]
    rows[...] = jnp.zeros_like(rows)
    for dx in range(3):
        first = jnp.where(core == 0, taps[dx].astype(F32), taps[6 + dx].astype(F32))
        second = jnp.where(core == 0, taps[3 + dx].astype(F32), 0.0)
        rows[OWN * dx : OWN * (dx + 1), :] = jnp.concatenate([first, second], axis=1)
    gather[COLS:, :] = rows[...].astype(BF16)


def attend_pair(query, keys, values, masked, lanes):
    low = lanes < HEAD_DIM
    zero = jnp.zeros_like(query)
    two = jnp.concatenate([jnp.where(low, query, zero), jnp.where(low, zero, query)], axis=0)
    scores = dot_t(two, keys)
    if masked is not None:
        scores = jnp.where(masked, -1e30, scores)
    row_max = jnp.max(scores, axis=-1, keepdims=True)
    exp_scores = jnp.exp(scores - row_max)
    row_sum = jnp.sum(exp_scores, axis=-1, keepdims=True)
    weighted = dot(exp_scores.astype(BF16), values)
    return row_max, row_sum, weighted


def attend_kernel(ids, sent, gathered, wk, wv, back):
    stale = gathered[:, :COLS, :].reshape(KEYS, D)
    normed = layer_norm(stale.astype(F32))
    keys = dot(normed, wk[...]).astype(BF16)
    values = dot(normed, wv[...]).astype(BF16)
    z, j = ids[0], ids[1]
    row = lax.broadcasted_iota(jnp.int32, (2 * QUERIES, KEYS), 0)
    col = lax.broadcasted_iota(jnp.int32, (2 * QUERIES, KEYS), 1)
    masked = (((row // COLS) % GROUP) == j) & ((col // COLS) == z)
    lanes = lane_ids(QUERIES)
    low = lanes < HEAD_DIM
    stats = jnp.zeros((QUERIES, LANES), F32)
    for pair in range(PAIRS):
        at = slice(pair * LANES, (pair + 1) * LANES)
        query = sent[:, :, at].reshape(QUERIES, LANES)
        row_max, row_sum, weighted = attend_pair(query, keys[:, at], values[:, at], masked, lanes)
        weighted = weighted / row_sum
        mixed = jnp.where(low, weighted[:QUERIES], weighted[QUERIES:])
        back[:, :, at] = mixed.astype(BF16).reshape(GROUP, COLS, LANES)
        for half in range(2):
            head = 2 * pair + half
            at_rows = slice(half * QUERIES, (half + 1) * QUERIES)
            stats = jnp.where(lanes == head, row_max[at_rows], stats)
            stats = jnp.where(lanes == 16 + head, row_sum[at_rows], stats)
    high = stats.astype(BF16).astype(F32)
    rest = stats - high
    middle = rest.astype(BF16).astype(F32)
    last = rest - middle
    packed = high + pltpu.roll(middle, 32, 1) + pltpu.roll(last, 64, 1)
    back[:, :, D : D + LANES] = packed.astype(BF16).reshape(GROUP, COLS, LANES)


def convolve_kernel(ids, sent, gathered, other, spread, back_in, back):
    del back_in
    core = ids[2]
    mine = gathered[:, COLS:, :].reshape(Z * 16, D)
    theirs = other[...].reshape(Z * 16, D)
    zero_core = core == 0
    lower_half = jnp.where(zero_core, mine, theirs)
    upper_half = jnp.where(zero_core, theirs, mine)
    weights = (lower_half[:, :CO], lower_half[:, CO:], upper_half[:, :CO])
    active = sent[:, :, :LANES]
    stale = sent[:, :, LANES : 2 * LANES]
    upper = jnp.concatenate([sent[7:8, :, 2 * LANES :], stale[:7]], axis=0)
    lower = jnp.concatenate([stale[1:], sent[0:1, :, 2 * LANES :]], axis=0)
    column = lax.broadcasted_iota(jnp.int32, (QUERIES, LANES), 0) % COLS
    total = jnp.zeros((QUERIES, CO), F32)
    for dy, source in enumerate((upper, active, lower)):
        rows = source.reshape(QUERIES, LANES).astype(F32)
        left = jnp.where(column == 0, 0.0, pltpu.roll(rows, 1, 0))
        right = jnp.where(column == COLS - 1, 0.0, pltpu.roll(rows, QUERIES - 1, 0))
        three = jnp.concatenate([left.astype(BF16), rows.astype(BF16), right.astype(BF16)], axis=1)
        total += dot(dot(three, spread[...]).astype(BF16), weights[dy])
    back[:, :, :CO] = total.astype(BF16).reshape(GROUP, COLS, CO)


def fresh_kernel(block, query, wk, wv, after, weighted_out, stats_out):
    del after
    normed = layer_norm(block[...].astype(F32))
    keys = dot(normed, wk[...]).astype(BF16)
    values = dot(normed, wv[...]).astype(BF16)
    lanes = lane_ids(COLS)
    low = lanes < HEAD_DIM
    stats = jnp.zeros((COLS, LANES), F32)
    for pair in range(PAIRS):
        at = slice(pair * LANES, (pair + 1) * LANES)
        row_max, row_sum, weighted = attend_pair(
            query[:, at], keys[:, at], values[:, at], None, lanes
        )
        weighted_out[:, at] = jnp.where(low, weighted[:COLS], weighted[COLS:])
        for half in range(2):
            head = 2 * pair + half
            at_rows = slice(half * COLS, (half + 1) * COLS)
            stats = jnp.where(lanes == head, row_max[at_rows], stats)
            stats = jnp.where(lanes == 16 + head, row_sum[at_rows], stats)
    stats_out[...] = stats


def finish_kernel(partial, fresh, fresh_stats, wo, attended, convolved):
    total = jnp.zeros((COLS, CO), F32)
    for d in range(GROUP):
        total += partial[d, :, D + LANES : D + LANES + CO].astype(F32)
    convolved[...] = total.astype(BF16)
    stats = []
    for d in range(GROUP):
        packed = partial[d, :, D : D + LANES].astype(F32)
        stats.append(
            packed + pltpu.roll(packed, LANES - 32, 1) + pltpu.roll(packed, LANES - 64, 1)
        )
    stats.append(fresh_stats[...])
    top = stats[0]
    for s in stats[1:]:
        top = jnp.maximum(top, s)
    scale = [jnp.exp(s - top) for s in stats]
    sums = [pltpu.roll(s, LANES - 16, 1) for s in stats]
    parts = [scale[d] * sums[d] for d in range(GROUP)]
    whole = scale[GROUP] * sums[GROUP]
    for p in parts:
        whole = whole + p
    weights = [p / whole for p in parts] + [scale[GROUP] / whole]
    low = lane_ids(COLS) < HEAD_DIM
    mixed = []
    for pair in range(PAIRS):
        at = slice(pair * LANES, (pair + 1) * LANES)
        sum_pair = jnp.zeros((COLS, LANES), F32)
        for d in range(GROUP + 1):
            w = jnp.where(
                low, weights[d][:, 2 * pair : 2 * pair + 1], weights[d][:, 2 * pair + 1 : 2 * pair + 2]
            )
            sum_pair += w * (partial[d, :, at].astype(F32) if d < GROUP else fresh[:, at])
        mixed.append(sum_pair.astype(BF16))
    attended[...] = dot(jnp.concatenate(mixed, axis=1), wo[...]).astype(BF16)


SMEM_SPEC = pl.BlockSpec(memory_space=pltpu.SMEM)
ANY_SPEC = pl.BlockSpec(memory_space=pl.ANY)


def whole(*shape):
    return pl.BlockSpec(shape, lambda i: (0,) * len(shape))


def params():
    return pltpu.CompilerParams(vmem_limit_bytes=VMEM)


def shape(dims, dtype=BF16):
    return jax.ShapeDtypeStruct(dims, dtype)


def local(block_input, stale_input, query_weight, key_weight, value_weight, out_weight, conv_weight):
    block = block_input.reshape(COLS, D)
    stale = stale_input.reshape(COLS, D)
    ids = jnp.stack(
        [lax.axis_index("z"), lax.axis_index(("yh", "x")), lax.axis_index("core")]
    ).astype(jnp.int32)
    pairs = [(GROUP * z + 7, GROUP * (z + 1) + 7) for z in range(Z - 1)]
    pairs += [(GROUP * (z + 1), GROUP * z) for z in range(Z - 1)]
    halo = lax.ppermute(stale, ("z", "yh", "x"), pairs)
    with jax.named_scope("prepare"):
        send, query, payload = pl.pallas_call(
            prepare_kernel,
            out_shape=(shape((GROUP, COLS, SEND)), shape((COLS, D)), shape((COLS + 16, D))),
            in_specs=[SMEM_SPEC] + [pl.BlockSpec(memory_space=pltpu.VMEM)] * 6,
            scratch_shapes=[pltpu.VMEM((16, D), F32)],
            compiler_params=params(),
        )(ids, block, stale, halo, conv_weight, query_weight, jnp.asarray(slice_matrix()))
    sent = lax.all_to_all(send, ("yh", "x"), 0, 0, tiled=True)
    gathered = lax.all_gather(payload, "z", axis=0)
    other = lax.ppermute(gathered[:, COLS:, :], "core", [(0, 1), (1, 0)])
    with jax.named_scope("attend"):
        back = pl.pallas_call(
            attend_kernel,
            grid=(1,),
            out_shape=shape((GROUP, COLS, BACK)),
            in_specs=[
                SMEM_SPEC,
                whole(GROUP, COLS, D),
                whole(Z, COLS + 16, D),
                whole(D, D),
                whole(D, D),
            ],
            out_specs=whole(GROUP, COLS, D + LANES),
            compiler_params=params(),
        )(ids, sent, gathered, key_weight, value_weight)
    with jax.named_scope("convolve"):
        back = pl.pallas_call(
            convolve_kernel,
            grid=(1,),
            out_shape=shape((GROUP, COLS, BACK)),
            in_specs=[
                SMEM_SPEC,
                pl.BlockSpec((pl.Element(GROUP), pl.Element(COLS), pl.Element(3 * LANES)), lambda i: (0, 0, D)),
                pl.BlockSpec((Z, COLS + 16, D), lambda i: (0, 0, 0)),
                pl.BlockSpec((Z, 16, D), lambda i: (0, 0, 0)),
                pl.BlockSpec((3 * LANES, 2 * LANES), lambda i: (0, 0)),
                ANY_SPEC,
            ],
            out_specs=pl.BlockSpec((GROUP, COLS, 3 * LANES), lambda i: (0, 0, 2)),
            input_output_aliases={5: 0},
            compiler_params=params(),
        )(ids, sent, gathered, other, jnp.asarray(tap_matrix()), back)
    partial = lax.all_to_all(back, ("yh", "x"), 0, 0, tiled=True)
    with jax.named_scope("fresh"):
        fresh, fresh_stats = pl.pallas_call(
            fresh_kernel,
            out_shape=(shape((COLS, D), F32), shape((COLS, LANES), F32)),
            in_specs=[pl.BlockSpec(memory_space=pltpu.VMEM)] * 4 + [ANY_SPEC],
            compiler_params=params(),
        )(block, query, key_weight, value_weight, back)
    with jax.named_scope("finish"):
        attended, convolved = pl.pallas_call(
            finish_kernel,
            out_shape=(shape((COLS, D)), shape((COLS, CO))),
            compiler_params=params(),
        )(partial, fresh, fresh_stats, out_weight)
    return attended.reshape(1, COLS, D), convolved.reshape(1, COLS, CO)


def solution(mesh):
    axes = Mesh(mesh.devices.reshape(Z, 2, 4, 2, 2), ("z", "yh", "x", "yl", "core"))
    rows, batch = ("z", "yh", "x"), ("yl", "core")
    placed = P(rows, batch, None)
    return jax.shard_map(
        local,
        mesh=axes,
        in_specs=(placed, placed, P(), P(), P(), P(), P(None, rows, None)),
        out_specs=(placed, placed),
        check_vma=False,
    )
```

time: 733 us -> 95.6 us (0.13); the launches traced: 724 us -> 95 us
  waiting for transfers between devices: 655 us -> 16.1 us
  blocking collectives: 0 us -> 35.6 us
  matrix products: 19.9 us -> 0 us
  local copies, waits for them, and re-layouts: 24.7 us -> 6.28 us
  starting transfers between devices: 5.98 us -> 24.4 us
  between operations: 14 us -> 0.73 us
  Pallas kernels: 0 us -> 11.8 us
    all_gather x3 -> x0, waiting for transfers between devices: 655 us -> none  [the longest x1 222 us: local(): all_taps = lax.all_gather(conv_weight, 'patch', axis=1, tiled=True)]
    all_gather x0 -> x1, blocking collectives: none -> 35.6 us  [local(): gathered = lax.all_gather(payload, 'z', axis=0)]
    all_gather x3 -> x0, local copies, waits for them, and re-layouts: 20.2 us -> none  [the longest x1 7.96 us: local(): lax.all_gather(key_stale, 'patch', axis=0, tiled=True)]
    dot_general x11 -> x0, matrix products: 19.9 us -> none  [the longest x2 5.98 us: accumulate(): jnp.einsum('hqk,khd->hqd', exp_scores.astype(jnp.bfloat16), values_three,...]
    all_to_all x0 -> x2, starting transfers between devices: none -> 12.8 us  [the longest x1 6.51 us: local(): partial = lax.all_to_all(back, ('yh', 'x'), 0, 0, tiled=True)]
    pallas_call x0 -> x5, Pallas kernels: none -> 11.8 us  [the longest x1 5.18 us: local(): pl.pallas_call(attend_kernel, grid=(1,), out_shape=shape((GROUP, COLS, BA...]
    all_to_all x0 -> x2, waiting for transfers between devices: none -> 11.5 us  [the longest x1 11.5 us: local(): partial = lax.all_to_all(back, ('yh', 'x'), 0, 0, tiled=True)]
  transfers between devices with their start and end apart: 5 -> 4, of which waited for: 3 -> 2; matrix products, arithmetic and copies ran while one was open for 4% -> 1% of each run, Pallas kernels for 0% -> 6%
where the time goes in v1:
time: 95.6 us; the launch traced here: 95 us
  blocking collectives  35.6 us (37%)
  starting transfers between devices  24.4 us (26%)
  waiting for transfers between devices  16.1 us (17%)
  Pallas kernels  11.8 us (12%)
  local copies, waits for them, and re-layouts  6.28 us (7%)
    all_gather x1, blocking collectives, local(): gathered = lax.all_gather(payload, 'z', axis=0)  35.6 us
    all_to_all x1, waiting for transfers between devices, local(): partial = lax.all_to_all(back, ('yh', 'x'), 0, 0, tiled=True)  11.5 us
    ppermute x1, starting transfers between devices, local(): other = lax.ppermute(gathered[:, COLS:, :], 'core', [(0, 1), (1, 0)])  10.3 us
    all_to_all x1, starting transfers between devices, local(): partial = lax.all_to_all(back, ('yh', 'x'), 0, 0, tiled=True)  6.51 us
    all_to_all x1, starting transfers between devices, local(): sent = lax.all_to_all(send, ('yh', 'x'), 0, 0, tiled=True)  6.32 us
    unnamed x24, local copies, waits for them, and re-layouts  5.51 us
    pallas_call x1, Pallas kernels, local(): pl.pallas_call(attend_kernel, grid=(1,), out_shape=shape((GROUP, COLS, BA...  5.18 us
    ppermute x1, waiting for transfers between devices, local(): halo = lax.ppermute(stale, ('z', 'yh', 'x'), pairs)  4.59 us
  transfers between devices with their start and end apart: 4, of which 2 were waited for; matrix products, arithmetic and copies ran while one was open for 1% of the time, Pallas kernels for 6%

profile of v1, /device:TPU:1, one launch (start us, length us, event | category | flops | bytes accessed | tf_op | source)
XLA Modules:
  0.0 95.0 jit_solution(11576828649523181045)
XLA Ops:
  0.6 1.3 %collective-permute-start = (bf16[32,640]{1,0:T(8,128)(2,1)}, bf16[32,640]{1,0:T(8,128)(2,1)S(1)}, u32[]{:S(2)}, u32[]{:S(2)}) collective-permute-start(bf16[32,640]{1,0:T(8,128)(2,1)} %bitcast.13), channel_id=1, source_target_pairs={{28,60},{60,92},{92,124},{124,156},{156,188},{188,220},{220,252},{... | collective-permute-start | bytes 122888 | tf_op jit(solution)/shard_map/ppermute | solution.py:247
  1.9 0.1 pad_add_fusion.ids
  2.0 4.6 %collective-permute-done.halo = bf16[32,640]{1,0:T(8,128)(2,1)S(1)} collective-permute-done((bf16[32,640]{1,0:T(8,128)(2,1)}, bf16[32,640]{1,0:T(8,128)(2,1)S(1)}, u32[]{:S(2)}, u32[]{:S(2)}) %collective-permute-start) | collective-permute-done | bytes 40992 | tf_op jit(solution)/shard_map/ppermute | solution.py:247
  6.6 1.3 %copy-done.2 = bf16[640,1024]{1,0:T(8,128)(2,1)S(1)} copy-done((bf16[640,1024]{1,0:T(8,128)(2,1)S(1)}, bf16[640,1024]{1,0:T(8,128)(2,1)}, u32[]{:S(2)}) %copy-start.2) | copy-done | bytes 1310744
  7.9 1.1 %copy-done.3 = bf16[640,640]{1,0:T(8,128)(2,1)S(1)} copy-done((bf16[640,640]{1,0:T(8,128)(2,1)S(1)}, bf16[640,640]{1,0:T(8,128)(2,1)}, u32[]{:S(2)}) %copy-start.3) | copy-done | bytes 819224
  9.1 0.8 copy-done.6
  9.8 0.8 copy-done.8
  10.7 0.8 copy-done.9
  11.4 2.0 %prepare.1 = (bf16[8,32,1024]{2,1,0:T(8,128)(2,1)}, bf16[32,640]{1,0:T(8,128)(2,1)S(1)}, bf16[48,640]{1,0:T(8,128)(2,1)S(1)}) custom-call(s32[3]{0:T(128)S(1)} %pad_add_fusion.ids, bf16[32,640]{1,0:T(8,128)(2,1)S(1)} %bitcast.11, bf16[32,640]{1,0:T(8,128)(2,1)S(1)} %bitcast.14, bf16[32,640]{1,0:T(8,128)(2,1)S(1)} %collective-permute-done.halo, ...), custom_call_target="tpu_custom_call" | custom-call | tf_op jit(solution)/shard_map/prepare/pallas_call | solution.py:249
  13.4 6.3 %all-to-all-start = ((bf16[8,32,1024]{2,1,0:T(8,128)(2,1)}), bf16[8,32,1024]{2,1,0:T(8,128)(2,1)S(1)}, u32[]{:S(2)}, u32[]{:S(2)}) async-start(bf16[8,32,1024]{2,1,0:T(8,128)(2,1)} %get-tuple-element.9), calls=%async_computation | async-start | bytes 1048576 | tf_op jit(solution)/shard_map/all_to_all | solution.py:256
  19.7 35.6 %all-gather = bf16[768,640]{1,0:T(8,128)(2,1)S(1)} all-gather(bf16[48,640]{1,0:T(8,128)(2,1)S(1)} %get-tuple-element.10), channel_id=2, replica_groups=mesh['z'=16,'yh'=2,'x'=4,'yl'=2,'core'=2] {'z'}, dimensions={0}, use_global_device_ids=true | all-gather | bytes 1044480 | tf_op jit(solution)/shard_map/all_gather | solution.py:257
  55.3 0.8 slice.4
  56.1 10.3 %collective-permute-start.1 = (bf16[16,16,640]{2,1,0:T(8,128)(2,1)}, bf16[16,16,640]{2,1,0:T(8,128)(2,1)S(1)}, u32[]{:S(2)}, u32[]{:S(2)}) collective-permute-start(bf16[16,16,640]{2,1,0:T(8,128)(2,1)} %slice.4), channel_id=1, source_target_pairs={{0,1},{1,0},{2,3},{3,2},{4,5},{5,4},{6,7},{7,6},{8,9},{9,8},{10,11... | collective-permute-start | bytes 983048 | tf_op jit(solution)/shard_map/ppermute | solution.py:258
  66.4 0.0 all-to-all-done.sent
  66.4 0.0 copy-start.5
  66.4 5.2 %attend.1.back_in = bf16[8,32,1152]{2,1,0:T(8,128)(2,1)} custom-call(s32[3]{0:T(128)S(1)} %pad_add_fusion.ids, bf16[8,32,1024]{2,1,0:T(8,128)(2,1)S(1)} %all-to-all-done.sent, bf16[16,48,640]{2,1,0:T(8,128)(2,1)S(1)} %bitcast.9, bf16[640,640]{1,0:T(8,128)(2,1)S(1)} %copy-done, bf16[640,640]{1,0:T(8,128)(2,1)S(1)} %copy-done.1), custom_call_target="tpu_custom_call" | custom-call | tf_op jit(solution)/shard_map/attend/pallas_call | solution.py:260
  71.6 0.0 collective-permute-done.1.other
  71.6 0.0 copy-start.11
  71.6 0.7 copy-done.11
  72.3 2.1 %convolve.1.after = bf16[8,32,1152]{2,1,0:T(8,128)(2,1)} custom-call(s32[3]{0:T(128)S(1)} %copy-done.11, bf16[8,32,1024]{2,1,0:T(8,128)(2,1)S(1)} %all-to-all-done.sent, bf16[16,48,640]{2,1,0:T(8,128)(2,1)S(1)} %bitcast.10, bf16[16,16,640]{2,1,0:T(8,128)(2,1)S(1)} %collective-permute-done.1.other, ...), custom_call_target="tpu_custom_call", output_to_operand_aliasing={{}: (5, {})} | custom-call | tf_op jit(solution)/shard_map/convolve/pallas_call | solution.py:275
  74.4 6.5 %all-to-all-start.1 = ((bf16[8,32,1152]{2,1,0:T(8,128)(2,1)}), bf16[8,32,1152]{2,1,0:T(8,128)(2,1)S(1)}, u32[]{:S(2)}, u32[]{:S(2)}) async-start(bf16[8,32,1152]{2,1,0:T(8,128)(2,1)} %convolve.1.after), calls=%async_computation.1 | async-start | bytes 1179648 | tf_op jit(solution)/shard_map/all_to_all | solution.py:291
  80.9 1.0 %fresh.1 = (f32[32,640]{1,0:T(8,128)S(1)}, f32[32,128]{1,0:T(8,128)S(1)}) custom-call(bf16[32,640]{1,0:T(8,128)(2,1)S(1)} %bitcast.12, bf16[32,640]{1,0:T(8,128)(2,1)S(1)} %get-tuple-element.11.query, bf16[640,640]{1,0:T(8,128)(2,1)S(1)} %copy-done, bf16[640,640]{1,0:T(8,128)(2,1)S(1)} %copy-done.1, bf16[8,32,1152]{2,1,0:T(8,128)(2,1)} %convolve.1.after), custom_call_target="tpu_custom_call" | custom-call | tf_op jit(solution)/shard_map/fresh/pallas_call | solution.py:293
  81.9 11.5 %all-to-all-done.1.partial = bf16[8,32,1152]{2,1,0:T(8,128)(2,1)S(1)} async-done(((bf16[8,32,1152]{2,1,0:T(8,128)(2,1)}), bf16[8,32,1152]{2,1,0:T(8,128)(2,1)S(1)}, u32[]{:S(2)}, u32[]{:S(2)}) %all-to-all-start.1) | async-done | bytes 589856 | tf_op jit(solution)/shard_map/all_to_all | solution.py:291
  93.4 1.6 %finish.1 = (bf16[32,640]{1,0:T(8,128)(2,1)}, bf16[32,320]{1,0:T(8,128)(2,1)}) custom-call(bf16[8,32,1152]{2,1,0:T(8,128)(2,1)S(1)} %all-to-all-done.1.partial, f32[32,640]{1,0:T(8,128)S(1)} %get-tuple-element.12.fresh, f32[32,128]{1,0:T(8,128)S(1)} %get-tuple-element.13.fresh_stats, bf16[640,640]{1,0:T(8,128)(2,1)S(1)} %copy-done.4), custom_call_target="tpu_custom_call" | custom-call | tf_op jit(solution)/shard_map/finish/pallas_call | solution.py:300
  (16 shorter events, 0.0 us)
Async XLA Ops:
  0.6 6.0 %collective-permute-start = (bf16[32,640]{1,0:T(8,128)(2,1)}, bf16[32,640]{1,0:T(8,128)(2,1)S(1)}, u32[]{:S(2)}, u32[]{:S(2)}) collective-permute-start(bf16[32,640]{1,0:T(8,128)(2,1)} %bitcast.13), channel_id=1, source_target_pairs={{28,60},{60,92},{92,124},{124,156},{156,188},{188,220},{220,252},{... | collective-permute-start | bytes 122888 | tf_op jit(solution)/shard_map/ppermute | solution.py:247
  2.0 64.4 %copy-start.10 = (s32[3]{0:T(128)}, s32[3]{0:T(128)S(1)}, u32[]{:S(2)}) copy-start(s32[3]{0:T(128)S(1)} %pad_add_fusion.ids) | copy-start | bytes 40
  6.6 1.3 %copy-start.2 = (bf16[640,1024]{1,0:T(8,128)(2,1)S(1)}, bf16[640,1024]{1,0:T(8,128)(2,1)}, u32[]{:S(2)}) copy-start(bf16[640,1024]{1,0:T(8,128)(2,1)} %constant.24.clone.slices) | copy-start | bytes 3932164
  7.9 1.1 %copy-start.3 = (bf16[640,640]{1,0:T(8,128)(2,1)S(1)}, bf16[640,640]{1,0:T(8,128)(2,1)}, u32[]{:S(2)}) copy-start(bf16[640,640]{1,0:T(8,128)(2,1)} %wq.1) | copy-start | bytes 2457604
  9.1 0.8 copy-start.6
  9.8 0.8 copy-start.8
  10.7 0.8 copy-start.9
  13.4 53.0 %copy-start = (bf16[640,640]{1,0:T(8,128)(2,1)S(1)}, bf16[640,640]{1,0:T(8,128)(2,1)}, u32[]{:S(2)}) copy-start(bf16[640,640]{1,0:T(8,128)(2,1)} %wk.3) | copy-start | bytes 2457604
  13.4 53.0 %copy-start.1 = (bf16[640,640]{1,0:T(8,128)(2,1)S(1)}, bf16[640,640]{1,0:T(8,128)(2,1)}, u32[]{:S(2)}) copy-start(bf16[640,640]{1,0:T(8,128)(2,1)} %wv.3) | copy-start | bytes 2457604
  13.4 52.9 %all-to-all-start = ((bf16[8,32,1024]{2,1,0:T(8,128)(2,1)}), bf16[8,32,1024]{2,1,0:T(8,128)(2,1)S(1)}, u32[]{:S(2)}, u32[]{:S(2)}) async-start(bf16[8,32,1024]{2,1,0:T(8,128)(2,1)} %get-tuple-element.9), calls=%async_computation | async-start | bytes 1048576 | tf_op jit(solution)/shard_map/all_to_all | solution.py:256
  56.1 15.5 %collective-permute-start.1 = (bf16[16,16,640]{2,1,0:T(8,128)(2,1)}, bf16[16,16,640]{2,1,0:T(8,128)(2,1)S(1)}, u32[]{:S(2)}, u32[]{:S(2)}) collective-permute-start(bf16[16,16,640]{2,1,0:T(8,128)(2,1)} %slice.4), channel_id=1, source_target_pairs={{0,1},{1,0},{2,3},{3,2},{4,5},{5,4},{6,7},{7,6},{8,9},{9,8},{10,11... | collective-permute-start | bytes 983048 | tf_op jit(solution)/shard_map/ppermute | solution.py:258
  66.4 5.2 %copy-start.5 = (bf16[384,256]{1,0:T(8,128)(2,1)S(1)}, bf16[384,256]{1,0:T(8,128)(2,1)}, u32[]{:S(2)}) copy-start(bf16[384,256]{1,0:T(8,128)(2,1)} %constant.25.clone.spread) | copy-start | bytes 589828
  71.6 9.3 %copy-start.7 = (bf16[1,32,640]{2,1,0:T(8,128)(2,1)S(1)}, bf16[1,32,640]{2,1,0:T(8,128)(2,1)}, u32[]{:S(2)}) copy-start(bf16[1,32,640]{2,1,0:T(8,128)(2,1)} %param.9) | copy-start | bytes 122884
  71.6 0.7 copy-start.11
  74.4 19.0 %all-to-all-start.1 = ((bf16[8,32,1152]{2,1,0:T(8,128)(2,1)}), bf16[8,32,1152]{2,1,0:T(8,128)(2,1)S(1)}, u32[]{:S(2)}, u32[]{:S(2)}) async-start(bf16[8,32,1152]{2,1,0:T(8,128)(2,1)} %convolve.1.after), calls=%async_computation.1 | async-start | bytes 1179648 | tf_op jit(solution)/shard_map/all_to_all | solution.py:291
  80.9 12.5 %copy-start.4 = (bf16[640,640]{1,0:T(8,128)(2,1)S(1)}, bf16[640,640]{1,0:T(8,128)(2,1)}, u32[]{:S(2)}) copy-start(bf16[640,640]{1,0:T(8,128)(2,1)} %wo.1) | copy-start | bytes 2457604

commit v2 on v1

v2 whole, which is shorter than its diff:
```python
import jax
import jax.numpy as jnp
import ml_dtypes
import numpy as np
from jax import lax
from jax.experimental import pallas as pl
from jax.experimental.pallas import tpu as pltpu
from jax.sharding import Mesh, PartitionSpec as P

HEADS = 10
HEAD_DIM = 64
D = 640
CO = 320
COLS = 32
Z = 16
GROUP = 8
OWN = 5
LANES = 128
PAIRS = HEADS // 2
QUERIES = GROUP * COLS
KEYS = Z * COLS
SEND = D + 3 * LANES
BACK = D + 3 * LANES
STATS_AT = (64, 84, 104)
VMEM = 24 * 1024 * 1024
F32 = jnp.float32
BF16 = jnp.bfloat16


def slice_matrix():
    out = np.zeros((D, GROUP * LANES), np.float32)
    for j in range(GROUP):
        for z in range(Z):
            for c in range(OWN):
                out[(z * GROUP + j) * OWN + c, LANES * j + 8 * z + c] = 1.0
    return out.astype(ml_dtypes.bfloat16)


def tap_matrix():
    out = np.zeros((3 * LANES, 2 * LANES), np.float32)
    for dx in range(3):
        for z in range(Z):
            for c in range(OWN):
                out[LANES * dx + 8 * z + c, 16 * z + OWN * dx + c] = 1.0
    return out.astype(ml_dtypes.bfloat16)


def layer_norm(values_in):
    mean = jnp.mean(values_in, axis=-1, keepdims=True)
    centered = values_in - mean
    variance = jnp.mean(centered * centered, axis=-1, keepdims=True)
    return (centered * lax.rsqrt(variance + 1e-05)).astype(BF16)


def silu(values_in):
    return (values_in * jax.nn.sigmoid(values_in)).astype(BF16)


def dot(a, b):
    return jnp.dot(a, b, preferred_element_type=F32)


def dot_t(a, b):
    return lax.dot_general(a, b, (((1,), (1,)), ((), ())), preferred_element_type=F32)


def lane_ids(rows):
    return lax.broadcasted_iota(jnp.int32, (rows, LANES), 1)


def place():
    return lax.axis_index("z"), lax.axis_index("yh") * 4 + lax.axis_index("x")


def payload_kernel(stale_hbm, taps_hbm, gather, stale, taps, rows, sems):
    copies = [
        pltpu.make_async_copy(taps_hbm, taps, sems.at[0]),
        pltpu.make_async_copy(stale_hbm, stale, sems.at[1]),
    ]
    for copy in copies:
        copy.start()
    core = lax.axis_index("core")
    rows[...] = jnp.zeros_like(rows)
    copies[0].wait()
    for dx in range(3):
        first = jnp.where(core == 0, taps[dx].astype(F32), taps[6 + dx].astype(F32))
        second = jnp.where(core == 0, taps[3 + dx].astype(F32), 0.0)
        rows[OWN * dx : OWN * (dx + 1), :] = jnp.concatenate([first, second], axis=1)
    gather[COLS:, :] = rows[...].astype(BF16)
    copies[1].wait()
    gather[:COLS, :] = stale[...]


def prepare_kernel(block, gathered, wq, slices, send, query_out):
    z, j = place()
    query = dot(layer_norm(block[...].astype(F32)), wq[...]).astype(BF16)
    query = query * jnp.array(HEAD_DIM**-0.5, BF16)
    query_out[...] = query
    stale = gathered[z, :COLS, :]
    beside = jnp.where(j == 0, jnp.minimum(z + 1, Z - 1), jnp.maximum(z - 1, 0))
    outside = ((j == 0) & (z == Z - 1)) | ((j != 0) & (z == 0))
    halo = gathered[beside, :COLS, :].astype(F32) * jnp.where(outside, 0.0, 1.0)
    three = jnp.concatenate(
        [silu(block[...].astype(F32)), silu(stale.astype(F32)), silu(halo)], axis=0
    )
    cut = dot(three, slices[...]).astype(BF16)
    for j in range(GROUP):
        send[j, :, :D] = query
        for part in range(3):
            send[j, :, D + part * LANES : D + (part + 1) * LANES] = cut[
                part * COLS : (part + 1) * COLS, j * LANES : (j + 1) * LANES
            ]


def project_kernel(gathered, wk, wv, after, keys, values):
    del after
    normed = layer_norm(gathered[:, :COLS, :].reshape(KEYS, D).astype(F32))
    keys[...] = dot(normed, wk[...]).astype(BF16)
    values[...] = dot(normed, wv[...]).astype(BF16)


def attend_pair(query, keys, values, masked, lanes):
    low = lanes < HEAD_DIM
    zero = jnp.zeros_like(query)
    two = jnp.concatenate([jnp.where(low, query, zero), jnp.where(low, zero, query)], axis=0)
    scores = dot_t(two, keys)
    if masked is not None:
        scores = jnp.where(masked, -1e30, scores)
    row_max = jnp.max(scores, axis=-1, keepdims=True)
    exp_scores = jnp.exp(scores - row_max)
    row_sum = jnp.sum(exp_scores, axis=-1, keepdims=True)
    weighted = dot(exp_scores.astype(BF16), values)
    return row_max, row_sum, weighted


def convolve(sent, gathered, other, spread):
    mine = gathered[:, COLS:, :].reshape(Z * 16, D)
    theirs = other[...].reshape(Z * 16, D)
    zero_core = lax.axis_index("core") == 0
    lower_half = jnp.where(zero_core, mine, theirs)
    upper_half = jnp.where(zero_core, theirs, mine)
    weights = (lower_half[:, :CO], lower_half[:, CO:], upper_half[:, :CO])
    active = sent[:, :, D : D + LANES]
    stale = sent[:, :, D + LANES : D + 2 * LANES]
    upper = jnp.concatenate([sent[7:8, :, D + 2 * LANES :], stale[:7]], axis=0)
    lower = jnp.concatenate([stale[1:], sent[0:1, :, D + 2 * LANES :]], axis=0)
    column = lax.broadcasted_iota(jnp.int32, (QUERIES, LANES), 0) % COLS
    total = jnp.zeros((QUERIES, CO), F32)
    for dy, source in enumerate((upper, active, lower)):
        rows = source.reshape(QUERIES, LANES).astype(F32)
        left = jnp.where(column == 0, 0.0, pltpu.roll(rows, 1, 0))
        right = jnp.where(column == COLS - 1, 0.0, pltpu.roll(rows, QUERIES - 1, 0))
        three = jnp.concatenate([left.astype(BF16), rows.astype(BF16), right.astype(BF16)], axis=1)
        total += dot(dot(three, spread[...]).astype(BF16), weights[dy])
    return total


def attend_kernel(sent, keys, values, gathered, other, spread, back):
    z, j = place()
    row = lax.broadcasted_iota(jnp.int32, (2 * QUERIES, KEYS), 0)
    col = lax.broadcasted_iota(jnp.int32, (2 * QUERIES, KEYS), 1)
    masked = (((row // COLS) % GROUP) == j) & ((col // COLS) == z)
    lanes = lane_ids(QUERIES)
    low = lanes < HEAD_DIM
    stats = jnp.zeros((QUERIES, LANES), F32)
    for pair in range(PAIRS):
        at = slice(pair * LANES, (pair + 1) * LANES)
        query = sent[:, :, at].reshape(QUERIES, LANES)
        row_max, row_sum, weighted = attend_pair(query, keys[:, at], values[:, at], masked, lanes)
        weighted = weighted / row_sum
        mixed = jnp.where(low, weighted[:QUERIES], weighted[QUERIES:])
        back[:, :, at] = mixed.astype(BF16).reshape(GROUP, COLS, LANES)
        for half in range(2):
            head = 2 * pair + half
            at_rows = slice(half * QUERIES, (half + 1) * QUERIES)
            stats = jnp.where(lanes == head, row_max[at_rows], stats)
            stats = jnp.where(lanes == HEADS + head, row_sum[at_rows], stats)
    high = stats.astype(BF16).astype(F32)
    rest = stats - high
    middle = rest.astype(BF16).astype(F32)
    last = rest - middle
    packed = sum(pltpu.roll(term, at, 1) for term, at in zip((high, middle, last), STATS_AT))
    total = convolve(sent, gathered, other, spread)
    back[:, :, D : D + 2 * LANES] = (
        total[:, : 2 * LANES].astype(BF16).reshape(GROUP, COLS, 2 * LANES)
    )
    tail = jnp.concatenate([total[:, 2 * LANES :], packed[:, CO - 2 * LANES :]], axis=1)
    back[:, :, D + 2 * LANES :] = tail.astype(BF16).reshape(GROUP, COLS, LANES)


def fresh_kernel(block, query, wk, wv, after, weighted_out, stats_out):
    del after
    normed = layer_norm(block[...].astype(F32))
    keys = dot(normed, wk[...]).astype(BF16)
    values = dot(normed, wv[...]).astype(BF16)
    lanes = lane_ids(COLS)
    low = lanes < HEAD_DIM
    stats = jnp.zeros((COLS, LANES), F32)
    for pair in range(PAIRS):
        at = slice(pair * LANES, (pair + 1) * LANES)
        row_max, row_sum, weighted = attend_pair(
            query[:, at], keys[:, at], values[:, at], None, lanes
        )
        weighted_out[:, at] = jnp.where(low, weighted[:COLS], weighted[COLS:])
        for half in range(2):
            head = 2 * pair + half
            at_rows = slice(half * COLS, (half + 1) * COLS)
            stats = jnp.where(lanes == head, row_max[at_rows], stats)
            stats = jnp.where(lanes == HEADS + head, row_sum[at_rows], stats)
    stats_out[...] = stats


def finish_kernel(partial, fresh, fresh_stats, wo, attended, convolved):
    total = jnp.zeros((COLS, CO), F32)
    for d in range(GROUP):
        total += partial[d, :, D : D + CO].astype(F32)
    convolved[...] = total.astype(BF16)
    stats = []
    for d in range(GROUP):
        packed = partial[d, :, D + 2 * LANES :].astype(F32)
        terms = sum(pltpu.roll(packed, LANES - at, 1) for at in STATS_AT)
        stats.append(jnp.where(lane_ids(COLS) < 2 * HEADS, terms, 0.0))
    stats.append(fresh_stats[...])
    top = stats[0]
    for s in stats[1:]:
        top = jnp.maximum(top, s)
    scale = [jnp.exp(s - top) for s in stats]
    sums = [pltpu.roll(s, LANES - HEADS, 1) for s in stats]
    parts = [scale[d] * sums[d] for d in range(GROUP)]
    whole = scale[GROUP] * sums[GROUP]
    for p in parts:
        whole = whole + p
    weights = [p / whole for p in parts] + [scale[GROUP] / whole]
    low = lane_ids(COLS) < HEAD_DIM
    mixed = []
    for pair in range(PAIRS):
        at = slice(pair * LANES, (pair + 1) * LANES)
        sum_pair = jnp.zeros((COLS, LANES), F32)
        for d in range(GROUP + 1):
            w = jnp.where(
                low, weights[d][:, 2 * pair : 2 * pair + 1], weights[d][:, 2 * pair + 1 : 2 * pair + 2]
            )
            sum_pair += w * (partial[d, :, at].astype(F32) if d < GROUP else fresh[:, at])
        mixed.append(sum_pair.astype(BF16))
    attended[...] = dot(jnp.concatenate(mixed, axis=1), wo[...]).astype(BF16)


ANY_SPEC = pl.BlockSpec(memory_space=pl.ANY)
HBM_SPEC = pl.BlockSpec(memory_space=pltpu.HBM)


def params():
    return pltpu.CompilerParams(vmem_limit_bytes=VMEM)


def shape(dims, dtype=BF16):
    return jax.ShapeDtypeStruct(dims, dtype)


def local(block_input, stale_input, query_weight, key_weight, value_weight, out_weight, conv_weight):
    block = block_input.reshape(COLS, D)
    stale = stale_input.reshape(COLS, D)
    with jax.named_scope("payload"):
        payload = pl.pallas_call(
            payload_kernel,
            out_shape=shape((COLS + 16, D)),
            in_specs=[HBM_SPEC] * 2,
            scratch_shapes=[
                pltpu.VMEM((COLS, D), BF16),
                pltpu.VMEM((9, OWN, CO), BF16),
                pltpu.VMEM((16, D), F32),
                pltpu.SemaphoreType.DMA((2,)),
            ],
            compiler_params=params(),
        )(stale, conv_weight)
    gathered = lax.all_gather(payload, "z", axis=0)
    with jax.named_scope("prepare"):
        send, query = pl.pallas_call(
            prepare_kernel,
            out_shape=(shape((GROUP, COLS, SEND)), shape((COLS, D))),
            compiler_params=params(),
        )(block, gathered, query_weight, jnp.asarray(slice_matrix()))
    sent = lax.all_to_all(send, ("yh", "x"), 0, 0, tiled=True)
    other = lax.ppermute(gathered[:, COLS:, :], "core", [(0, 1), (1, 0)])
    with jax.named_scope("project"):
        keys, values = pl.pallas_call(
            project_kernel,
            out_shape=(shape((KEYS, D)), shape((KEYS, D))),
            in_specs=[pl.BlockSpec(memory_space=pltpu.VMEM)] * 3 + [ANY_SPEC],
            compiler_params=params(),
        )(gathered, key_weight, value_weight, send)
    with jax.named_scope("attend"):
        back = pl.pallas_call(
            attend_kernel,
            out_shape=shape((GROUP, COLS, BACK)),
            compiler_params=params(),
        )(sent, keys, values, gathered, other, jnp.asarray(tap_matrix()))
    partial = lax.all_to_all(back, ("yh", "x"), 0, 0, tiled=True)
    with jax.named_scope("fresh"):
        fresh, fresh_stats = pl.pallas_call(
            fresh_kernel,
            out_shape=(shape((COLS, D), F32), shape((COLS, LANES), F32)),
            in_specs=[pl.BlockSpec(memory_space=pltpu.VMEM)] * 4 + [ANY_SPEC],
            compiler_params=params(),
        )(block, query, key_weight, value_weight, back)
    with jax.named_scope("finish"):
        attended, convolved = pl.pallas_call(
            finish_kernel,
            out_shape=(shape((COLS, D)), shape((COLS, CO))),
            compiler_params=params(),
        )(partial, fresh, fresh_stats, out_weight)
    return attended.reshape(1, COLS, D), convolved.reshape(1, COLS, CO)


def solution(mesh):
    axes = Mesh(mesh.devices.reshape(Z, 2, 4, 2, 2), ("z", "yh", "x", "yl", "core"))
    rows, batch = ("z", "yh", "x"), ("yl", "core")
    placed = P(rows, batch, None)
    return jax.shard_map(
        local,
        mesh=axes,
        in_specs=(placed, placed, P(), P(), P(), P(), P(None, rows, None)),
        out_specs=(placed, placed),
        check_vma=False,
    )
```

time: 95.6 us -> 88.4 us (0.925)
  waiting for transfers between devices: 16.1 us -> 10.6 us
  Pallas kernels: 11.8 us -> 9.3 us
  local copies, waits for them, and re-layouts: 6.28 us -> 8.61 us
    ppermute x1 -> x0, waiting for transfers between devices: 4.59 us -> none  [local(): halo = lax.ppermute(stale, ('z', 'yh', 'x'), pairs)]
    unnamed x24 -> x28, local copies, waits for them, and re-layouts: 5.51 us -> 8.58 us
    pallas_call x2 -> x3, Pallas kernels: 7.29 us -> 5.3 us  [the longest x1 3.49 us: local(): pl.pallas_call(attend_kernel, out_shape=shape((GROUP, COLS, BACK)), compi...]
    ppermute x1 -> x0, starting transfers between devices: 1.29 us -> none  [local(): halo = lax.ppermute(stale, ('z', 'yh', 'x'), pairs)]
  transfers between devices with their start and end apart: 4 -> 3, of which waited for: 2 -> 1; matrix products, arithmetic and copies ran while one was open for 1% -> 0% of each run, Pallas kernels for 6% -> 3%
where the time goes in v2:
time: 88.4 us; the launch traced here: 87.8 us
  blocking collectives  35 us (40%)
  starting transfers between devices  23.5 us (27%)
  waiting for transfers between devices  10.6 us (12%)
  Pallas kernels  9.3 us (11%)
  local copies, waits for them, and re-layouts  8.61 us (10%)
    all_gather x1, blocking collectives, local(): gathered = lax.all_gather(payload, 'z', axis=0)  35 us
    all_to_all x1, waiting for transfers between devices, local(): partial = lax.all_to_all(back, ('yh', 'x'), 0, 0, tiled=True)  10.6 us
    ppermute x1, starting transfers between devices, local(): other = lax.ppermute(gathered[:, COLS:, :], 'core', [(0, 1), (1, 0)])  9.78 us
    unnamed x28, local copies, waits for them, and re-layouts  8.58 us
    all_to_all x1, starting transfers between devices, local(): partial = lax.all_to_all(back, ('yh', 'x'), 0, 0, tiled=True)  6.93 us
    all_to_all x1, starting transfers between devices, local(): sent = lax.all_to_all(send, ('yh', 'x'), 0, 0, tiled=True)  6.78 us
    pallas_call x1, Pallas kernels, local(): pl.pallas_call(attend_kernel, out_shape=shape((GROUP, COLS, BACK)), compi...  3.49 us
  transfers between devices with their start and end apart: 3, of which 1 were waited for; matrix products, arithmetic and copies ran while one was open for 0% of the time, Pallas kernels for 3%

profile of v2, /device:TPU:1, one launch (start us, length us, event | category | flops | bytes accessed | tf_op | source)
XLA Modules:
  0.0 87.8 jit_solution(3270675889354974836)
XLA Ops:
  0.6 0.0 copy-start.3
  0.7 0.9 %copy-done.12 = bf16[9,5,320]{2,1,0:T(8,128)(2,1)S(1)} copy-done((bf16[9,5,320]{2,1,0:T(8,128)(2,1)S(1)}, bf16[9,5,320]{2,1,0:T(8,128)(2,1)}, u32[]{:S(2)}) %copy-start.12) | copy-done | bytes 28824
  1.5 0.8 copy-done.13
  2.3 0.2 payload.1
  2.5 35.0 %all-gather = bf16[768,640]{1,0:T(8,128)(2,1)S(1)} all-gather(bf16[48,640]{1,0:T(8,128)(2,1)S(1)} %payload.1), channel_id=2, replica_groups=mesh['z'=16,'yh'=2,'x'=4,'yl'=2,'core'=2] {'z'}, dimensions={0}, use_global_device_ids=true | all-gather | bytes 1044480 | tf_op jit(solution)/shard_map/all_gather | solution.py:276
  37.5 1.3 %copy-done.2 = bf16[640,1024]{1,0:T(8,128)(2,1)S(1)} copy-done((bf16[640,1024]{1,0:T(8,128)(2,1)S(1)}, bf16[640,1024]{1,0:T(8,128)(2,1)}, u32[]{:S(2)}) %copy-start.2) | copy-done | bytes 1310744
  38.8 0.8 copy-done.10
  39.6 1.4 %prepare.1 = (bf16[8,32,1024]{2,1,0:T(8,128)(2,1)}, bf16[32,640]{1,0:T(8,128)(2,1)S(1)}) custom-call(bf16[32,640]{1,0:T(8,128)(2,1)S(1)} %bitcast.9, bf16[16,48,640]{2,1,0:T(8,128)(2,1)S(1)} %bitcast.5, bf16[640,640]{1,0:T(8,128)(2,1)S(1)} %copy-done.3, bf16[640,1024]{1,0:T(8,128)(2,1)S(1)} %copy-done.2), custom_call_target="tpu_custom_call" | custom-call | tf_op jit(solution)/shard_map/prepare/pallas_call | solution.py:278
  41.1 6.8 %all-to-all-start = ((bf16[8,32,1024]{2,1,0:T(8,128)(2,1)}), bf16[8,32,1024]{2,1,0:T(8,128)(2,1)S(1)}, u32[]{:S(2)}, u32[]{:S(2)}) async-start(bf16[8,32,1024]{2,1,0:T(8,128)(2,1)} %get-tuple-element.10.after), calls=%async_computation | async-start | bytes 1048576 | tf_op jit(solution)/shard_map/all_to_all | solution.py:283
  47.9 9.8 %collective-permute-start = (bf16[16,16,640]{2,1,0:T(8,128)(2,1)S(1)}, bf16[16,16,640]{2,1,0:T(8,128)(2,1)S(1)}, u32[]{:S(2)}, u32[]{:S(2)}) collective-permute-start(bf16[16,16,640]{2,1,0:T(8,128)(2,1)S(1)} %slice.4), channel_id=1, source_target_pairs={{0,1},{1,0},{2,3},{3,2},{4,5},{5,4},{6,7},{7,6},{8,9},{9,8},{10,11... | collective-permute-start | bytes 983048 | tf_op jit(solution)/shard_map/ppermute | solution.py:284
  57.7 1.6 %project.1 = (bf16[512,640]{1,0:T(8,128)(2,1)S(1)}, bf16[512,640]{1,0:T(8,128)(2,1)S(1)}) custom-call(bf16[16,48,640]{2,1,0:T(8,128)(2,1)S(1)} %bitcast.7, bf16[640,640]{1,0:T(8,128)(2,1)S(1)} %copy-done, bf16[640,640]{1,0:T(8,128)(2,1)S(1)} %copy-done.1, bf16[8,32,1024]{2,1,0:T(8,128)(2,1)} %get-tuple-element.10.after), custom_call_target="tpu_custom_call" | custom-call | tf_op jit(solution)/shard_map/project/pallas_call | solution.py:286
  59.3 0.0 copy-start.5
  59.3 0.9 copy-done.5
  60.2 0.8 copy-done.7
  61.0 0.0 collective-permute-done.other
  61.0 0.0 all-to-all-done.sent
  61.0 1.1 %copy-done.6 = bf16[512,640]{1,0:T(8,128)(2,1)S(1)} copy-done((bf16[512,640]{1,0:T(8,128)(2,1)S(1)}, bf16[512,640]{1,0:T(8,128)(2,1)}, u32[]{:S(2)}) %copy-start.6) | copy-done | bytes 655384
  62.1 1.1 %copy-done.8 = bf16[512,640]{1,0:T(8,128)(2,1)S(1)} copy-done((bf16[512,640]{1,0:T(8,128)(2,1)S(1)}, bf16[512,640]{1,0:T(8,128)(2,1)}, u32[]{:S(2)}) %copy-start.8) | copy-done | bytes 655384
  63.2 0.9 %copy-done.9 = bf16[384,256]{1,0:T(8,128)(2,1)S(1)} copy-done((bf16[384,256]{1,0:T(8,128)(2,1)S(1)}, bf16[384,256]{1,0:T(8,128)(2,1)}, u32[]{:S(2)}) %copy-start.9) | copy-done | bytes 196632
  64.1 3.5 %attend.1.after = bf16[8,32,1024]{2,1,0:T(8,128)(2,1)} custom-call(bf16[8,32,1024]{2,1,0:T(8,128)(2,1)S(1)} %all-to-all-done.sent, bf16[512,640]{1,0:T(8,128)(2,1)S(1)} %copy-done.6, bf16[512,640]{1,0:T(8,128)(2,1)S(1)} %copy-done.8, bf16[16,48,640]{2,1,0:T(8,128)(2,1)S(1)} %bitcast.8, bf16[16,16,640]{2,1,0:T(8,128)(2,1)S(1)} %collective-permute-done.other, ...), custom_call_target="tpu_custom_call" | custom-call | tf_op jit(solution)/shard_map/attend/pallas_call | solution.py:293
  67.6 6.9 %all-to-all-start.1 = ((bf16[8,32,1024]{2,1,0:T(8,128)(2,1)}), bf16[8,32,1024]{2,1,0:T(8,128)(2,1)S(1)}, u32[]{:S(2)}, u32[]{:S(2)}) async-start(bf16[8,32,1024]{2,1,0:T(8,128)(2,1)} %attend.1.after), calls=%async_computation.1 | async-start | bytes 1048576 | tf_op jit(solution)/shard_map/all_to_all | solution.py:298
  74.6 1.0 %fresh.1 = (f32[32,640]{1,0:T(8,128)S(1)}, f32[32,128]{1,0:T(8,128)S(1)}) custom-call(bf16[32,640]{1,0:T(8,128)(2,1)S(1)} %bitcast.10, bf16[32,640]{1,0:T(8,128)(2,1)S(1)} %get-tuple-element.13.query, bf16[640,640]{1,0:T(8,128)(2,1)S(1)} %copy-done, bf16[640,640]{1,0:T(8,128)(2,1)S(1)} %copy-done.1, bf16[8,32,1024]{2,1,0:T(8,128)(2,1)} %attend.1.after), custom_call_target="tpu_custom_call" | custom-call | tf_op jit(solution)/shard_map/fresh/pallas_call | solution.py:300
  75.5 10.6 %all-to-all-done.1.partial = bf16[8,32,1024]{2,1,0:T(8,128)(2,1)S(1)} async-done(((bf16[8,32,1024]{2,1,0:T(8,128)(2,1)}), bf16[8,32,1024]{2,1,0:T(8,128)(2,1)S(1)}, u32[]{:S(2)}, u32[]{:S(2)}) %all-to-all-start.1) | async-done | bytes 524320 | tf_op jit(solution)/shard_map/all_to_all | solution.py:298
  86.2 1.6 %finish.1 = (bf16[32,640]{1,0:T(8,128)(2,1)}, bf16[32,320]{1,0:T(8,128)(2,1)}) custom-call(bf16[8,32,1024]{2,1,0:T(8,128)(2,1)S(1)} %all-to-all-done.1.partial, f32[32,640]{1,0:T(8,128)S(1)} %get-tuple-element.14.fresh, f32[32,128]{1,0:T(8,128)S(1)} %get-tuple-element.15.fresh_stats, bf16[640,640]{1,0:T(8,128)(2,1)S(1)} %copy-done.4), custom_call_target="tpu_custom_call" | custom-call | tf_op jit(solution)/shard_map/finish/pallas_call | solution.py:307
  (18 shorter events, 0.1 us)
Async XLA Ops:
  0.6 36.9 %copy-start.3 = (bf16[640,640]{1,0:T(8,128)(2,1)S(1)}, bf16[640,640]{1,0:T(8,128)(2,1)}, u32[]{:S(2)}) copy-start(bf16[640,640]{1,0:T(8,128)(2,1)} %wq.1) | copy-start | bytes 2457604
  0.6 0.9 %copy-start.12 = (bf16[9,5,320]{2,1,0:T(8,128)(2,1)S(1)}, bf16[9,5,320]{2,1,0:T(8,128)(2,1)}, u32[]{:S(2)}) copy-start(bf16[9,5,320]{2,1,0:T(8,128)(2,1)} %taps_hbm.1) | copy-start | bytes 86404
  1.5 0.8 copy-start.13
  37.5 1.3 %copy-start.2 = (bf16[640,1024]{1,0:T(8,128)(2,1)S(1)}, bf16[640,1024]{1,0:T(8,128)(2,1)}, u32[]{:S(2)}) copy-start(bf16[640,1024]{1,0:T(8,128)(2,1)} %constant.4.clone.slices) | copy-start | bytes 3932164
  38.8 0.8 copy-start.10
  41.1 16.6 %copy-start = (bf16[640,640]{1,0:T(8,128)(2,1)S(1)}, bf16[640,640]{1,0:T(8,128)(2,1)}, u32[]{:S(2)}) copy-start(bf16[640,640]{1,0:T(8,128)(2,1)} %wk.3) | copy-start | bytes 2457604
  41.1 16.6 %copy-start.1 = (bf16[640,640]{1,0:T(8,128)(2,1)S(1)}, bf16[640,640]{1,0:T(8,128)(2,1)}, u32[]{:S(2)}) copy-start(bf16[640,640]{1,0:T(8,128)(2,1)} %wv.3) | copy-start | bytes 2457604
  41.1 20.0 %all-to-all-start = ((bf16[8,32,1024]{2,1,0:T(8,128)(2,1)}), bf16[8,32,1024]{2,1,0:T(8,128)(2,1)S(1)}, u32[]{:S(2)}, u32[]{:S(2)}) async-start(bf16[8,32,1024]{2,1,0:T(8,128)(2,1)} %get-tuple-element.10.after), calls=%async_computation | async-start | bytes 1048576 | tf_op jit(solution)/shard_map/all_to_all | solution.py:283
  47.9 13.1 %collective-permute-start = (bf16[16,16,640]{2,1,0:T(8,128)(2,1)S(1)}, bf16[16,16,640]{2,1,0:T(8,128)(2,1)S(1)}, u32[]{:S(2)}, u32[]{:S(2)}) collective-permute-start(bf16[16,16,640]{2,1,0:T(8,128)(2,1)S(1)} %slice.4), channel_id=1, source_target_pairs={{0,1},{1,0},{2,3},{3,2},{4,5},{5,4},{6,7},{7,6},{8,9},{9,8},{10,11... | collective-permute-start | bytes 983048 | tf_op jit(solution)/shard_map/ppermute | solution.py:284
  59.3 0.9 copy-start.5
  60.2 0.8 copy-start.7
  61.0 1.1 %copy-start.6 = (bf16[512,640]{1,0:T(8,128)(2,1)S(1)}, bf16[512,640]{1,0:T(8,128)(2,1)}, u32[]{:S(2)}) copy-start(bf16[512,640]{1,0:T(8,128)(2,1)} %copy-done.5) | copy-start | bytes 1966084
  62.1 1.1 %copy-start.8 = (bf16[512,640]{1,0:T(8,128)(2,1)S(1)}, bf16[512,640]{1,0:T(8,128)(2,1)}, u32[]{:S(2)}) copy-start(bf16[512,640]{1,0:T(8,128)(2,1)} %copy-done.7) | copy-start | bytes 1966084
  63.2 0.9 %copy-start.9 = (bf16[384,256]{1,0:T(8,128)(2,1)S(1)}, bf16[384,256]{1,0:T(8,128)(2,1)}, u32[]{:S(2)}) copy-start(bf16[384,256]{1,0:T(8,128)(2,1)} %constant.5.clone.spread) | copy-start | bytes 589828
  64.1 10.4 %copy-start.11 = (bf16[1,32,640]{2,1,0:T(8,128)(2,1)S(1)}, bf16[1,32,640]{2,1,0:T(8,128)(2,1)}, u32[]{:S(2)}) copy-start(bf16[1,32,640]{2,1,0:T(8,128)(2,1)} %param.9) | copy-start | bytes 122884
  67.6 18.5 %all-to-all-start.1 = ((bf16[8,32,1024]{2,1,0:T(8,128)(2,1)}), bf16[8,32,1024]{2,1,0:T(8,128)(2,1)S(1)}, u32[]{:S(2)}, u32[]{:S(2)}) async-start(bf16[8,32,1024]{2,1,0:T(8,128)(2,1)} %attend.1.after), calls=%async_computation.1 | async-start | bytes 1048576 | tf_op jit(solution)/shard_map/all_to_all | solution.py:298
  74.6 11.6 %copy-start.4 = (bf16[640,640]{1,0:T(8,128)(2,1)S(1)}, bf16[640,640]{1,0:T(8,128)(2,1)}, u32[]{:S(2)}) copy-start(bf16[640,640]{1,0:T(8,128)(2,1)} %wo.1) | copy-start | bytes 2457604

commit v3 on v2

--- a/solution.py
+++ b/solution.py
@@ -22,7 +22,9 @@
 SEND = D + 3 * LANES
 BACK = D + 3 * LANES
 STATS_AT = (64, 84, 104)
-VMEM = 24 * 1024 * 1024
+WIDE = 60
+NARROW = 24
+ATTEND = 52
 F32 = jnp.float32
 BF16 = jnp.bfloat16
 
@@ -37,12 +39,11 @@
 
 
 def tap_matrix():
-    out = np.zeros((3 * LANES, 2 * LANES), np.float32)
-    for dx in range(3):
-        for z in range(Z):
-            for c in range(OWN):
-                out[LANES * dx + 8 * z + c, 16 * z + OWN * dx + c] = 1.0
-    return out.astype(ml_dtypes.bfloat16)
+    row = lax.broadcasted_iota(jnp.int32, (3 * LANES, 2 * LANES), 0)
+    col = lax.broadcasted_iota(jnp.int32, (3 * LANES, 2 * LANES), 1)
+    z, c = (row % LANES) // 8, row % 8
+    target = 16 * z + OWN * (row // LANES) + c
+    return jnp.where((c < OWN) & (col == target), 1.0, 0.0).astype(BF16)
 
 
 def layer_norm(values_in):
@@ -91,17 +92,19 @@
     gather[:COLS, :] = stale[...]
 
 
-def prepare_kernel(block, gathered, wq, slices, send, query_out):
+def prepare_kernel(block, stale, gathered, wq, slices, send, query_out, halo_rows, sem):
     z, j = place()
+    beside = jnp.where(j == 0, jnp.minimum(z + 1, Z - 1), jnp.maximum(z - 1, 0))
+    fetch = pltpu.make_async_copy(gathered.at[beside, pl.ds(0, COLS), :], halo_rows, sem)
+    fetch.start()
     query = dot(layer_norm(block[...].astype(F32)), wq[...]).astype(BF16)
     query = query * jnp.array(HEAD_DIM**-0.5, BF16)
     query_out[...] = query
-    stale = gathered[z, :COLS, :]
-    beside = jnp.where(j == 0, jnp.minimum(z + 1, Z - 1), jnp.maximum(z - 1, 0))
     outside = ((j == 0) & (z == Z - 1)) | ((j != 0) & (z == 0))
-    halo = gathered[beside, :COLS, :].astype(F32) * jnp.where(outside, 0.0, 1.0)
+    fetch.wait()
+    halo = halo_rows[...].astype(F32) * jnp.where(outside, 0.0, 1.0)
     three = jnp.concatenate(
-        [silu(block[...].astype(F32)), silu(stale.astype(F32)), silu(halo)], axis=0
+        [silu(block[...].astype(F32)), silu(stale[...].astype(F32)), silu(halo)], axis=0
     )
     cut = dot(three, slices[...]).astype(BF16)
     for j in range(GROUP):
@@ -112,11 +115,11 @@
             ]
 
 
-def project_kernel(gathered, wk, wv, after, keys, values):
+def project_kernel(gathered, wk, wv, after, both):
     del after
     normed = layer_norm(gathered[:, :COLS, :].reshape(KEYS, D).astype(F32))
-    keys[...] = dot(normed, wk[...]).astype(BF16)
-    values[...] = dot(normed, wv[...]).astype(BF16)
+    both[:, :D] = dot(normed, wk[...]).astype(BF16)
+    both[:, D:] = dot(normed, wv[...]).astype(BF16)
 
 
 def attend_pair(query, keys, values, masked, lanes):
@@ -133,7 +136,8 @@
     return row_max, row_sum, weighted
 
 
-def convolve(sent, gathered, other, spread):
+def convolve(sent, gathered, other):
+    spread = tap_matrix()
     mine = gathered[:, COLS:, :].reshape(Z * 16, D)
     theirs = other[...].reshape(Z * 16, D)
     zero_core = lax.axis_index("core") == 0
@@ -151,11 +155,11 @@
         left = jnp.where(column == 0, 0.0, pltpu.roll(rows, 1, 0))
         right = jnp.where(column == COLS - 1, 0.0, pltpu.roll(rows, QUERIES - 1, 0))
         three = jnp.concatenate([left.astype(BF16), rows.astype(BF16), right.astype(BF16)], axis=1)
-        total += dot(dot(three, spread[...]).astype(BF16), weights[dy])
+        total += dot(dot(three, spread).astype(BF16), weights[dy])
     return total
 
 
-def attend_kernel(sent, keys, values, gathered, other, spread, back):
+def attend_kernel(sent, both, gathered, other, back):
     z, j = place()
     row = lax.broadcasted_iota(jnp.int32, (2 * QUERIES, KEYS), 0)
     col = lax.broadcasted_iota(jnp.int32, (2 * QUERIES, KEYS), 1)
@@ -166,7 +170,8 @@
     for pair in range(PAIRS):
         at = slice(pair * LANES, (pair + 1) * LANES)
         query = sent[:, :, at].reshape(QUERIES, LANES)
-        row_max, row_sum, weighted = attend_pair(query, keys[:, at], values[:, at], masked, lanes)
+        keys, values = both[:, at], both[:, D + pair * LANES : D + (pair + 1) * LANES]
+        row_max, row_sum, weighted = attend_pair(query, keys, values, masked, lanes)
         weighted = weighted / row_sum
         mixed = jnp.where(low, weighted[:QUERIES], weighted[QUERIES:])
         back[:, :, at] = mixed.astype(BF16).reshape(GROUP, COLS, LANES)
@@ -180,7 +185,7 @@
     middle = rest.astype(BF16).astype(F32)
     last = rest - middle
     packed = sum(pltpu.roll(term, at, 1) for term, at in zip((high, middle, last), STATS_AT))
-    total = convolve(sent, gathered, other, spread)
+    total = convolve(sent, gathered, other)
     back[:, :, D : D + 2 * LANES] = (
         total[:, : 2 * LANES].astype(BF16).reshape(GROUP, COLS, 2 * LANES)
     )
@@ -246,11 +251,12 @@
 
 
 ANY_SPEC = pl.BlockSpec(memory_space=pl.ANY)
+VMEM_SPEC = pl.BlockSpec(memory_space=pltpu.VMEM)
 HBM_SPEC = pl.BlockSpec(memory_space=pltpu.HBM)
 
 
-def params():
-    return pltpu.CompilerParams(vmem_limit_bytes=VMEM)
+def params(mib):
+    return pltpu.CompilerParams(vmem_limit_bytes=mib * 1024 * 1024)
 
 
 def shape(dims, dtype=BF16):
@@ -271,43 +277,45 @@
                 pltpu.VMEM((16, D), F32),
                 pltpu.SemaphoreType.DMA((2,)),
             ],
-            compiler_params=params(),
+            compiler_params=params(WIDE),
         )(stale, conv_weight)
     gathered = lax.all_gather(payload, "z", axis=0)
     with jax.named_scope("prepare"):
         send, query = pl.pallas_call(
             prepare_kernel,
             out_shape=(shape((GROUP, COLS, SEND)), shape((COLS, D))),
-            compiler_params=params(),
-        )(block, gathered, query_weight, jnp.asarray(slice_matrix()))
+            in_specs=[VMEM_SPEC, VMEM_SPEC, HBM_SPEC, VMEM_SPEC, VMEM_SPEC],
+            scratch_shapes=[pltpu.VMEM((COLS, D), BF16), pltpu.SemaphoreType.DMA],
+            compiler_params=params(WIDE),
+        )(block, stale, gathered, query_weight, jnp.asarray(slice_matrix()))
     sent = lax.all_to_all(send, ("yh", "x"), 0, 0, tiled=True)
     other = lax.ppermute(gathered[:, COLS:, :], "core", [(0, 1), (1, 0)])
     with jax.named_scope("project"):
-        keys, values = pl.pallas_call(
+        both = pl.pallas_call(
             project_kernel,
-            out_shape=(shape((KEYS, D)), shape((KEYS, D))),
-            in_specs=[pl.BlockSpec(memory_space=pltpu.VMEM)] * 3 + [ANY_SPEC],
-            compiler_params=params(),
+            out_shape=shape((KEYS, 2 * D)),
+            in_specs=[VMEM_SPEC] * 3 + [ANY_SPEC],
+            compiler_params=params(WIDE),
         )(gathered, key_weight, value_weight, send)
     with jax.named_scope("attend"):
         back = pl.pallas_call(
             attend_kernel,
             out_shape=shape((GROUP, COLS, BACK)),
-            compiler_params=params(),
-        )(sent, keys, values, gathered, other, jnp.asarray(tap_matrix()))
+            compiler_params=params(ATTEND),
+        )(sent, both, gathered, other)
     partial = lax.all_to_all(back, ("yh", "x"), 0, 0, tiled=True)
     with jax.named_scope("fresh"):
         fresh, fresh_stats = pl.pallas_call(
             fresh_kernel,
             out_shape=(shape((COLS, D), F32), shape((COLS, LANES), F32)),
-            in_specs=[pl.BlockSpec(memory_space=pltpu.VMEM)] * 4 + [ANY_SPEC],
-            compiler_params=params(),
+            in_specs=[VMEM_SPEC] * 4 + [ANY_SPEC],
+            compiler_params=params(NARROW),
         )(block, query, key_weight, value_weight, back)
     with jax.named_scope("finish"):
         attended, convolved = pl.pallas_call(
             finish_kernel,
             out_shape=(shape((COLS, D)), shape((COLS, CO))),
-            compiler_params=params(),
+            compiler_params=params(NARROW),
         )(partial, fresh, fresh_stats, out_weight)
     return attended.reshape(1, COLS, D), convolved.reshape(1, COLS, CO)
 

time: 88.4 us -> 91.5 us (1.035)
  Pallas kernels: 9.3 us -> 17.4 us
  local copies, waits for them, and re-layouts: 8.61 us -> 1.02 us
  blocking collectives: 35 us -> 37.9 us
    unnamed x28 -> x10, local copies, waits for them, and re-layouts: 8.58 us -> 0.02 us
    all_gather x1, blocking collectives: 35 us -> 37.9 us  [local(): gathered = lax.all_gather(payload, 'z', axis=0)]
    pallas_call x1, Pallas kernels: 1.6 us -> 4.38 us  [local(): pl.pallas_call(project_kernel, out_shape=shape((KEYS, 2 * D)), in_specs=[...]
    pallas_call x1, Pallas kernels: 1.45 us -> 3.61 us  [local(): pl.pallas_call(prepare_kernel, out_shape=(shape((GROUP, COLS, SEND)), sha...]
    pallas_call x1, Pallas kernels: 3.49 us -> 5.28 us  [local(): pl.pallas_call(attend_kernel, out_shape=shape((GROUP, COLS, BACK)), compi...]
    pallas_call x1, Pallas kernels: 0.2 us -> 1.56 us  [local(): pl.pallas_call(payload_kernel, out_shape=shape((COLS + 16, D)), in_specs=...]
    slice x1, local copies, waits for them, and re-layouts: 0.03 us -> 1 us  [local(): other = lax.ppermute(gathered[:, COLS:, :], 'core', [(0, 1), (1, 0)])]
  transfers between devices with their start and end apart: 3 -> 3, of which waited for: 1 -> 1; matrix products, arithmetic and copies ran while one was open for 0% -> 1% of each run, Pallas kernels for 3% -> 6%
where the time goes in v3:
time: 91.5 us; the launch traced here: 91 us
  blocking collectives  37.9 us (41%)
  starting transfers between devices  23.2 us (25%)
  Pallas kernels  17.4 us (19%)
  waiting for transfers between devices  10.8 us (12%)
  local copies, waits for them, and re-layouts  1.02 us (1%)
    all_gather x1, blocking collectives, local(): gathered = lax.all_gather(payload, 'z', axis=0)  37.9 us
    all_to_all x1, waiting for transfers between devices, local(): partial = lax.all_to_all(back, ('yh', 'x'), 0, 0, tiled=True)  10.8 us
    ppermute x1, starting transfers between devices, local(): other = lax.ppermute(gathered[:, COLS:, :], 'core', [(0, 1), (1, 0)])  9.49 us
    all_to_all x1, starting transfers between devices, local(): partial = lax.all_to_all(back, ('yh', 'x'), 0, 0, tiled=True)  7.06 us
    all_to_all x1, starting transfers between devices, local(): sent = lax.all_to_all(send, ('yh', 'x'), 0, 0, tiled=True)  6.67 us
    pallas_call x1, Pallas kernels, local(): pl.pallas_call(attend_kernel, out_shape=shape((GROUP, COLS, BACK)), compi...  5.28 us
    pallas_call x1, Pallas kernels, local(): pl.pallas_call(project_kernel, out_shape=shape((KEYS, 2 * D)), in_specs=[...  4.38 us
    pallas_call x1, Pallas kernels, local(): pl.pallas_call(prepare_kernel, out_shape=(shape((GROUP, COLS, SEND)), sha...  3.61 us
  transfers between devices with their start and end apart: 3, of which 1 were waited for; matrix products, arithmetic and copies ran while one was open for 1% of the time, Pallas kernels for 6%

profile of v3, /device:TPU:1, one launch (start us, length us, event | category | flops | bytes accessed | tf_op | source)
XLA Modules:
  0.0 91.0 jit_solution(11021549679571347166)
XLA Ops:
  0.6 1.6 %payload.1 = bf16[48,640]{1,0:T(8,128)(2,1)} custom-call(bf16[32,640]{1,0:T(8,128)(2,1)} %bitcast.11, bf16[9,5,320]{2,1,0:T(8,128)(2,1)} %taps_hbm.1), custom_call_target="tpu_custom_call" | custom-call | tf_op jit(solution)/shard_map/payload/pallas_call | solution.py:270
  2.2 37.9 %all-gather = bf16[768,640]{1,0:T(8,128)(2,1)} all-gather(bf16[48,640]{1,0:T(8,128)(2,1)} %payload.1), channel_id=2, replica_groups=mesh['z'=16,'yh'=2,'x'=4,'yl'=2,'core'=2] {'z'}, dimensions={0}, use_global_device_ids=true | all-gather | bytes 1044480 | tf_op jit(solution)/shard_map/all_gather | solution.py:282
  40.1 3.6 %prepare.1 = (bf16[8,32,1024]{2,1,0:T(8,128)(2,1)}, bf16[32,640]{1,0:T(8,128)(2,1)}) custom-call(bf16[32,640]{1,0:T(8,128)(2,1)} %bitcast.5, bf16[32,640]{1,0:T(8,128)(2,1)} %bitcast.12, bf16[16,48,640]{2,1,0:T(8,128)(2,1)} %bitcast.7, bf16[640,640]{1,0:T(8,128)(2,1)} %wq.1, bf16[640,1024]{1,0:T(8,128)(2,1)} %constant.2.clone.slices), custom_call_target="tpu_custom_call" | custom-call | tf_op jit(solution)/shard_map/prepare/pallas_call | solution.py:284
  43.7 6.7 %all-to-all-start = ((bf16[8,32,1024]{2,1,0:T(8,128)(2,1)}), bf16[8,32,1024]{2,1,0:T(8,128)(2,1)S(1)}, u32[]{:S(2)}, u32[]{:S(2)}) async-start(bf16[8,32,1024]{2,1,0:T(8,128)(2,1)} %get-tuple-element.8.after), calls=%async_computation | async-start | bytes 1048576 | tf_op jit(solution)/shard_map/all_to_all | solution.py:291
  50.3 1.0 %slice.4 = bf16[16,16,640]{2,1,0:T(8,128)(2,1)S(1)} slice(bf16[16,48,640]{2,1,0:T(8,128)(2,1)} %bitcast.8), slice={[0:16], [32:48], [0:640]} | slice | bytes 655360 | tf_op jit(solution)/shard_map/slice | solution.py:292
  51.4 9.5 %collective-permute-start = (bf16[16,16,640]{2,1,0:T(8,128)(2,1)S(1)}, bf16[16,16,640]{2,1,0:T(8,128)(2,1)S(1)}, u32[]{:S(2)}, u32[]{:S(2)}) collective-permute-start(bf16[16,16,640]{2,1,0:T(8,128)(2,1)S(1)} %slice.4), channel_id=1, source_target_pairs={{0,1},{1,0},{2,3},{3,2},{4,5},{5,4},{6,7},{7,6},{8,9},{9,8},{10,11... | collective-permute-start | bytes 983048 | tf_op jit(solution)/shard_map/ppermute | solution.py:292
  60.8 4.4 %project.1.both = bf16[512,1280]{1,0:T(8,128)(2,1)} custom-call(bf16[16,48,640]{2,1,0:T(8,128)(2,1)} %bitcast.9, bf16[640,640]{1,0:T(8,128)(2,1)} %wk.3, bf16[640,640]{1,0:T(8,128)(2,1)} %wv.3, bf16[8,32,1024]{2,1,0:T(8,128)(2,1)} %get-tuple-element.8.after), custom_call_target="tpu_custom_call" | custom-call | tf_op jit(solution)/shard_map/project/pallas_call | solution.py:294
  65.2 0.0 copy-start.3
  65.2 0.0 copy-start.4
  65.2 0.0 collective-permute-done.other
  65.2 0.0 all-to-all-done.sent
  65.2 0.0 copy-start.1
  65.3 5.3 %attend.1.after = bf16[8,32,1024]{2,1,0:T(8,128)(2,1)} custom-call(bf16[8,32,1024]{2,1,0:T(8,128)(2,1)S(1)} %all-to-all-done.sent, bf16[512,1280]{1,0:T(8,128)(2,1)} %project.1.both, bf16[16,48,640]{2,1,0:T(8,128)(2,1)} %bitcast.10, bf16[16,16,640]{2,1,0:T(8,128)(2,1)S(1)} %collective-permute-done.other), custom_call_target="tpu_custom_call" | custom-call | tf_op jit(solution)/shard_map/attend/pallas_call | solution.py:301
  70.5 0.0 copy-start
  70.5 7.1 %all-to-all-start.1 = ((bf16[8,32,1024]{2,1,0:T(8,128)(2,1)}), bf16[8,32,1024]{2,1,0:T(8,128)(2,1)S(1)}, u32[]{:S(2)}, u32[]{:S(2)}) async-start(bf16[8,32,1024]{2,1,0:T(8,128)(2,1)} %attend.1.after), calls=%async_computation.1 | async-start | bytes 1048576 | tf_op jit(solution)/shard_map/all_to_all | solution.py:306
  77.6 0.0 copy-start.2
  77.6 0.0 copy-done.3
  77.6 0.0 copy-done.4
  77.6 0.0 copy-done.1
  77.6 0.0 copy-done
  77.6 1.0 %fresh.1 = (f32[32,640]{1,0:T(8,128)S(1)}, f32[32,128]{1,0:T(8,128)S(1)}) custom-call(bf16[32,640]{1,0:T(8,128)(2,1)S(1)} %bitcast.6, bf16[32,640]{1,0:T(8,128)(2,1)S(1)} %copy-done.4, bf16[640,640]{1,0:T(8,128)(2,1)S(1)} %copy-done, bf16[640,640]{1,0:T(8,128)(2,1)S(1)} %copy-done.1, bf16[8,32,1024]{2,1,0:T(8,128)(2,1)} %attend.1.after), custom_call_target="tpu_custom_call" | custom-call | tf_op jit(solution)/shard_map/fresh/pallas_call | solution.py:308
  78.6 10.8 %all-to-all-done.1.partial = bf16[8,32,1024]{2,1,0:T(8,128)(2,1)S(1)} async-done(((bf16[8,32,1024]{2,1,0:T(8,128)(2,1)}), bf16[8,32,1024]{2,1,0:T(8,128)(2,1)S(1)}, u32[]{:S(2)}, u32[]{:S(2)}) %all-to-all-start.1) | async-done | bytes 524320 | tf_op jit(solution)/shard_map/all_to_all | solution.py:306
  89.4 0.0 copy-done.2
  89.4 1.6 %finish.1 = (bf16[32,640]{1,0:T(8,128)(2,1)}, bf16[32,320]{1,0:T(8,128)(2,1)}) custom-call(bf16[8,32,1024]{2,1,0:T(8,128)(2,1)S(1)} %all-to-all-done.1.partial, f32[32,640]{1,0:T(8,128)S(1)} %get-tuple-element.10.fresh, f32[32,128]{1,0:T(8,128)S(1)} %get-tuple-element.11.fresh_stats, bf16[640,640]{1,0:T(8,128)(2,1)S(1)} %copy-done.2), custom_call_target="tpu_custom_call" | custom-call | tf_op jit(solution)/shard_map/finish/pallas_call | solution.py:315
Async XLA Ops:
  43.7 21.6 %all-to-all-start = ((bf16[8,32,1024]{2,1,0:T(8,128)(2,1)}), bf16[8,32,1024]{2,1,0:T(8,128)(2,1)S(1)}, u32[]{:S(2)}, u32[]{:S(2)}) async-start(bf16[8,32,1024]{2,1,0:T(8,128)(2,1)} %get-tuple-element.8.after), calls=%async_computation | async-start | bytes 1048576 | tf_op jit(solution)/shard_map/all_to_all | solution.py:291
  51.4 13.9 %collective-permute-start = (bf16[16,16,640]{2,1,0:T(8,128)(2,1)S(1)}, bf16[16,16,640]{2,1,0:T(8,128)(2,1)S(1)}, u32[]{:S(2)}, u32[]{:S(2)}) collective-permute-start(bf16[16,16,640]{2,1,0:T(8,128)(2,1)S(1)} %slice.4), channel_id=1, source_target_pairs={{0,1},{1,0},{2,3},{3,2},{4,5},{5,4},{6,7},{7,6},{8,9},{9,8},{10,11... | collective-permute-start | bytes 983048 | tf_op jit(solution)/shard_map/ppermute | solution.py:292
  65.2 12.4 %copy-start.3 = (bf16[1,32,640]{2,1,0:T(8,128)(2,1)S(1)}, bf16[1,32,640]{2,1,0:T(8,128)(2,1)}, u32[]{:S(2)}) copy-start(bf16[1,32,640]{2,1,0:T(8,128)(2,1)} %param.8) | copy-start | bytes 122884
  65.2 12.4 %copy-start.4 = (bf16[32,640]{1,0:T(8,128)(2,1)S(1)}, bf16[32,640]{1,0:T(8,128)(2,1)}, u32[]{:S(2)}) copy-start(bf16[32,640]{1,0:T(8,128)(2,1)} %get-tuple-element.9.query) | copy-start | bytes 122884
  65.2 12.4 %copy-start.1 = (bf16[640,640]{1,0:T(8,128)(2,1)S(1)}, bf16[640,640]{1,0:T(8,128)(2,1)}, u32[]{:S(2)}) copy-start(bf16[640,640]{1,0:T(8,128)(2,1)} %wv.3) | copy-start | bytes 2457604
  70.5 7.1 %copy-start = (bf16[640,640]{1,0:T(8,128)(2,1)S(1)}, bf16[640,640]{1,0:T(8,128)(2,1)}, u32[]{:S(2)}) copy-start(bf16[640,640]{1,0:T(8,128)(2,1)} %wk.3) | copy-start | bytes 2457604
  70.5 18.8 %all-to-all-start.1 = ((bf16[8,32,1024]{2,1,0:T(8,128)(2,1)}), bf16[8,32,1024]{2,1,0:T(8,128)(2,1)S(1)}, u32[]{:S(2)}, u32[]{:S(2)}) async-start(bf16[8,32,1024]{2,1,0:T(8,128)(2,1)} %attend.1.after), calls=%async_computation.1 | async-start | bytes 1048576 | tf_op jit(solution)/shard_map/all_to_all | solution.py:306
  77.6 11.8 %copy-start.2 = (bf16[640,640]{1,0:T(8,128)(2,1)S(1)}, bf16[640,640]{1,0:T(8,128)(2,1)}, u32[]{:S(2)}) copy-start(bf16[640,640]{1,0:T(8,128)(2,1)} %wo.1) | copy-start | bytes 2457604

commit v4 on v3

--- a/solution.py
+++ b/solution.py
@@ -21,10 +21,9 @@
 KEYS = Z * COLS
 SEND = D + 3 * LANES
 BACK = D + 3 * LANES
+VMEM = 24 * 1024 * 1024
+PAYLOAD, PREPARE, PROJECT, ATTEND, FRESH, FINISH = 1, 2, 2, 3, 1, 2
 STATS_AT = (64, 84, 104)
-WIDE = 60
-NARROW = 24
-ATTEND = 52
 F32 = jnp.float32
 BF16 = jnp.bfloat16
 
@@ -92,19 +91,17 @@
     gather[:COLS, :] = stale[...]
 
 
-def prepare_kernel(block, stale, gathered, wq, slices, send, query_out, halo_rows, sem):
+def prepare_kernel(block, gathered, wq, slices, send, query_out):
     z, j = place()
     beside = jnp.where(j == 0, jnp.minimum(z + 1, Z - 1), jnp.maximum(z - 1, 0))
-    fetch = pltpu.make_async_copy(gathered.at[beside, pl.ds(0, COLS), :], halo_rows, sem)
-    fetch.start()
+    stale = gathered[z, :COLS, :]
     query = dot(layer_norm(block[...].astype(F32)), wq[...]).astype(BF16)
     query = query * jnp.array(HEAD_DIM**-0.5, BF16)
     query_out[...] = query
     outside = ((j == 0) & (z == Z - 1)) | ((j != 0) & (z == 0))
-    fetch.wait()
-    halo = halo_rows[...].astype(F32) * jnp.where(outside, 0.0, 1.0)
+    halo = gathered[beside, :COLS, :].astype(F32) * jnp.where(outside, 0.0, 1.0)
     three = jnp.concatenate(
-        [silu(block[...].astype(F32)), silu(stale[...].astype(F32)), silu(halo)], axis=0
+        [silu(block[...].astype(F32)), silu(stale.astype(F32)), silu(halo)], axis=0
     )
     cut = dot(three, slices[...]).astype(BF16)
     for j in range(GROUP):
@@ -255,8 +252,12 @@
 HBM_SPEC = pl.BlockSpec(memory_space=pltpu.HBM)
 
 
-def params(mib):
-    return pltpu.CompilerParams(vmem_limit_bytes=mib * 1024 * 1024)
+def params():
+    return pltpu.CompilerParams(vmem_limit_bytes=VMEM)
+
+
+def cost(us):
+    return pl.CostEstimate(flops=int(us * 1e9), bytes_accessed=0, transcendentals=0)
 
 
 def shape(dims, dtype=BF16):
@@ -277,17 +278,17 @@
                 pltpu.VMEM((16, D), F32),
                 pltpu.SemaphoreType.DMA((2,)),
             ],
-            compiler_params=params(WIDE),
+            compiler_params=params(),
+            cost_estimate=cost(PAYLOAD),
         )(stale, conv_weight)
     gathered = lax.all_gather(payload, "z", axis=0)
     with jax.named_scope("prepare"):
         send, query = pl.pallas_call(
             prepare_kernel,
             out_shape=(shape((GROUP, COLS, SEND)), shape((COLS, D))),
-            in_specs=[VMEM_SPEC, VMEM_SPEC, HBM_SPEC, VMEM_SPEC, VMEM_SPEC],
-            scratch_shapes=[pltpu.VMEM((COLS, D), BF16), pltpu.SemaphoreType.DMA],
-            compiler_params=params(WIDE),
-        )(block, stale, gathered, query_weight, jnp.asarray(slice_matrix()))
+            compiler_params=params(),
+            cost_estimate=cost(PREPARE),
+        )(block, gathered, query_weight, jnp.asarray(slice_matrix()))
     sent = lax.all_to_all(send, ("yh", "x"), 0, 0, tiled=True)
     other = lax.ppermute(gathered[:, COLS:, :], "core", [(0, 1), (1, 0)])
     with jax.named_scope("project"):
@@ -295,13 +296,15 @@
             project_kernel,
             out_shape=shape((KEYS, 2 * D)),
             in_specs=[VMEM_SPEC] * 3 + [ANY_SPEC],
-            compiler_params=params(WIDE),
+            compiler_params=params(),
+            cost_estimate=cost(PROJECT),
         )(gathered, key_weight, value_weight, send)
     with jax.named_scope("attend"):
         back = pl.pallas_call(
             attend_kernel,
             out_shape=shape((GROUP, COLS, BACK)),
-            compiler_params=params(ATTEND),
+            compiler_params=params(),
+            cost_estimate=cost(ATTEND),
         )(sent, both, gathered, other)
     partial = lax.all_to_all(back, ("yh", "x"), 0, 0, tiled=True)
     with jax.named_scope("fresh"):
@@ -309,13 +312,15 @@
             fresh_kernel,
             out_shape=(shape((COLS, D), F32), shape((COLS, LANES), F32)),
             in_specs=[VMEM_SPEC] * 4 + [ANY_SPEC],
-            compiler_params=params(NARROW),
+            compiler_params=params(),
+            cost_estimate=cost(FRESH),
         )(block, query, key_weight, value_weight, back)
     with jax.named_scope("finish"):
         attended, convolved = pl.pallas_call(
             finish_kernel,
             out_shape=(shape((COLS, D)), shape((COLS, CO))),
-            compiler_params=params(NARROW),
+            compiler_params=params(),
+            cost_estimate=cost(FINISH),
         )(partial, fresh, fresh_stats, out_weight)
     return attended.reshape(1, COLS, D), convolved.reshape(1, COLS, CO)
 

time: 91.5 us -> 82.7 us (0.904)
  Pallas kernels: 17.4 us -> 9.44 us
  local copies, waits for them, and re-layouts: 1.02 us -> 4.02 us
  blocking collectives: 37.9 us -> 35.1 us
  waiting for transfers between devices: 10.8 us -> 8.78 us
    unnamed x10 -> x20, local copies, waits for them, and re-layouts: 0.02 us -> 3.99 us
    pallas_call x1, Pallas kernels: 4.38 us -> 1.6 us  [local(): pl.pallas_call(project_kernel, out_shape=shape((KEYS, 2 * D)), in_specs=[...]
    all_gather x1, blocking collectives: 37.9 us -> 35.1 us  [local(): gathered = lax.all_gather(payload, 'z', axis=0)]
    pallas_call x1, Pallas kernels: 3.61 us -> 1.46 us  [local(): pl.pallas_call(prepare_kernel, out_shape=(shape((GROUP, COLS, SEND)), sha...]
    all_to_all x1, waiting for transfers between devices: 10.8 us -> 8.78 us  [local(): partial = lax.all_to_all(back, ('yh', 'x'), 0, 0, tiled=True)]
    pallas_call x1, Pallas kernels: 5.28 us -> 3.59 us  [local(): pl.pallas_call(attend_kernel, out_shape=shape((GROUP, COLS, BACK)), compi...]
    pallas_call x1, Pallas kernels: 1.56 us -> 0.23 us  [local(): pl.pallas_call(payload_kernel, out_shape=shape((COLS + 16, D)), in_specs=...]
    slice x1, local copies, waits for them, and re-layouts: 1 us -> 0.03 us  [local(): other = lax.ppermute(gathered[:, COLS:, :], 'core', [(0, 1), (1, 0)])]
  transfers between devices with their start and end apart: 3 -> 3, of which waited for: 1 -> 1; matrix products, arithmetic and copies ran while one was open for 1% -> 0% of each run, Pallas kernels for 6% -> 3%
where the time goes in v4:
time: 82.7 us; the launch traced here: 81.6 us
  blocking collectives  35.1 us (42%)
  starting transfers between devices  23.5 us (28%)
  Pallas kernels  9.44 us (11%)
  waiting for transfers between devices  8.78 us (11%)
  local copies, waits for them, and re-layouts  4.02 us (5%)
    all_gather x1, blocking collectives, local(): gathered = lax.all_gather(payload, 'z', axis=0)  35.1 us
    ppermute x1, starting transfers between devices, local(): other = lax.ppermute(gathered[:, COLS:, :], 'core', [(0, 1), (1, 0)])  9.79 us
    all_to_all x1, waiting for transfers between devices, local(): partial = lax.all_to_all(back, ('yh', 'x'), 0, 0, tiled=True)  8.78 us
    all_to_all x1, starting transfers between devices, local(): partial = lax.all_to_all(back, ('yh', 'x'), 0, 0, tiled=True)  6.93 us
    all_to_all x1, starting transfers between devices, local(): sent = lax.all_to_all(send, ('yh', 'x'), 0, 0, tiled=True)  6.79 us
    unnamed x20, local copies, waits for them, and re-layouts  3.99 us
    pallas_call x1, Pallas kernels, local(): pl.pallas_call(attend_kernel, out_shape=shape((GROUP, COLS, BACK)), compi...  3.59 us
  transfers between devices with their start and end apart: 3, of which 1 were waited for; matrix products, arithmetic and copies ran while one was open for 0% of the time, Pallas kernels for 3%

profile of v4, /device:TPU:1, one launch (start us, length us, event | category | flops | bytes accessed | tf_op | source)
XLA Modules:
  0.0 81.6 jit_solution(8923224800226644448)
XLA Ops:
  0.6 0.0 copy-start.4
  0.6 0.8 copy-done.4
  1.4 0.8 copy-done.5
  2.2 0.2 payload.1
  2.5 35.1 %all-gather = bf16[768,640]{1,0:T(8,128)(2,1)S(1)} all-gather(bf16[48,640]{1,0:T(8,128)(2,1)S(1)} %payload.1), channel_id=2, replica_groups=mesh['z'=16,'yh'=2,'x'=4,'yl'=2,'core'=2] {'z'}, dimensions={0}, use_global_device_ids=true | all-gather | bytes 1044480 | tf_op jit(solution)/shard_map/all_gather | solution.py:284
  37.6 0.0 copy-done
  37.6 0.0 copy-done.6
  37.6 0.0 copy-done.7
  37.6 1.5 %prepare.1 = (bf16[8,32,1024]{2,1,0:T(8,128)(2,1)}, bf16[32,640]{1,0:T(8,128)(2,1)S(1)}) custom-call(bf16[32,640]{1,0:T(8,128)(2,1)S(1)} %bitcast.10, bf16[16,48,640]{2,1,0:T(8,128)(2,1)S(1)} %bitcast.5, bf16[640,640]{1,0:T(8,128)(2,1)S(1)} %copy-done, bf16[640,1024]{1,0:T(8,128)(2,1)S(1)} %copy-done.7), custom_call_target="tpu_custom_call" | custom-call | flops 2000000000 | tf_op jit(solution)/shard_map/prepare/pallas_call | solution.py:286
  39.1 6.8 %all-to-all-start = ((bf16[8,32,1024]{2,1,0:T(8,128)(2,1)}), bf16[8,32,1024]{2,1,0:T(8,128)(2,1)S(1)}, u32[]{:S(2)}, u32[]{:S(2)}) async-start(bf16[8,32,1024]{2,1,0:T(8,128)(2,1)} %get-tuple-element.8.after), calls=%async_computation | async-start | bytes 1048576 | tf_op jit(solution)/shard_map/all_to_all | solution.py:292
  45.9 9.8 %collective-permute-start = (bf16[16,16,640]{2,1,0:T(8,128)(2,1)S(1)}, bf16[16,16,640]{2,1,0:T(8,128)(2,1)S(1)}, u32[]{:S(2)}, u32[]{:S(2)}) collective-permute-start(bf16[16,16,640]{2,1,0:T(8,128)(2,1)S(1)} %slice.4), channel_id=1, source_target_pairs={{0,1},{1,0},{2,3},{3,2},{4,5},{5,4},{6,7},{7,6},{8,9},{9,8},{10,11... | collective-permute-start | bytes 983048 | tf_op jit(solution)/shard_map/ppermute | solution.py:293
  55.7 0.0 copy-done.1
  55.7 0.0 copy-done.2
  55.7 1.6 %project.1.both = bf16[512,1280]{1,0:T(8,128)(2,1)S(1)} custom-call(bf16[16,48,640]{2,1,0:T(8,128)(2,1)S(1)} %bitcast.7, bf16[640,640]{1,0:T(8,128)(2,1)S(1)} %copy-done.1, bf16[640,640]{1,0:T(8,128)(2,1)S(1)} %copy-done.2, bf16[8,32,1024]{2,1,0:T(8,128)(2,1)} %get-tuple-element.8.after), custom_call_target="tpu_custom_call" | custom-call | flops 2000000000 | tf_op jit(solution)/shard_map/project/pallas_call | solution.py:295
  57.3 0.0 copy-start.8
  57.3 1.1 %copy-done.8 = bf16[512,1280]{1,0:T(8,128)(2,1)} copy-done((bf16[512,1280]{1,0:T(8,128)(2,1)}, bf16[512,1280]{1,0:T(8,128)(2,1)S(1)}, u32[]{:S(2)}) %copy-start.8) | copy-done | bytes 1310744
  58.4 0.0 collective-permute-done.other
  58.4 0.0 all-to-all-done.sent
  58.4 1.3 %copy-done.9 = bf16[512,1280]{1,0:T(8,128)(2,1)S(1)} copy-done((bf16[512,1280]{1,0:T(8,128)(2,1)S(1)}, bf16[512,1280]{1,0:T(8,128)(2,1)}, u32[]{:S(2)}) %copy-start.9) | copy-done | bytes 1310744
  59.7 3.6 %attend.1.after = bf16[8,32,1024]{2,1,0:T(8,128)(2,1)} custom-call(bf16[8,32,1024]{2,1,0:T(8,128)(2,1)S(1)} %all-to-all-done.sent, bf16[512,1280]{1,0:T(8,128)(2,1)S(1)} %copy-done.9, bf16[16,48,640]{2,1,0:T(8,128)(2,1)S(1)} %bitcast.8, bf16[16,16,640]{2,1,0:T(8,128)(2,1)S(1)} %collective-permute-done.other), custom_call_target="tpu_custom_call" | custom-call | flops 3000000000 | tf_op jit(solution)/shard_map/attend/pallas_call | solution.py:303
  63.3 6.9 %all-to-all-start.1 = ((bf16[8,32,1024]{2,1,0:T(8,128)(2,1)}), bf16[8,32,1024]{2,1,0:T(8,128)(2,1)S(1)}, u32[]{:S(2)}, u32[]{:S(2)}) async-start(bf16[8,32,1024]{2,1,0:T(8,128)(2,1)} %attend.1.after), calls=%async_computation.1 | async-start | bytes 1048576 | tf_op jit(solution)/shard_map/all_to_all | solution.py:309
  70.3 1.0 %fresh.1 = (f32[32,640]{1,0:T(8,128)S(1)}, f32[32,128]{1,0:T(8,128)S(1)}) custom-call(bf16[32,640]{1,0:T(8,128)(2,1)S(1)} %bitcast.11, bf16[32,640]{1,0:T(8,128)(2,1)S(1)} %get-tuple-element.9.query, bf16[640,640]{1,0:T(8,128)(2,1)S(1)} %copy-done.1, bf16[640,640]{1,0:T(8,128)(2,1)S(1)} %copy-done.2, bf16[8,32,1024]{2,1,0:T(8,128)(2,1)} %attend.1.after), custom_call_target="tpu_custom_call" | custom-call | flops 1000000000 | tf_op jit(solution)/shard_map/fresh/pallas_call | solution.py:311
  71.2 8.8 %all-to-all-done.1.partial = bf16[8,32,1024]{2,1,0:T(8,128)(2,1)S(1)} async-done(((bf16[8,32,1024]{2,1,0:T(8,128)(2,1)}), bf16[8,32,1024]{2,1,0:T(8,128)(2,1)S(1)}, u32[]{:S(2)}, u32[]{:S(2)}) %all-to-all-start.1) | async-done | bytes 524320 | tf_op jit(solution)/shard_map/all_to_all | solution.py:309
  80.0 1.6 %finish.1 = (bf16[32,640]{1,0:T(8,128)(2,1)}, bf16[32,320]{1,0:T(8,128)(2,1)}) custom-call(bf16[8,32,1024]{2,1,0:T(8,128)(2,1)S(1)} %all-to-all-done.1.partial, f32[32,640]{1,0:T(8,128)S(1)} %get-tuple-element.10.fresh, f32[32,128]{1,0:T(8,128)S(1)} %get-tuple-element.11.fresh_stats, bf16[640,640]{1,0:T(8,128)(2,1)S(1)} %copy-done.3), custom_call_target="tpu_custom_call" | custom-call | flops 2000000000 | tf_op jit(solution)/shard_map/finish/pallas_call | solution.py:319
  (10 shorter events, 0.0 us)
Async XLA Ops:
  0.6 0.8 copy-start.4
  1.4 0.8 copy-start.5
  2.2 35.4 %copy-start = (bf16[640,640]{1,0:T(8,128)(2,1)S(1)}, bf16[640,640]{1,0:T(8,128)(2,1)}, u32[]{:S(2)}) copy-start(bf16[640,640]{1,0:T(8,128)(2,1)} %wq.1) | copy-start | bytes 2457604
  2.2 35.4 %copy-start.6 = (bf16[1,32,640]{2,1,0:T(8,128)(2,1)S(1)}, bf16[1,32,640]{2,1,0:T(8,128)(2,1)}, u32[]{:S(2)}) copy-start(bf16[1,32,640]{2,1,0:T(8,128)(2,1)} %param.8) | copy-start | bytes 122884
  2.2 35.4 %copy-start.7 = (bf16[640,1024]{1,0:T(8,128)(2,1)S(1)}, bf16[640,1024]{1,0:T(8,128)(2,1)}, u32[]{:S(2)}) copy-start(bf16[640,1024]{1,0:T(8,128)(2,1)} %constant.2.clone.slices) | copy-start | bytes 3932164
  39.1 16.6 %copy-start.1 = (bf16[640,640]{1,0:T(8,128)(2,1)S(1)}, bf16[640,640]{1,0:T(8,128)(2,1)}, u32[]{:S(2)}) copy-start(bf16[640,640]{1,0:T(8,128)(2,1)} %wk.3) | copy-start | bytes 2457604
  39.1 16.6 %copy-start.2 = (bf16[640,640]{1,0:T(8,128)(2,1)S(1)}, bf16[640,640]{1,0:T(8,128)(2,1)}, u32[]{:S(2)}) copy-start(bf16[640,640]{1,0:T(8,128)(2,1)} %wv.3) | copy-start | bytes 2457604
  39.1 19.3 %all-to-all-start = ((bf16[8,32,1024]{2,1,0:T(8,128)(2,1)}), bf16[8,32,1024]{2,1,0:T(8,128)(2,1)S(1)}, u32[]{:S(2)}, u32[]{:S(2)}) async-start(bf16[8,32,1024]{2,1,0:T(8,128)(2,1)} %get-tuple-element.8.after), calls=%async_computation | async-start | bytes 1048576 | tf_op jit(solution)/shard_map/all_to_all | solution.py:292
  45.9 12.5 %collective-permute-start = (bf16[16,16,640]{2,1,0:T(8,128)(2,1)S(1)}, bf16[16,16,640]{2,1,0:T(8,128)(2,1)S(1)}, u32[]{:S(2)}, u32[]{:S(2)}) collective-permute-start(bf16[16,16,640]{2,1,0:T(8,128)(2,1)S(1)} %slice.4), channel_id=1, source_target_pairs={{0,1},{1,0},{2,3},{3,2},{4,5},{5,4},{6,7},{7,6},{8,9},{9,8},{10,11... | collective-permute-start | bytes 983048 | tf_op jit(solution)/shard_map/ppermute | solution.py:293
  57.3 1.1 %copy-start.8 = (bf16[512,1280]{1,0:T(8,128)(2,1)}, bf16[512,1280]{1,0:T(8,128)(2,1)S(1)}, u32[]{:S(2)}) copy-start(bf16[512,1280]{1,0:T(8,128)(2,1)S(1)} %project.1.both) | copy-start | bytes 3932164
  58.4 1.3 %copy-start.9 = (bf16[512,1280]{1,0:T(8,128)(2,1)S(1)}, bf16[512,1280]{1,0:T(8,128)(2,1)}, u32[]{:S(2)}) copy-start(bf16[512,1280]{1,0:T(8,128)(2,1)} %copy-done.8) | copy-start | bytes 3932164
  63.3 16.7 %all-to-all-start.1 = ((bf16[8,32,1024]{2,1,0:T(8,128)(2,1)}), bf16[8,32,1024]{2,1,0:T(8,128)(2,1)S(1)}, u32[]{:S(2)}, u32[]{:S(2)}) async-start(bf16[8,32,1024]{2,1,0:T(8,128)(2,1)} %attend.1.after), calls=%async_computation.1 | async-start | bytes 1048576 | tf_op jit(solution)/shard_map/all_to_all | solution.py:309
  70.3 9.7 %copy-start.3 = (bf16[640,640]{1,0:T(8,128)(2,1)S(1)}, bf16[640,640]{1,0:T(8,128)(2,1)}, u32[]{:S(2)}) copy-start(bf16[640,640]{1,0:T(8,128)(2,1)} %wo.1) | copy-start | bytes 2457604

commit v5 on v4

--- a/solution.py
+++ b/solution.py
@@ -112,11 +112,12 @@
             ]
 
 
-def project_kernel(gathered, wk, wv, after, both):
+def project_kernel(gathered, block, weight, after, out, own):
     del after
     normed = layer_norm(gathered[:, :COLS, :].reshape(KEYS, D).astype(F32))
-    both[:, :D] = dot(normed, wk[...]).astype(BF16)
-    both[:, D:] = dot(normed, wv[...]).astype(BF16)
+    fresh = layer_norm(block[...].astype(F32))
+    out[...] = dot(normed, weight[...]).astype(BF16)
+    own[...] = dot(fresh, weight[...]).astype(BF16)
 
 
 def attend_pair(query, keys, values, masked, lanes):
@@ -156,7 +157,7 @@
     return total
 
 
-def attend_kernel(sent, both, gathered, other, back):
+def attend_kernel(sent, all_keys, all_values, gathered, other, back):
     z, j = place()
     row = lax.broadcasted_iota(jnp.int32, (2 * QUERIES, KEYS), 0)
     col = lax.broadcasted_iota(jnp.int32, (2 * QUERIES, KEYS), 1)
@@ -167,7 +168,7 @@
     for pair in range(PAIRS):
         at = slice(pair * LANES, (pair + 1) * LANES)
         query = sent[:, :, at].reshape(QUERIES, LANES)
-        keys, values = both[:, at], both[:, D + pair * LANES : D + (pair + 1) * LANES]
+        keys, values = all_keys[:, at], all_values[:, at]
         row_max, row_sum, weighted = attend_pair(query, keys, values, masked, lanes)
         weighted = weighted / row_sum
         mixed = jnp.where(low, weighted[:QUERIES], weighted[QUERIES:])
@@ -190,18 +191,15 @@
     back[:, :, D + 2 * LANES :] = tail.astype(BF16).reshape(GROUP, COLS, LANES)
 
 
-def fresh_kernel(block, query, wk, wv, after, weighted_out, stats_out):
+def fresh_kernel(own_keys, own_values, query, after, weighted_out, stats_out):
     del after
-    normed = layer_norm(block[...].astype(F32))
-    keys = dot(normed, wk[...]).astype(BF16)
-    values = dot(normed, wv[...]).astype(BF16)
     lanes = lane_ids(COLS)
     low = lanes < HEAD_DIM
     stats = jnp.zeros((COLS, LANES), F32)
     for pair in range(PAIRS):
         at = slice(pair * LANES, (pair + 1) * LANES)
         row_max, row_sum, weighted = attend_pair(
-            query[:, at], keys[:, at], values[:, at], None, lanes
+            query[:, at], own_keys[:, at], own_values[:, at], None, lanes
         )
         weighted_out[:, at] = jnp.where(low, weighted[:COLS], weighted[COLS:])
         for half in range(2):
@@ -291,30 +289,35 @@
         )(block, gathered, query_weight, jnp.asarray(slice_matrix()))
     sent = lax.all_to_all(send, ("yh", "x"), 0, 0, tiled=True)
     other = lax.ppermute(gathered[:, COLS:, :], "core", [(0, 1), (1, 0)])
-    with jax.named_scope("project"):
-        both = pl.pallas_call(
-            project_kernel,
-            out_shape=shape((KEYS, 2 * D)),
-            in_specs=[VMEM_SPEC] * 3 + [ANY_SPEC],
-            compiler_params=params(),
-            cost_estimate=cost(PROJECT),
-        )(gathered, key_weight, value_weight, send)
+    sides = []
+    for name, weight in (("keys", key_weight), ("values", value_weight)):
+        with jax.named_scope(name):
+            sides.append(
+                pl.pallas_call(
+                    project_kernel,
+                    out_shape=(shape((KEYS, D)), shape((COLS, D))),
+                    in_specs=[VMEM_SPEC] * 3 + [ANY_SPEC],
+                    compiler_params=params(),
+                    cost_estimate=cost(PROJECT),
+                )(gathered, block, weight, sides[0][0] if sides else send)
+            )
+    (keys, own_keys), (values, own_values) = sides
     with jax.named_scope("attend"):
         back = pl.pallas_call(
             attend_kernel,
             out_shape=shape((GROUP, COLS, BACK)),
             compiler_params=params(),
             cost_estimate=cost(ATTEND),
-        )(sent, both, gathered, other)
+        )(sent, keys, values, gathered, other)
     partial = lax.all_to_all(back, ("yh", "x"), 0, 0, tiled=True)
     with jax.named_scope("fresh"):
         fresh, fresh_stats = pl.pallas_call(
             fresh_kernel,
             out_shape=(shape((COLS, D), F32), shape((COLS, LANES), F32)),
-            in_specs=[VMEM_SPEC] * 4 + [ANY_SPEC],
+            in_specs=[VMEM_SPEC] * 3 + [ANY_SPEC],
             compiler_params=params(),
             cost_estimate=cost(FRESH),
-        )(block, query, key_weight, value_weight, back)
+        )(own_keys, own_values, query, back)
     with jax.named_scope("finish"):
         attended, convolved = pl.pallas_call(
             finish_kernel,

time: 82.7 us -> 81.1 us (0.981)
  local copies, waits for them, and re-layouts: 4.02 us -> 1.64 us
    unnamed x20 -> x16, local copies, waits for them, and re-layouts: 3.99 us -> 1.61 us
    pallas_call x1 -> x2, Pallas kernels: 1.6 us -> 2.25 us  [local(): pl.pallas_call(project_kernel, out_shape=(shape((KEYS, D)), shape((COLS,...]
  transfers between devices with their start and end apart: 3 -> 3, of which waited for: 1 -> 1; matrix products, arithmetic and copies ran while one was open for 0% -> 0% of each run, Pallas kernels for 3% -> 4%
where the time goes in v5:
time: 81.1 us; the launch traced here: 79.8 us
  blocking collectives  35.1 us (43%)
  starting transfers between devices  23.6 us (29%)
  Pallas kernels  9.69 us (12%)
  waiting for transfers between devices  8.99 us (11%)
  local copies, waits for them, and re-layouts  1.64 us (2%)
    all_gather x1, blocking collectives, local(): gathered = lax.all_gather(payload, 'z', axis=0)  35.1 us
    ppermute x1, starting transfers between devices, local(): other = lax.ppermute(gathered[:, COLS:, :], 'core', [(0, 1), (1, 0)])  9.92 us
    all_to_all x1, waiting for transfers between devices, local(): partial = lax.all_to_all(back, ('yh', 'x'), 0, 0, tiled=True)  8.98 us
    all_to_all x1, starting transfers between devices, local(): partial = lax.all_to_all(back, ('yh', 'x'), 0, 0, tiled=True)  6.93 us
    all_to_all x1, starting transfers between devices, local(): sent = lax.all_to_all(send, ('yh', 'x'), 0, 0, tiled=True)  6.78 us
    pallas_call x1, Pallas kernels, local(): pl.pallas_call(attend_kernel, out_shape=shape((GROUP, COLS, BACK)), compi...  3.61 us
    pallas_call x2, Pallas kernels, local(): pl.pallas_call(project_kernel, out_shape=(shape((KEYS, D)), shape((COLS,...  2.25 us
  transfers between devices with their start and end apart: 3, of which 1 were waited for; matrix products, arithmetic and copies ran while one was open for 0% of the time, Pallas kernels for 4%

profile of v5, /device:TPU:1, one launch (start us, length us, event | category | flops | bytes accessed | tf_op | source)
XLA Modules:
  0.0 79.8 jit_solution(15843098695251963346)
XLA Ops:
  0.6 0.0 copy-start.4
  0.6 0.8 %copy-done.4 = bf16[9,5,320]{2,1,0:T(8,128)(2,1)S(1)} copy-done((bf16[9,5,320]{2,1,0:T(8,128)(2,1)S(1)}, bf16[9,5,320]{2,1,0:T(8,128)(2,1)}, u32[]{:S(2)}) %copy-start.4) | copy-done | bytes 28824
  1.4 0.8 copy-done.5
  2.2 0.2 payload.1
  2.5 35.1 %all-gather = bf16[768,640]{1,0:T(8,128)(2,1)S(1)} all-gather(bf16[48,640]{1,0:T(8,128)(2,1)S(1)} %payload.1), channel_id=2, replica_groups=mesh['z'=16,'yh'=2,'x'=4,'yl'=2,'core'=2] {'z'}, dimensions={0}, use_global_device_ids=true | all-gather | bytes 1044480 | tf_op jit(solution)/shard_map/all_gather | solution.py:282
  37.6 0.0 copy-done
  37.6 0.0 copy-done.6
  37.6 0.0 copy-done.7
  37.6 1.4 %prepare.1 = (bf16[8,32,1024]{2,1,0:T(8,128)(2,1)}, bf16[32,640]{1,0:T(8,128)(2,1)S(1)}) custom-call(bf16[32,640]{1,0:T(8,128)(2,1)S(1)} %bitcast.11, bf16[16,48,640]{2,1,0:T(8,128)(2,1)S(1)} %bitcast.5, bf16[640,640]{1,0:T(8,128)(2,1)S(1)} %copy-done, bf16[640,1024]{1,0:T(8,128)(2,1)S(1)} %copy-done.7), custom_call_target="tpu_custom_call" | custom-call | flops 2000000000 | tf_op jit(solution)/shard_map/prepare/pallas_call | solution.py:284
  39.1 6.8 %all-to-all-start = ((bf16[8,32,1024]{2,1,0:T(8,128)(2,1)}), bf16[8,32,1024]{2,1,0:T(8,128)(2,1)S(1)}, u32[]{:S(2)}, u32[]{:S(2)}) async-start(bf16[8,32,1024]{2,1,0:T(8,128)(2,1)} %get-tuple-element.12.after), calls=%async_computation | async-start | bytes 1048576 | tf_op jit(solution)/shard_map/all_to_all | solution.py:290
  45.9 0.0 copy-start.2
  45.9 9.9 %collective-permute-start = (bf16[16,16,640]{2,1,0:T(8,128)(2,1)S(1)}, bf16[16,16,640]{2,1,0:T(8,128)(2,1)S(1)}, u32[]{:S(2)}, u32[]{:S(2)}) collective-permute-start(bf16[16,16,640]{2,1,0:T(8,128)(2,1)S(1)} %slice.4), channel_id=1, source_target_pairs={{0,1},{1,0},{2,3},{3,2},{4,5},{5,4},{6,7},{7,6},{8,9},{9,8},{10,11... | collective-permute-start | bytes 983048 | tf_op jit(solution)/shard_map/ppermute | solution.py:291
  55.8 0.0 copy-done.1
  55.8 1.1 %keys.1 = (bf16[512,640]{1,0:T(8,128)(2,1)S(1)}, bf16[32,640]{1,0:T(8,128)(2,1)S(1)}) custom-call(bf16[16,48,640]{2,1,0:T(8,128)(2,1)S(1)} %bitcast.7, bf16[32,640]{1,0:T(8,128)(2,1)S(1)} %bitcast.12, bf16[640,640]{1,0:T(8,128)(2,1)S(1)} %copy-done.1, bf16[8,32,1024]{2,1,0:T(8,128)(2,1)} %get-tuple-element.12.after), custom_call_target="tpu_custom_call" | custom-call | flops 2000000000 | tf_op jit(solution)/shard_map/keys/pallas_call | solution.py:296
  56.9 0.0 copy-done.2
  57.0 1.1 %values.1 = (bf16[512,640]{1,0:T(8,128)(2,1)S(1)}, bf16[32,640]{1,0:T(8,128)(2,1)S(1)}) custom-call(bf16[16,48,640]{2,1,0:T(8,128)(2,1)S(1)} %bitcast.8, bf16[32,640]{1,0:T(8,128)(2,1)S(1)} %bitcast.13, bf16[640,640]{1,0:T(8,128)(2,1)S(1)} %copy-done.2, bf16[512,640]{1,0:T(8,128)(2,1)S(1)} %get-tuple-element.13.after.all_keys), custom_call_target="tpu_custom_call" | custom-call | flops 2000000000 | tf_op jit(solution)/shard_map/values/pallas_call | solution.py:296
  58.1 0.0 collective-permute-done.other
  58.1 0.0 all-to-all-done.sent
  58.1 3.6 %attend.1.after = bf16[8,32,1024]{2,1,0:T(8,128)(2,1)} custom-call(bf16[8,32,1024]{2,1,0:T(8,128)(2,1)S(1)} %all-to-all-done.sent, bf16[512,640]{1,0:T(8,128)(2,1)S(1)} %get-tuple-element.13.after.all_keys, bf16[512,640]{1,0:T(8,128)(2,1)S(1)} %get-tuple-element.14.all_values, bf16[16,48,640]{2,1,0:T(8,128)(2,1)S(1)} %bitcast.9, ...), custom_call_target="tpu_custom_call" | custom-call | flops 3000000000 | tf_op jit(solution)/shard_map/attend/pallas_call | solution.py:306
  61.7 6.9 %all-to-all-start.1 = ((bf16[8,32,1024]{2,1,0:T(8,128)(2,1)}), bf16[8,32,1024]{2,1,0:T(8,128)(2,1)S(1)}, u32[]{:S(2)}, u32[]{:S(2)}) async-start(bf16[8,32,1024]{2,1,0:T(8,128)(2,1)} %attend.1.after), calls=%async_computation.1 | async-start | bytes 1048576 | tf_op jit(solution)/shard_map/all_to_all | solution.py:312
  68.7 0.6 fresh.1
  69.2 9.0 %all-to-all-done.1.partial = bf16[8,32,1024]{2,1,0:T(8,128)(2,1)S(1)} async-done(((bf16[8,32,1024]{2,1,0:T(8,128)(2,1)}), bf16[8,32,1024]{2,1,0:T(8,128)(2,1)S(1)}, u32[]{:S(2)}, u32[]{:S(2)}) %all-to-all-start.1) | async-done | bytes 524320 | tf_op jit(solution)/shard_map/all_to_all | solution.py:312
  78.2 0.0 copy-done.3
  78.2 1.6 %finish.1 = (bf16[32,640]{1,0:T(8,128)(2,1)}, bf16[32,320]{1,0:T(8,128)(2,1)}) custom-call(bf16[8,32,1024]{2,1,0:T(8,128)(2,1)S(1)} %all-to-all-done.1.partial, f32[32,640]{1,0:T(8,128)S(1)} %get-tuple-element.18.fresh, f32[32,128]{1,0:T(8,128)S(1)} %get-tuple-element.19.fresh_stats, bf16[640,640]{1,0:T(8,128)(2,1)S(1)} %copy-done.3), custom_call_target="tpu_custom_call" | custom-call | flops 2000000000 | tf_op jit(solution)/shard_map/finish/pallas_call | solution.py:322
  (7 shorter events, 0.0 us)
Async XLA Ops:
  0.6 0.8 %copy-start.4 = (bf16[9,5,320]{2,1,0:T(8,128)(2,1)S(1)}, bf16[9,5,320]{2,1,0:T(8,128)(2,1)}, u32[]{:S(2)}) copy-start(bf16[9,5,320]{2,1,0:T(8,128)(2,1)} %taps_hbm.1) | copy-start | bytes 86404
  1.4 0.8 copy-start.5
  2.2 35.4 %copy-start = (bf16[640,640]{1,0:T(8,128)(2,1)S(1)}, bf16[640,640]{1,0:T(8,128)(2,1)}, u32[]{:S(2)}) copy-start(bf16[640,640]{1,0:T(8,128)(2,1)} %wq.1) | copy-start | bytes 2457604
  2.2 35.4 %copy-start.6 = (bf16[1,32,640]{2,1,0:T(8,128)(2,1)S(1)}, bf16[1,32,640]{2,1,0:T(8,128)(2,1)}, u32[]{:S(2)}) copy-start(bf16[1,32,640]{2,1,0:T(8,128)(2,1)} %param.8) | copy-start | bytes 122884
  2.2 35.4 %copy-start.7 = (bf16[640,1024]{1,0:T(8,128)(2,1)S(1)}, bf16[640,1024]{1,0:T(8,128)(2,1)}, u32[]{:S(2)}) copy-start(bf16[640,1024]{1,0:T(8,128)(2,1)} %constant.2.clone.slices) | copy-start | bytes 3932164
  39.1 16.8 %copy-start.1 = (bf16[640,640]{1,0:T(8,128)(2,1)S(1)}, bf16[640,640]{1,0:T(8,128)(2,1)}, u32[]{:S(2)}) copy-start(bf16[640,640]{1,0:T(8,128)(2,1)} %weight.2) | copy-start | bytes 2457604
  39.1 19.0 %all-to-all-start = ((bf16[8,32,1024]{2,1,0:T(8,128)(2,1)}), bf16[8,32,1024]{2,1,0:T(8,128)(2,1)S(1)}, u32[]{:S(2)}, u32[]{:S(2)}) async-start(bf16[8,32,1024]{2,1,0:T(8,128)(2,1)} %get-tuple-element.12.after), calls=%async_computation | async-start | bytes 1048576 | tf_op jit(solution)/shard_map/all_to_all | solution.py:290
  45.9 11.1 %copy-start.2 = (bf16[640,640]{1,0:T(8,128)(2,1)S(1)}, bf16[640,640]{1,0:T(8,128)(2,1)}, u32[]{:S(2)}) copy-start(bf16[640,640]{1,0:T(8,128)(2,1)} %weight.3) | copy-start | bytes 2457604
  45.9 12.2 %collective-permute-start = (bf16[16,16,640]{2,1,0:T(8,128)(2,1)S(1)}, bf16[16,16,640]{2,1,0:T(8,128)(2,1)S(1)}, u32[]{:S(2)}, u32[]{:S(2)}) collective-permute-start(bf16[16,16,640]{2,1,0:T(8,128)(2,1)S(1)} %slice.4), channel_id=1, source_target_pairs={{0,1},{1,0},{2,3},{3,2},{4,5},{5,4},{6,7},{7,6},{8,9},{9,8},{10,11... | collective-permute-start | bytes 983048 | tf_op jit(solution)/shard_map/ppermute | solution.py:291
  61.7 16.5 %all-to-all-start.1 = ((bf16[8,32,1024]{2,1,0:T(8,128)(2,1)}), bf16[8,32,1024]{2,1,0:T(8,128)(2,1)S(1)}, u32[]{:S(2)}, u32[]{:S(2)}) async-start(bf16[8,32,1024]{2,1,0:T(8,128)(2,1)} %attend.1.after), calls=%async_computation.1 | async-start | bytes 1048576 | tf_op jit(solution)/shard_map/all_to_all | solution.py:312
  68.7 9.6 %copy-start.3 = (bf16[640,640]{1,0:T(8,128)(2,1)S(1)}, bf16[640,640]{1,0:T(8,128)(2,1)}, u32[]{:S(2)}) copy-start(bf16[640,640]{1,0:T(8,128)(2,1)} %wo.1) | copy-start | bytes 2457604

commit v6 on v5

--- a/solution.py
+++ b/solution.py
@@ -22,7 +22,7 @@
 SEND = D + 3 * LANES
 BACK = D + 3 * LANES
 VMEM = 24 * 1024 * 1024
-PAYLOAD, PREPARE, PROJECT, ATTEND, FRESH, FINISH = 1, 2, 2, 3, 1, 2
+PAYLOAD, PREPARE, PROJECT, ATTEND, FRESH, FINISH = 1, 2, 1, 3, 0.2, 2
 STATS_AT = (64, 84, 104)
 F32 = jnp.float32
 BF16 = jnp.bfloat16
@@ -124,9 +124,10 @@
     low = lanes < HEAD_DIM
     zero = jnp.zeros_like(query)
     two = jnp.concatenate([jnp.where(low, query, zero), jnp.where(low, zero, query)], axis=0)
+    if masked is not None:
+        two = jnp.concatenate([two, masked[0]], axis=1)
+        keys = jnp.concatenate([keys, masked[1]], axis=1)
     scores = dot_t(two, keys)
-    if masked is not None:
-        scores = jnp.where(masked, -1e30, scores)
     row_max = jnp.max(scores, axis=-1, keepdims=True)
     exp_scores = jnp.exp(scores - row_max)
     row_sum = jnp.sum(exp_scores, axis=-1, keepdims=True)
@@ -157,11 +158,14 @@
     return total
 
 
-def attend_kernel(sent, all_keys, all_values, gathered, other, back):
+def attend_kernel(sent, all_keys, all_values, gathered, other, after, back):
+    del after
     z, j = place()
-    row = lax.broadcasted_iota(jnp.int32, (2 * QUERIES, KEYS), 0)
-    col = lax.broadcasted_iota(jnp.int32, (2 * QUERIES, KEYS), 1)
-    masked = (((row // COLS) % GROUP) == j) & ((col // COLS) == z)
+    rows = lax.broadcasted_iota(jnp.int32, (2 * QUERIES, LANES), 0)
+    here = lax.broadcasted_iota(jnp.int32, (2 * QUERIES, LANES), 1) == 0
+    own_query = jnp.where(here & (((rows // COLS) % GROUP) == j), -1e30, 0.0).astype(BF16)
+    own_key = jnp.where(here & ((rows // COLS) == z), 1.0, 0.0).astype(BF16)
+    masked = (own_query, own_key)
     lanes = lane_ids(QUERIES)
     low = lanes < HEAD_DIM
     stats = jnp.zeros((QUERIES, LANES), F32)
@@ -191,8 +195,7 @@
     back[:, :, D + 2 * LANES :] = tail.astype(BF16).reshape(GROUP, COLS, LANES)
 
 
-def fresh_kernel(own_keys, own_values, query, after, weighted_out, stats_out):
-    del after
+def fresh_kernel(own_keys, own_values, query, weighted_out, stats_out):
     lanes = lane_ids(COLS)
     low = lanes < HEAD_DIM
     stats = jnp.zeros((COLS, LANES), F32)
@@ -302,22 +305,22 @@
                 )(gathered, block, weight, sides[0][0] if sides else send)
             )
     (keys, own_keys), (values, own_values) = sides
+    with jax.named_scope("fresh"):
+        fresh, fresh_stats = pl.pallas_call(
+            fresh_kernel,
+            out_shape=(shape((COLS, D), F32), shape((COLS, LANES), F32)),
+            compiler_params=params(),
+            cost_estimate=cost(FRESH),
+        )(own_keys, own_values, query)
     with jax.named_scope("attend"):
         back = pl.pallas_call(
             attend_kernel,
             out_shape=shape((GROUP, COLS, BACK)),
+            in_specs=[VMEM_SPEC] * 5 + [ANY_SPEC],
             compiler_params=params(),
             cost_estimate=cost(ATTEND),
-        )(sent, keys, values, gathered, other)
+        )(sent, keys, values, gathered, other, fresh_stats)
     partial = lax.all_to_all(back, ("yh", "x"), 0, 0, tiled=True)
-    with jax.named_scope("fresh"):
-        fresh, fresh_stats = pl.pallas_call(
-            fresh_kernel,
-            out_shape=(shape((COLS, D), F32), shape((COLS, LANES), F32)),
-            in_specs=[VMEM_SPEC] * 3 + [ANY_SPEC],
-            compiler_params=params(),
-            cost_estimate=cost(FRESH),
-        )(own_keys, own_values, query, back)
     with jax.named_scope("finish"):
         attended, convolved = pl.pallas_call(
             finish_kernel,

time: 81.1 us -> 80.5 us (level); the launches traced: 79.8 us -> 80.2 us
  blocking collectives: 35.1 us -> 52.5 us
  waiting for transfers between devices: 8.99 us -> 0.01 us
  starting transfers between devices: 23.6 us -> 16.7 us
  Pallas kernels: 9.69 us -> 8.63 us
    all_to_all x0 -> x1, blocking collectives: none -> 17.3 us  [local(): partial = lax.all_to_all(back, ('yh', 'x'), 0, 0, tiled=True)]
    all_to_all x1 -> x0, waiting for transfers between devices: 8.98 us -> none  [local(): partial = lax.all_to_all(back, ('yh', 'x'), 0, 0, tiled=True)]
    all_to_all x1 -> x0, starting transfers between devices: 6.93 us -> none  [local(): partial = lax.all_to_all(back, ('yh', 'x'), 0, 0, tiled=True)]
    pallas_call x1, Pallas kernels: 3.61 us -> 2.54 us  [local(): pl.pallas_call(attend_kernel, out_shape=shape((GROUP, COLS, BACK)), in_sp...]
  transfers between devices with their start and end apart: 3 -> 2, of which waited for: 1 -> 0; matrix products, arithmetic and copies ran while one was open for 0% -> 0% of each run, Pallas kernels for 4% -> 4%
where the time goes in v6:
time: 80.5 us; the launch traced here: 80.2 us
  blocking collectives  52.5 us (65%)
  starting transfers between devices  16.7 us (21%)
  Pallas kernels  8.63 us (11%)
  local copies, waits for them, and re-layouts  1.64 us (2%)
    all_gather x1, blocking collectives, local(): gathered = lax.all_gather(payload, 'z', axis=0)  35.1 us
    all_to_all x1, blocking collectives, local(): partial = lax.all_to_all(back, ('yh', 'x'), 0, 0, tiled=True)  17.3 us
    ppermute x1, starting transfers between devices, local(): other = lax.ppermute(gathered[:, COLS:, :], 'core', [(0, 1), (1, 0)])  9.92 us
    all_to_all x1, starting transfers between devices, local(): sent = lax.all_to_all(send, ('yh', 'x'), 0, 0, tiled=True)  6.78 us
    pallas_call x1, Pallas kernels, local(): pl.pallas_call(attend_kernel, out_shape=shape((GROUP, COLS, BACK)), in_sp...  2.54 us
    pallas_call x2, Pallas kernels, local(): pl.pallas_call(project_kernel, out_shape=(shape((KEYS, D)), shape((COLS,...  2.26 us
    unnamed x16, local copies, waits for them, and re-layouts  1.61 us
  transfers between devices with their start and end apart: 2, of which 0 were waited for; matrix products, arithmetic and copies ran while one was open for 0% of the time, Pallas kernels for 4%

profile of v6, /device:TPU:1, one launch (start us, length us, event | category | flops | bytes accessed | tf_op | source)
XLA Modules:
  0.0 80.2 jit_solution(18123956836444776994)
XLA Ops:
  0.6 0.0 copy-start.4
  0.6 0.8 %copy-done.4 = bf16[9,5,320]{2,1,0:T(8,128)(2,1)S(1)} copy-done((bf16[9,5,320]{2,1,0:T(8,128)(2,1)S(1)}, bf16[9,5,320]{2,1,0:T(8,128)(2,1)}, u32[]{:S(2)}) %copy-start.4) | copy-done | bytes 28824
  1.4 0.8 copy-done.5
  2.2 0.2 payload.1
  2.5 35.1 %all-gather = bf16[768,640]{1,0:T(8,128)(2,1)S(1)} all-gather(bf16[48,640]{1,0:T(8,128)(2,1)S(1)} %payload.1), channel_id=2, replica_groups=mesh['z'=16,'yh'=2,'x'=4,'yl'=2,'core'=2] {'z'}, dimensions={0}, use_global_device_ids=true | all-gather | bytes 1044480 | tf_op jit(solution)/shard_map/all_gather | solution.py:285
  37.6 0.0 copy-done
  37.6 0.0 copy-done.6
  37.6 0.0 copy-done.7
  37.6 1.4 %prepare.1 = (bf16[8,32,1024]{2,1,0:T(8,128)(2,1)}, bf16[32,640]{1,0:T(8,128)(2,1)S(1)}) custom-call(bf16[32,640]{1,0:T(8,128)(2,1)S(1)} %bitcast.11, bf16[16,48,640]{2,1,0:T(8,128)(2,1)S(1)} %bitcast.5, bf16[640,640]{1,0:T(8,128)(2,1)S(1)} %copy-done, bf16[640,1024]{1,0:T(8,128)(2,1)S(1)} %copy-done.7), custom_call_target="tpu_custom_call" | custom-call | flops 2000000000 | tf_op jit(solution)/shard_map/prepare/pallas_call | solution.py:287
  39.1 6.8 %all-to-all-start = ((bf16[8,32,1024]{2,1,0:T(8,128)(2,1)}), bf16[8,32,1024]{2,1,0:T(8,128)(2,1)S(1)}, u32[]{:S(2)}, u32[]{:S(2)}) async-start(bf16[8,32,1024]{2,1,0:T(8,128)(2,1)} %get-tuple-element.12.after), calls=%async_computation | async-start | bytes 1048576 | tf_op jit(solution)/shard_map/all_to_all | solution.py:293
  45.9 0.0 copy-start.2
  45.9 9.9 %collective-permute-start = (bf16[16,16,640]{2,1,0:T(8,128)(2,1)S(1)}, bf16[16,16,640]{2,1,0:T(8,128)(2,1)S(1)}, u32[]{:S(2)}, u32[]{:S(2)}) collective-permute-start(bf16[16,16,640]{2,1,0:T(8,128)(2,1)S(1)} %slice.4), channel_id=1, source_target_pairs={{0,1},{1,0},{2,3},{3,2},{4,5},{5,4},{6,7},{7,6},{8,9},{9,8},{10,11... | collective-permute-start | bytes 983048 | tf_op jit(solution)/shard_map/ppermute | solution.py:294
  55.8 0.0 copy-done.1
  55.8 1.1 %keys.1 = (bf16[512,640]{1,0:T(8,128)(2,1)S(1)}, bf16[32,640]{1,0:T(8,128)(2,1)S(1)}) custom-call(bf16[16,48,640]{2,1,0:T(8,128)(2,1)S(1)} %bitcast.7, bf16[32,640]{1,0:T(8,128)(2,1)S(1)} %bitcast.12, bf16[640,640]{1,0:T(8,128)(2,1)S(1)} %copy-done.1, bf16[8,32,1024]{2,1,0:T(8,128)(2,1)} %get-tuple-element.12.after), custom_call_target="tpu_custom_call" | custom-call | flops 1000000000 | tf_op jit(solution)/shard_map/keys/pallas_call | solution.py:299
  56.9 0.0 copy-done.2
  57.0 1.1 %values.1 = (bf16[512,640]{1,0:T(8,128)(2,1)S(1)}, bf16[32,640]{1,0:T(8,128)(2,1)S(1)}) custom-call(bf16[16,48,640]{2,1,0:T(8,128)(2,1)S(1)} %bitcast.8, bf16[32,640]{1,0:T(8,128)(2,1)S(1)} %bitcast.13, bf16[640,640]{1,0:T(8,128)(2,1)S(1)} %copy-done.2, bf16[512,640]{1,0:T(8,128)(2,1)S(1)} %get-tuple-element.13.after.all_keys), custom_call_target="tpu_custom_call" | custom-call | flops 1000000000 | tf_op jit(solution)/shard_map/values/pallas_call | solution.py:299
  58.1 0.6 fresh.1
  58.7 0.0 collective-permute-done.other
  58.7 0.0 all-to-all-done.sent
  58.7 0.0 copy-start.3
  58.7 2.5 %attend.1 = bf16[8,32,1024]{2,1,0:T(8,128)(2,1)S(1)} custom-call(bf16[8,32,1024]{2,1,0:T(8,128)(2,1)S(1)} %all-to-all-done.sent, bf16[512,640]{1,0:T(8,128)(2,1)S(1)} %get-tuple-element.13.after.all_keys, bf16[512,640]{1,0:T(8,128)(2,1)S(1)} %get-tuple-element.14.all_values, bf16[16,48,640]{2,1,0:T(8,128)(2,1)S(1)} %bitcast.9, ...), custom_call_target="tpu_custom_call" | custom-call | flops 3000000000 | tf_op jit(solution)/shard_map/attend/pallas_call | solution.py:316
  61.2 17.3 %all_to_all.10.partial = bf16[8,32,1024]{2,1,0:T(8,128)(2,1)S(1)} all-to-all(bf16[8,32,1024]{2,1,0:T(8,128)(2,1)S(1)} %attend.1), channel_id=1, replica_groups=mesh['z'=16,'yh'=2,'x'=4,'yl'=2,'core'=2] {'yh','x'}, dimensions={0} | all-to-all | bytes 1048576 | tf_op jit(solution)/shard_map/all_to_all | solution.py:323
  78.6 0.0 copy-done.3
  78.6 1.6 %finish.1 = (bf16[32,640]{1,0:T(8,128)(2,1)}, bf16[32,320]{1,0:T(8,128)(2,1)}) custom-call(bf16[8,32,1024]{2,1,0:T(8,128)(2,1)S(1)} %all_to_all.10.partial, f32[32,640]{1,0:T(8,128)S(1)} %get-tuple-element.19.fresh, f32[32,128]{1,0:T(8,128)S(1)} %get-tuple-element.18.after.fresh_stats, bf16[640,640]{1,0:T(8,128)(2,1)S(1)} %copy-done.3), custom_call_target="tpu_custom_call" | custom-call | flops 2000000000 | tf_op jit(solution)/shard_map/finish/pallas_call | solution.py:325
  (6 shorter events, 0.0 us)
Async XLA Ops:
  0.6 0.8 %copy-start.4 = (bf16[9,5,320]{2,1,0:T(8,128)(2,1)S(1)}, bf16[9,5,320]{2,1,0:T(8,128)(2,1)}, u32[]{:S(2)}) copy-start(bf16[9,5,320]{2,1,0:T(8,128)(2,1)} %taps_hbm.1) | copy-start | bytes 86404
  1.4 0.8 copy-start.5
  2.2 35.4 %copy-start = (bf16[640,640]{1,0:T(8,128)(2,1)S(1)}, bf16[640,640]{1,0:T(8,128)(2,1)}, u32[]{:S(2)}) copy-start(bf16[640,640]{1,0:T(8,128)(2,1)} %wq.1) | copy-start | bytes 2457604
  2.2 35.4 %copy-start.6 = (bf16[1,32,640]{2,1,0:T(8,128)(2,1)S(1)}, bf16[1,32,640]{2,1,0:T(8,128)(2,1)}, u32[]{:S(2)}) copy-start(bf16[1,32,640]{2,1,0:T(8,128)(2,1)} %param.8) | copy-start | bytes 122884
  2.2 35.4 %copy-start.7 = (bf16[640,1024]{1,0:T(8,128)(2,1)S(1)}, bf16[640,1024]{1,0:T(8,128)(2,1)}, u32[]{:S(2)}) copy-start(bf16[640,1024]{1,0:T(8,128)(2,1)} %constant.2.clone.slices) | copy-start | bytes 3932164
  39.1 16.8 %copy-start.1 = (bf16[640,640]{1,0:T(8,128)(2,1)S(1)}, bf16[640,640]{1,0:T(8,128)(2,1)}, u32[]{:S(2)}) copy-start(bf16[640,640]{1,0:T(8,128)(2,1)} %weight.2) | copy-start | bytes 2457604
  39.1 19.6 %all-to-all-start = ((bf16[8,32,1024]{2,1,0:T(8,128)(2,1)}), bf16[8,32,1024]{2,1,0:T(8,128)(2,1)S(1)}, u32[]{:S(2)}, u32[]{:S(2)}) async-start(bf16[8,32,1024]{2,1,0:T(8,128)(2,1)} %get-tuple-element.12.after), calls=%async_computation | async-start | bytes 1048576 | tf_op jit(solution)/shard_map/all_to_all | solution.py:293
  45.9 11.1 %copy-start.2 = (bf16[640,640]{1,0:T(8,128)(2,1)S(1)}, bf16[640,640]{1,0:T(8,128)(2,1)}, u32[]{:S(2)}) copy-start(bf16[640,640]{1,0:T(8,128)(2,1)} %weight.3) | copy-start | bytes 2457604
  45.9 12.8 %collective-permute-start = (bf16[16,16,640]{2,1,0:T(8,128)(2,1)S(1)}, bf16[16,16,640]{2,1,0:T(8,128)(2,1)S(1)}, u32[]{:S(2)}, u32[]{:S(2)}) collective-permute-start(bf16[16,16,640]{2,1,0:T(8,128)(2,1)S(1)} %slice.4), channel_id=1, source_target_pairs={{0,1},{1,0},{2,3},{3,2},{4,5},{5,4},{6,7},{7,6},{8,9},{9,8},{10,11... | collective-permute-start | bytes 983048 | tf_op jit(solution)/shard_map/ppermute | solution.py:294
  58.7 19.9 %copy-start.3 = (bf16[640,640]{1,0:T(8,128)(2,1)S(1)}, bf16[640,640]{1,0:T(8,128)(2,1)}, u32[]{:S(2)}) copy-start(bf16[640,640]{1,0:T(8,128)(2,1)} %wo.1) | copy-start | bytes 2457604

commit v7 on v6

--- a/solution.py
+++ b/solution.py
@@ -23,6 +23,7 @@
 BACK = D + 3 * LANES
 VMEM = 24 * 1024 * 1024
 PAYLOAD, PREPARE, PROJECT, ATTEND, FRESH, FINISH = 1, 2, 1, 3, 0.2, 2
+AHEAD = 3
 STATS_AT = (64, 84, 104)
 F32 = jnp.float32
 BF16 = jnp.bfloat16
@@ -72,7 +73,12 @@
     return lax.axis_index("z"), lax.axis_index("yh") * 4 + lax.axis_index("x")
 
 
-def payload_kernel(stale_hbm, taps_hbm, gather, stale, taps, rows, sems):
+def ahead_kernel(out):
+    out[...] = jnp.zeros_like(out)
+
+
+def payload_kernel(stale_hbm, taps_hbm, after, gather, stale, taps, rows, sems):
+    del after
     copies = [
         pltpu.make_async_copy(taps_hbm, taps, sems.at[0]),
         pltpu.make_async_copy(stale_hbm, stale, sems.at[1]),
@@ -268,11 +274,18 @@
 def local(block_input, stale_input, query_weight, key_weight, value_weight, out_weight, conv_weight):
     block = block_input.reshape(COLS, D)
     stale = stale_input.reshape(COLS, D)
+    with jax.named_scope("ahead"):
+        ahead = pl.pallas_call(
+            ahead_kernel,
+            out_shape=shape((8, LANES), F32),
+            compiler_params=params(),
+            cost_estimate=cost(AHEAD),
+        )()
     with jax.named_scope("payload"):
         payload = pl.pallas_call(
             payload_kernel,
             out_shape=shape((COLS + 16, D)),
-            in_specs=[HBM_SPEC] * 2,
+            in_specs=[HBM_SPEC] * 2 + [ANY_SPEC],
             scratch_shapes=[
                 pltpu.VMEM((COLS, D), BF16),
                 pltpu.VMEM((9, OWN, CO), BF16),
@@ -281,7 +294,7 @@
             ],
             compiler_params=params(),
             cost_estimate=cost(PAYLOAD),
-        )(stale, conv_weight)
+        )(stale, conv_weight, ahead)
     gathered = lax.all_gather(payload, "z", axis=0)
     with jax.named_scope("prepare"):
         send, query = pl.pallas_call(

time: 80.5 us -> 79.7 us (0.990)
  no operation moved by 1% of the time
where the time goes in v7:
time: 79.7 us; the launch traced here: 79.4 us
  blocking collectives  52.5 us (66%)
  starting transfers between devices  16.7 us (21%)
  Pallas kernels  8.63 us (11%)
  local copies, waits for them, and re-layouts  0.85 us (1%)
    all_gather x1, blocking collectives, local(): gathered = lax.all_gather(payload, 'z', axis=0)  35.1 us
    all_to_all x1, blocking collectives, local(): partial = lax.all_to_all(back, ('yh', 'x'), 0, 0, tiled=True)  17.3 us
    ppermute x1, starting transfers between devices, local(): other = lax.ppermute(gathered[:, COLS:, :], 'core', [(0, 1), (1, 0)])  9.92 us
    all_to_all x1, starting transfers between devices, local(): sent = lax.all_to_all(send, ('yh', 'x'), 0, 0, tiled=True)  6.78 us
    pallas_call x1, Pallas kernels, local(): pl.pallas_call(attend_kernel, out_shape=shape((GROUP, COLS, BACK)), in_sp...  2.54 us
    pallas_call x2, Pallas kernels, local(): pl.pallas_call(project_kernel, out_shape=(shape((KEYS, D)), shape((COLS,...  2.25 us
    pallas_call x1, Pallas kernels, local(): pl.pallas_call(finish_kernel, out_shape=(shape((COLS, D)), shape((COLS, C...  1.6 us
  transfers between devices with their start and end apart: 2, of which 0 were waited for; matrix products, arithmetic and copies ran while one was open for 0% of the time, Pallas kernels for 4%

profile of v7, /device:TPU:1, one launch (start us, length us, event | category | flops | bytes accessed | tf_op | source)
XLA Modules:
  0.0 79.4 jit_solution(11580498453663208163)
XLA Ops:
  0.6 0.0 copy-start.4
  0.6 0.0 copy-start.5
  0.7 0.8 copy-done.4
  1.4 0.0 copy-done.5
  1.5 0.2 payload.1
  1.7 35.1 %all-gather = bf16[768,640]{1,0:T(8,128)(2,1)S(1)} all-gather(bf16[48,640]{1,0:T(8,128)(2,1)S(1)} %payload.1), channel_id=2, replica_groups=mesh['z'=16,'yh'=2,'x'=4,'yl'=2,'core'=2] {'z'}, dimensions={0}, use_global_device_ids=true | all-gather | bytes 1044480 | tf_op jit(solution)/shard_map/all_gather | solution.py:298
  36.8 0.0 copy-done
  36.8 0.0 copy-done.6
  36.8 0.0 copy-done.7
  36.9 1.4 %prepare.1 = (bf16[8,32,1024]{2,1,0:T(8,128)(2,1)}, bf16[32,640]{1,0:T(8,128)(2,1)S(1)}) custom-call(bf16[32,640]{1,0:T(8,128)(2,1)S(1)} %bitcast.11, bf16[16,48,640]{2,1,0:T(8,128)(2,1)S(1)} %bitcast.5, bf16[640,640]{1,0:T(8,128)(2,1)S(1)} %copy-done, bf16[640,1024]{1,0:T(8,128)(2,1)S(1)} %copy-done.7), custom_call_target="tpu_custom_call" | custom-call | flops 2000000000 | tf_op jit(solution)/shard_map/prepare/pallas_call | solution.py:300
  38.3 6.8 %all-to-all-start = ((bf16[8,32,1024]{2,1,0:T(8,128)(2,1)}), bf16[8,32,1024]{2,1,0:T(8,128)(2,1)S(1)}, u32[]{:S(2)}, u32[]{:S(2)}) async-start(bf16[8,32,1024]{2,1,0:T(8,128)(2,1)} %get-tuple-element.12.after), calls=%async_computation | async-start | bytes 1048576 | tf_op jit(solution)/shard_map/all_to_all | solution.py:306
  45.1 0.0 copy-start.2
  45.1 9.9 %collective-permute-start = (bf16[16,16,640]{2,1,0:T(8,128)(2,1)S(1)}, bf16[16,16,640]{2,1,0:T(8,128)(2,1)S(1)}, u32[]{:S(2)}, u32[]{:S(2)}) collective-permute-start(bf16[16,16,640]{2,1,0:T(8,128)(2,1)S(1)} %slice.4), channel_id=1, source_target_pairs={{0,1},{1,0},{2,3},{3,2},{4,5},{5,4},{6,7},{7,6},{8,9},{9,8},{10,11... | collective-permute-start | bytes 983048 | tf_op jit(solution)/shard_map/ppermute | solution.py:307
  55.0 0.0 copy-done.1
  55.1 1.1 %keys.1 = (bf16[512,640]{1,0:T(8,128)(2,1)S(1)}, bf16[32,640]{1,0:T(8,128)(2,1)S(1)}) custom-call(bf16[16,48,640]{2,1,0:T(8,128)(2,1)S(1)} %bitcast.7, bf16[32,640]{1,0:T(8,128)(2,1)S(1)} %bitcast.12, bf16[640,640]{1,0:T(8,128)(2,1)S(1)} %copy-done.1, bf16[8,32,1024]{2,1,0:T(8,128)(2,1)} %get-tuple-element.12.after), custom_call_target="tpu_custom_call" | custom-call | flops 1000000000 | tf_op jit(solution)/shard_map/keys/pallas_call | solution.py:312
  56.2 0.0 copy-done.2
  56.2 1.1 %values.1 = (bf16[512,640]{1,0:T(8,128)(2,1)S(1)}, bf16[32,640]{1,0:T(8,128)(2,1)S(1)}) custom-call(bf16[16,48,640]{2,1,0:T(8,128)(2,1)S(1)} %bitcast.8, bf16[32,640]{1,0:T(8,128)(2,1)S(1)} %bitcast.13, bf16[640,640]{1,0:T(8,128)(2,1)S(1)} %copy-done.2, bf16[512,640]{1,0:T(8,128)(2,1)S(1)} %get-tuple-element.13.after.all_keys), custom_call_target="tpu_custom_call" | custom-call | flops 1000000000 | tf_op jit(solution)/shard_map/values/pallas_call | solution.py:312
  57.3 0.6 fresh.1
  57.9 0.0 collective-permute-done.other
  57.9 0.0 all-to-all-done.sent
  57.9 0.0 copy-start.3
  57.9 2.5 %attend.1 = bf16[8,32,1024]{2,1,0:T(8,128)(2,1)S(1)} custom-call(bf16[8,32,1024]{2,1,0:T(8,128)(2,1)S(1)} %all-to-all-done.sent, bf16[512,640]{1,0:T(8,128)(2,1)S(1)} %get-tuple-element.13.after.all_keys, bf16[512,640]{1,0:T(8,128)(2,1)S(1)} %get-tuple-element.14.all_values, bf16[16,48,640]{2,1,0:T(8,128)(2,1)S(1)} %bitcast.9, ...), custom_call_target="tpu_custom_call" | custom-call | flops 3000000000 | tf_op jit(solution)/shard_map/attend/pallas_call | solution.py:329
  60.5 17.3 %all_to_all.10.partial = bf16[8,32,1024]{2,1,0:T(8,128)(2,1)S(1)} all-to-all(bf16[8,32,1024]{2,1,0:T(8,128)(2,1)S(1)} %attend.1), channel_id=1, replica_groups=mesh['z'=16,'yh'=2,'x'=4,'yl'=2,'core'=2] {'yh','x'}, dimensions={0} | all-to-all | bytes 1048576 | tf_op jit(solution)/shard_map/all_to_all | solution.py:336
  77.8 1.6 %finish.1 = (bf16[32,640]{1,0:T(8,128)(2,1)}, bf16[32,320]{1,0:T(8,128)(2,1)}) custom-call(bf16[8,32,1024]{2,1,0:T(8,128)(2,1)S(1)} %all_to_all.10.partial, f32[32,640]{1,0:T(8,128)S(1)} %get-tuple-element.19.fresh, f32[32,128]{1,0:T(8,128)S(1)} %get-tuple-element.18.after.fresh_stats, bf16[640,640]{1,0:T(8,128)(2,1)S(1)} %copy-done.3), custom_call_target="tpu_custom_call" | custom-call | flops 2000000000 | tf_op jit(solution)/shard_map/finish/pallas_call | solution.py:338
  (7 shorter events, 0.0 us)
Async XLA Ops:
  0.6 0.8 %copy-start.4 = (bf16[9,5,320]{2,1,0:T(8,128)(2,1)S(1)}, bf16[9,5,320]{2,1,0:T(8,128)(2,1)}, u32[]{:S(2)}) copy-start(bf16[9,5,320]{2,1,0:T(8,128)(2,1)} %taps_hbm.1) | copy-start | bytes 86404
  0.6 0.8 %copy-start.5 = (bf16[1,32,640]{2,1,0:T(8,128)(2,1)S(1)}, bf16[1,32,640]{2,1,0:T(8,128)(2,1)}, u32[]{:S(2)}) copy-start(bf16[1,32,640]{2,1,0:T(8,128)(2,1)} %param.9) | copy-start | bytes 122884
  1.4 35.4 %copy-start = (bf16[640,640]{1,0:T(8,128)(2,1)S(1)}, bf16[640,640]{1,0:T(8,128)(2,1)}, u32[]{:S(2)}) copy-start(bf16[640,640]{1,0:T(8,128)(2,1)} %wq.1) | copy-start | bytes 2457604
  1.4 35.4 %copy-start.6 = (bf16[1,32,640]{2,1,0:T(8,128)(2,1)S(1)}, bf16[1,32,640]{2,1,0:T(8,128)(2,1)}, u32[]{:S(2)}) copy-start(bf16[1,32,640]{2,1,0:T(8,128)(2,1)} %param.8) | copy-start | bytes 122884
  1.5 35.4 %copy-start.7 = (bf16[640,1024]{1,0:T(8,128)(2,1)S(1)}, bf16[640,1024]{1,0:T(8,128)(2,1)}, u32[]{:S(2)}) copy-start(bf16[640,1024]{1,0:T(8,128)(2,1)} %constant.2.clone.slices) | copy-start | bytes 3932164
  38.3 16.8 %copy-start.1 = (bf16[640,640]{1,0:T(8,128)(2,1)S(1)}, bf16[640,640]{1,0:T(8,128)(2,1)}, u32[]{:S(2)}) copy-start(bf16[640,640]{1,0:T(8,128)(2,1)} %weight.2) | copy-start | bytes 2457604
  38.3 19.6 %all-to-all-start = ((bf16[8,32,1024]{2,1,0:T(8,128)(2,1)}), bf16[8,32,1024]{2,1,0:T(8,128)(2,1)S(1)}, u32[]{:S(2)}, u32[]{:S(2)}) async-start(bf16[8,32,1024]{2,1,0:T(8,128)(2,1)} %get-tuple-element.12.after), calls=%async_computation | async-start | bytes 1048576 | tf_op jit(solution)/shard_map/all_to_all | solution.py:306
  45.1 11.1 %copy-start.2 = (bf16[640,640]{1,0:T(8,128)(2,1)S(1)}, bf16[640,640]{1,0:T(8,128)(2,1)}, u32[]{:S(2)}) copy-start(bf16[640,640]{1,0:T(8,128)(2,1)} %weight.3) | copy-start | bytes 2457604
  45.1 12.8 %collective-permute-start = (bf16[16,16,640]{2,1,0:T(8,128)(2,1)S(1)}, bf16[16,16,640]{2,1,0:T(8,128)(2,1)S(1)}, u32[]{:S(2)}, u32[]{:S(2)}) collective-permute-start(bf16[16,16,640]{2,1,0:T(8,128)(2,1)S(1)} %slice.4), channel_id=1, source_target_pairs={{0,1},{1,0},{2,3},{3,2},{4,5},{5,4},{6,7},{7,6},{8,9},{9,8},{10,11... | collective-permute-start | bytes 983048 | tf_op jit(solution)/shard_map/ppermute | solution.py:307
  57.9 19.9 %copy-start.3 = (bf16[640,640]{1,0:T(8,128)(2,1)S(1)}, bf16[640,640]{1,0:T(8,128)(2,1)}, u32[]{:S(2)}) copy-start(bf16[640,640]{1,0:T(8,128)(2,1)} %wo.1) | copy-start | bytes 2457604

commit v8 on v7

--- a/solution.py
+++ b/solution.py
@@ -180,8 +180,9 @@
         query = sent[:, :, at].reshape(QUERIES, LANES)
         keys, values = all_keys[:, at], all_values[:, at]
         row_max, row_sum, weighted = attend_pair(query, keys, values, masked, lanes)
-        weighted = weighted / row_sum
-        mixed = jnp.where(low, weighted[:QUERIES], weighted[QUERIES:])
+        mixed = jnp.where(low, weighted[:QUERIES], weighted[QUERIES:]) / jnp.where(
+            low, row_sum[:QUERIES], row_sum[QUERIES:]
+        )
         back[:, :, at] = mixed.astype(BF16).reshape(GROUP, COLS, LANES)
         for half in range(2):
             head = 2 * pair + half
@@ -239,7 +240,8 @@
     whole = scale[GROUP] * sums[GROUP]
     for p in parts:
         whole = whole + p
-    weights = [p / whole for p in parts] + [scale[GROUP] / whole]
+    share = 1.0 / whole
+    weights = [p * share for p in parts] + [scale[GROUP] * share]
     low = lane_ids(COLS) < HEAD_DIM
     mixed = []
     for pair in range(PAIRS):

time: 79.7 us -> 79.7 us (level)
  no operation moved by 1% of the time
where the time goes in v8:
time: 79.7 us; the launch traced here: 79.4 us
  blocking collectives  52.5 us (66%)
  starting transfers between devices  16.7 us (21%)
  Pallas kernels  8.61 us (11%)
  local copies, waits for them, and re-layouts  0.85 us (1%)
    all_gather x1, blocking collectives, local(): gathered = lax.all_gather(payload, 'z', axis=0)  35.1 us
    all_to_all x1, blocking collectives, local(): partial = lax.all_to_all(back, ('yh', 'x'), 0, 0, tiled=True)  17.3 us
    ppermute x1, starting transfers between devices, local(): other = lax.ppermute(gathered[:, COLS:, :], 'core', [(0, 1), (1, 0)])  9.92 us
    all_to_all x1, starting transfers between devices, local(): sent = lax.all_to_all(send, ('yh', 'x'), 0, 0, tiled=True)  6.78 us
    pallas_call x1, Pallas kernels, local(): pl.pallas_call(attend_kernel, out_shape=shape((GROUP, COLS, BACK)), in_sp...  2.52 us
    pallas_call x2, Pallas kernels, local(): pl.pallas_call(project_kernel, out_shape=(shape((KEYS, D)), shape((COLS,...  2.25 us
    pallas_call x1, Pallas kernels, local(): pl.pallas_call(finish_kernel, out_shape=(shape((COLS, D)), shape((COLS, C...  1.6 us
  transfers between devices with their start and end apart: 2, of which 0 were waited for; matrix products, arithmetic and copies ran while one was open for 0% of the time, Pallas kernels for 4%

profile of v8, /device:TPU:1, one launch (start us, length us, event | category | flops | bytes accessed | tf_op | source)
XLA Modules:
  0.0 79.4 jit_solution(2999902312997252540)
XLA Ops:
  0.6 0.0 copy-start.4
  0.6 0.0 copy-start.5
  0.7 0.8 copy-done.4
  1.4 0.0 copy-done.5
  1.5 0.2 payload.1
  1.7 35.1 %all-gather = bf16[768,640]{1,0:T(8,128)(2,1)S(1)} all-gather(bf16[48,640]{1,0:T(8,128)(2,1)S(1)} %payload.1), channel_id=2, replica_groups=mesh['z'=16,'yh'=2,'x'=4,'yl'=2,'core'=2] {'z'}, dimensions={0}, use_global_device_ids=true | all-gather | bytes 1044480 | tf_op jit(solution)/shard_map/all_gather | solution.py:300
  36.8 0.0 copy-done
  36.8 0.0 copy-done.6
  36.8 0.0 copy-done.7
  36.9 1.4 %prepare.1 = (bf16[8,32,1024]{2,1,0:T(8,128)(2,1)}, bf16[32,640]{1,0:T(8,128)(2,1)S(1)}) custom-call(bf16[32,640]{1,0:T(8,128)(2,1)S(1)} %bitcast.11, bf16[16,48,640]{2,1,0:T(8,128)(2,1)S(1)} %bitcast.5, bf16[640,640]{1,0:T(8,128)(2,1)S(1)} %copy-done, bf16[640,1024]{1,0:T(8,128)(2,1)S(1)} %copy-done.7), custom_call_target="tpu_custom_call" | custom-call | flops 2000000000 | tf_op jit(solution)/shard_map/prepare/pallas_call | solution.py:302
  38.3 6.8 %all-to-all-start = ((bf16[8,32,1024]{2,1,0:T(8,128)(2,1)}), bf16[8,32,1024]{2,1,0:T(8,128)(2,1)S(1)}, u32[]{:S(2)}, u32[]{:S(2)}) async-start(bf16[8,32,1024]{2,1,0:T(8,128)(2,1)} %get-tuple-element.12.after), calls=%async_computation | async-start | bytes 1048576 | tf_op jit(solution)/shard_map/all_to_all | solution.py:308
  45.1 0.0 copy-start.2
  45.1 9.9 %collective-permute-start = (bf16[16,16,640]{2,1,0:T(8,128)(2,1)S(1)}, bf16[16,16,640]{2,1,0:T(8,128)(2,1)S(1)}, u32[]{:S(2)}, u32[]{:S(2)}) collective-permute-start(bf16[16,16,640]{2,1,0:T(8,128)(2,1)S(1)} %slice.4), channel_id=1, source_target_pairs={{0,1},{1,0},{2,3},{3,2},{4,5},{5,4},{6,7},{7,6},{8,9},{9,8},{10,11... | collective-permute-start | bytes 983048 | tf_op jit(solution)/shard_map/ppermute | solution.py:309
  55.0 0.0 copy-done.1
  55.1 1.1 %keys.1 = (bf16[512,640]{1,0:T(8,128)(2,1)S(1)}, bf16[32,640]{1,0:T(8,128)(2,1)S(1)}) custom-call(bf16[16,48,640]{2,1,0:T(8,128)(2,1)S(1)} %bitcast.7, bf16[32,640]{1,0:T(8,128)(2,1)S(1)} %bitcast.12, bf16[640,640]{1,0:T(8,128)(2,1)S(1)} %copy-done.1, bf16[8,32,1024]{2,1,0:T(8,128)(2,1)} %get-tuple-element.12.after), custom_call_target="tpu_custom_call" | custom-call | flops 1000000000 | tf_op jit(solution)/shard_map/keys/pallas_call | solution.py:314
  56.2 0.0 copy-done.2
  56.2 1.1 %values.1 = (bf16[512,640]{1,0:T(8,128)(2,1)S(1)}, bf16[32,640]{1,0:T(8,128)(2,1)S(1)}) custom-call(bf16[16,48,640]{2,1,0:T(8,128)(2,1)S(1)} %bitcast.8, bf16[32,640]{1,0:T(8,128)(2,1)S(1)} %bitcast.13, bf16[640,640]{1,0:T(8,128)(2,1)S(1)} %copy-done.2, bf16[512,640]{1,0:T(8,128)(2,1)S(1)} %get-tuple-element.13.after.all_keys), custom_call_target="tpu_custom_call" | custom-call | flops 1000000000 | tf_op jit(solution)/shard_map/values/pallas_call | solution.py:314
  57.3 0.6 fresh.1
  57.9 0.0 collective-permute-done.other
  57.9 0.0 all-to-all-done.sent
  57.9 0.0 copy-start.3
  57.9 2.5 %attend.1 = bf16[8,32,1024]{2,1,0:T(8,128)(2,1)S(1)} custom-call(bf16[8,32,1024]{2,1,0:T(8,128)(2,1)S(1)} %all-to-all-done.sent, bf16[512,640]{1,0:T(8,128)(2,1)S(1)} %get-tuple-element.13.after.all_keys, bf16[512,640]{1,0:T(8,128)(2,1)S(1)} %get-tuple-element.14.all_values, bf16[16,48,640]{2,1,0:T(8,128)(2,1)S(1)} %bitcast.9, ...), custom_call_target="tpu_custom_call" | custom-call | flops 3000000000 | tf_op jit(solution)/shard_map/attend/pallas_call | solution.py:331
  60.4 17.3 %all_to_all.10.partial = bf16[8,32,1024]{2,1,0:T(8,128)(2,1)S(1)} all-to-all(bf16[8,32,1024]{2,1,0:T(8,128)(2,1)S(1)} %attend.1), channel_id=1, replica_groups=mesh['z'=16,'yh'=2,'x'=4,'yl'=2,'core'=2] {'yh','x'}, dimensions={0} | all-to-all | bytes 1048576 | tf_op jit(solution)/shard_map/all_to_all | solution.py:338
  77.8 1.6 %finish.1 = (bf16[32,640]{1,0:T(8,128)(2,1)}, bf16[32,320]{1,0:T(8,128)(2,1)}) custom-call(bf16[8,32,1024]{2,1,0:T(8,128)(2,1)S(1)} %all_to_all.10.partial, f32[32,640]{1,0:T(8,128)S(1)} %get-tuple-element.19.fresh, f32[32,128]{1,0:T(8,128)S(1)} %get-tuple-element.18.after.fresh_stats, bf16[640,640]{1,0:T(8,128)(2,1)S(1)} %copy-done.3), custom_call_target="tpu_custom_call" | custom-call | flops 2000000000 | tf_op jit(solution)/shard_map/finish/pallas_call | solution.py:340
  (7 shorter events, 0.0 us)
Async XLA Ops:
  0.6 0.8 %copy-start.4 = (bf16[9,5,320]{2,1,0:T(8,128)(2,1)S(1)}, bf16[9,5,320]{2,1,0:T(8,128)(2,1)}, u32[]{:S(2)}) copy-start(bf16[9,5,320]{2,1,0:T(8,128)(2,1)} %taps_hbm.1) | copy-start | bytes 86404
  0.6 0.8 %copy-start.5 = (bf16[1,32,640]{2,1,0:T(8,128)(2,1)S(1)}, bf16[1,32,640]{2,1,0:T(8,128)(2,1)}, u32[]{:S(2)}) copy-start(bf16[1,32,640]{2,1,0:T(8,128)(2,1)} %param.9) | copy-start | bytes 122884
  1.4 35.4 %copy-start = (bf16[640,640]{1,0:T(8,128)(2,1)S(1)}, bf16[640,640]{1,0:T(8,128)(2,1)}, u32[]{:S(2)}) copy-start(bf16[640,640]{1,0:T(8,128)(2,1)} %wq.1) | copy-start | bytes 2457604
  1.4 35.4 %copy-start.6 = (bf16[1,32,640]{2,1,0:T(8,128)(2,1)S(1)}, bf16[1,32,640]{2,1,0:T(8,128)(2,1)}, u32[]{:S(2)}) copy-start(bf16[1,32,640]{2,1,0:T(8,128)(2,1)} %param.8) | copy-start | bytes 122884
  1.5 35.4 %copy-start.7 = (bf16[640,1024]{1,0:T(8,128)(2,1)S(1)}, bf16[640,1024]{1,0:T(8,128)(2,1)}, u32[]{:S(2)}) copy-start(bf16[640,1024]{1,0:T(8,128)(2,1)} %constant.2.clone.slices) | copy-start | bytes 3932164
  38.3 16.8 %copy-start.1 = (bf16[640,640]{1,0:T(8,128)(2,1)S(1)}, bf16[640,640]{1,0:T(8,128)(2,1)}, u32[]{:S(2)}) copy-start(bf16[640,640]{1,0:T(8,128)(2,1)} %weight.2) | copy-start | bytes 2457604
  38.3 19.6 %all-to-all-start = ((bf16[8,32,1024]{2,1,0:T(8,128)(2,1)}), bf16[8,32,1024]{2,1,0:T(8,128)(2,1)S(1)}, u32[]{:S(2)}, u32[]{:S(2)}) async-start(bf16[8,32,1024]{2,1,0:T(8,128)(2,1)} %get-tuple-element.12.after), calls=%async_computation | async-start | bytes 1048576 | tf_op jit(solution)/shard_map/all_to_all | solution.py:308
  45.1 11.1 %copy-start.2 = (bf16[640,640]{1,0:T(8,128)(2,1)S(1)}, bf16[640,640]{1,0:T(8,128)(2,1)}, u32[]{:S(2)}) copy-start(bf16[640,640]{1,0:T(8,128)(2,1)} %weight.3) | copy-start | bytes 2457604
  45.1 12.8 %collective-permute-start = (bf16[16,16,640]{2,1,0:T(8,128)(2,1)S(1)}, bf16[16,16,640]{2,1,0:T(8,128)(2,1)S(1)}, u32[]{:S(2)}, u32[]{:S(2)}) collective-permute-start(bf16[16,16,640]{2,1,0:T(8,128)(2,1)S(1)} %slice.4), channel_id=1, source_target_pairs={{0,1},{1,0},{2,3},{3,2},{4,5},{5,4},{6,7},{7,6},{8,9},{9,8},{10,11... | collective-permute-start | bytes 983048 | tf_op jit(solution)/shard_map/ppermute | solution.py:309
  57.9 19.9 %copy-start.3 = (bf16[640,640]{1,0:T(8,128)(2,1)S(1)}, bf16[640,640]{1,0:T(8,128)(2,1)}, u32[]{:S(2)}) copy-start(bf16[640,640]{1,0:T(8,128)(2,1)} %wo.1) | copy-start | bytes 2457604

commit v9 on v8

--- a/solution.py
+++ b/solution.py
@@ -120,10 +120,10 @@
 
 def project_kernel(gathered, block, weight, after, out, own):
     del after
-    normed = layer_norm(gathered[:, :COLS, :].reshape(KEYS, D).astype(F32))
-    fresh = layer_norm(block[...].astype(F32))
-    out[...] = dot(normed, weight[...]).astype(BF16)
-    own[...] = dot(fresh, weight[...]).astype(BF16)
+    rows = jnp.concatenate([gathered[:, :COLS, :].reshape(KEYS, D), block[...]], axis=0)
+    projected = dot(layer_norm(rows.astype(F32)), weight[...]).astype(BF16)
+    out[...] = projected[:KEYS]
+    own[...] = projected[KEYS:]
 
 
 def attend_pair(query, keys, values, masked, lanes):

time: 79.7 us -> 79.6 us (level)
  transfers between devices with their start and end apart: 2 -> 2, of which waited for: 0 -> 0; matrix products, arithmetic and copies ran while one was open for 0% -> 0% of each run, Pallas kernels for 4% -> 3%
where the time goes in v9:
time: 79.6 us; the launch traced here: 79.2 us
  blocking collectives  52.4 us (66%)
  starting transfers between devices  16.7 us (21%)
  Pallas kernels  8.54 us (11%)
  local copies, waits for them, and re-layouts  0.85 us (1%)
    all_gather x1, blocking collectives, local(): gathered = lax.all_gather(payload, 'z', axis=0)  35.1 us
    all_to_all x1, blocking collectives, local(): partial = lax.all_to_all(back, ('yh', 'x'), 0, 0, tiled=True)  17.2 us
    ppermute x1, starting transfers between devices, local(): other = lax.ppermute(gathered[:, COLS:, :], 'core', [(0, 1), (1, 0)])  9.92 us
    all_to_all x1, starting transfers between devices, local(): sent = lax.all_to_all(send, ('yh', 'x'), 0, 0, tiled=True)  6.78 us
    pallas_call x1, Pallas kernels, local(): pl.pallas_call(attend_kernel, out_shape=shape((GROUP, COLS, BACK)), in_sp...  2.52 us
    pallas_call x2, Pallas kernels, local(): pl.pallas_call(project_kernel, out_shape=(shape((KEYS, D)), shape((COLS,...  2.18 us
    pallas_call x1, Pallas kernels, local(): pl.pallas_call(finish_kernel, out_shape=(shape((COLS, D)), shape((COLS, C...  1.6 us
  transfers between devices with their start and end apart: 2, of which 0 were waited for; matrix products, arithmetic and copies ran while one was open for 0% of the time, Pallas kernels for 3%

profile of v9, /device:TPU:1, one launch (start us, length us, event | category | flops | bytes accessed | tf_op | source)
XLA Modules:
  0.0 79.2 jit_solution(5890625999989671982)
XLA Ops:
  0.6 0.0 copy-start.4
  0.6 0.0 copy-start.5
  0.7 0.8 copy-done.4
  1.4 0.0 copy-done.5
  1.5 0.2 payload.1
  1.7 35.1 %all-gather = bf16[768,640]{1,0:T(8,128)(2,1)S(1)} all-gather(bf16[48,640]{1,0:T(8,128)(2,1)S(1)} %payload.1), channel_id=2, replica_groups=mesh['z'=16,'yh'=2,'x'=4,'yl'=2,'core'=2] {'z'}, dimensions={0}, use_global_device_ids=true | all-gather | bytes 1044480 | tf_op jit(solution)/shard_map/all_gather | solution.py:300
  36.8 0.0 copy-done
  36.8 0.0 copy-done.6
  36.8 0.0 copy-done.7
  36.9 1.4 %prepare.1 = (bf16[8,32,1024]{2,1,0:T(8,128)(2,1)}, bf16[32,640]{1,0:T(8,128)(2,1)S(1)}) custom-call(bf16[32,640]{1,0:T(8,128)(2,1)S(1)} %bitcast.11, bf16[16,48,640]{2,1,0:T(8,128)(2,1)S(1)} %bitcast.5, bf16[640,640]{1,0:T(8,128)(2,1)S(1)} %copy-done, bf16[640,1024]{1,0:T(8,128)(2,1)S(1)} %copy-done.7), custom_call_target="tpu_custom_call" | custom-call | flops 2000000000 | tf_op jit(solution)/shard_map/prepare/pallas_call | solution.py:302
  38.3 6.8 %all-to-all-start = ((bf16[8,32,1024]{2,1,0:T(8,128)(2,1)}), bf16[8,32,1024]{2,1,0:T(8,128)(2,1)S(1)}, u32[]{:S(2)}, u32[]{:S(2)}) async-start(bf16[8,32,1024]{2,1,0:T(8,128)(2,1)} %get-tuple-element.12.after), calls=%async_computation | async-start | bytes 1048576 | tf_op jit(solution)/shard_map/all_to_all | solution.py:308
  45.1 0.0 copy-start.2
  45.1 9.9 %collective-permute-start = (bf16[16,16,640]{2,1,0:T(8,128)(2,1)S(1)}, bf16[16,16,640]{2,1,0:T(8,128)(2,1)S(1)}, u32[]{:S(2)}, u32[]{:S(2)}) collective-permute-start(bf16[16,16,640]{2,1,0:T(8,128)(2,1)S(1)} %slice.4), channel_id=1, source_target_pairs={{0,1},{1,0},{2,3},{3,2},{4,5},{5,4},{6,7},{7,6},{8,9},{9,8},{10,11... | collective-permute-start | bytes 983048 | tf_op jit(solution)/shard_map/ppermute | solution.py:309
  55.0 0.0 copy-done.1
  55.1 1.1 %keys.1 = (bf16[512,640]{1,0:T(8,128)(2,1)S(1)}, bf16[32,640]{1,0:T(8,128)(2,1)S(1)}) custom-call(bf16[16,48,640]{2,1,0:T(8,128)(2,1)S(1)} %bitcast.7, bf16[32,640]{1,0:T(8,128)(2,1)S(1)} %bitcast.12, bf16[640,640]{1,0:T(8,128)(2,1)S(1)} %copy-done.1, bf16[8,32,1024]{2,1,0:T(8,128)(2,1)} %get-tuple-element.12.after), custom_call_target="tpu_custom_call" | custom-call | flops 1000000000 | tf_op jit(solution)/shard_map/keys/pallas_call | solution.py:314
  56.1 0.0 copy-done.2
  56.2 1.1 %values.1 = (bf16[512,640]{1,0:T(8,128)(2,1)S(1)}, bf16[32,640]{1,0:T(8,128)(2,1)S(1)}) custom-call(bf16[16,48,640]{2,1,0:T(8,128)(2,1)S(1)} %bitcast.8, bf16[32,640]{1,0:T(8,128)(2,1)S(1)} %bitcast.13, bf16[640,640]{1,0:T(8,128)(2,1)S(1)} %copy-done.2, bf16[512,640]{1,0:T(8,128)(2,1)S(1)} %get-tuple-element.13.after.all_keys), custom_call_target="tpu_custom_call" | custom-call | flops 1000000000 | tf_op jit(solution)/shard_map/values/pallas_call | solution.py:314
  57.3 0.6 fresh.1
  57.8 0.0 collective-permute-done.other
  57.8 0.0 all-to-all-done.sent
  57.8 0.0 copy-start.3
  57.9 2.5 %attend.1 = bf16[8,32,1024]{2,1,0:T(8,128)(2,1)S(1)} custom-call(bf16[8,32,1024]{2,1,0:T(8,128)(2,1)S(1)} %all-to-all-done.sent, bf16[512,640]{1,0:T(8,128)(2,1)S(1)} %get-tuple-element.13.after.all_keys, bf16[512,640]{1,0:T(8,128)(2,1)S(1)} %get-tuple-element.14.all_values, bf16[16,48,640]{2,1,0:T(8,128)(2,1)S(1)} %bitcast.9, ...), custom_call_target="tpu_custom_call" | custom-call | flops 3000000000 | tf_op jit(solution)/shard_map/attend/pallas_call | solution.py:331
  60.4 17.2 %all_to_all.10.partial = bf16[8,32,1024]{2,1,0:T(8,128)(2,1)S(1)} all-to-all(bf16[8,32,1024]{2,1,0:T(8,128)(2,1)S(1)} %attend.1), channel_id=1, replica_groups=mesh['z'=16,'yh'=2,'x'=4,'yl'=2,'core'=2] {'yh','x'}, dimensions={0} | all-to-all | bytes 1048576 | tf_op jit(solution)/shard_map/all_to_all | solution.py:338
  77.6 1.6 %finish.1 = (bf16[32,640]{1,0:T(8,128)(2,1)}, bf16[32,320]{1,0:T(8,128)(2,1)}) custom-call(bf16[8,32,1024]{2,1,0:T(8,128)(2,1)S(1)} %all_to_all.10.partial, f32[32,640]{1,0:T(8,128)S(1)} %get-tuple-element.19.fresh, f32[32,128]{1,0:T(8,128)S(1)} %get-tuple-element.18.after.fresh_stats, bf16[640,640]{1,0:T(8,128)(2,1)S(1)} %copy-done.3), custom_call_target="tpu_custom_call" | custom-call | flops 2000000000 | tf_op jit(solution)/shard_map/finish/pallas_call | solution.py:340
  (7 shorter events, 0.0 us)
Async XLA Ops:
  0.6 0.8 %copy-start.4 = (bf16[9,5,320]{2,1,0:T(8,128)(2,1)S(1)}, bf16[9,5,320]{2,1,0:T(8,128)(2,1)}, u32[]{:S(2)}) copy-start(bf16[9,5,320]{2,1,0:T(8,128)(2,1)} %taps_hbm.1) | copy-start | bytes 86404
  0.6 0.8 %copy-start.5 = (bf16[1,32,640]{2,1,0:T(8,128)(2,1)S(1)}, bf16[1,32,640]{2,1,0:T(8,128)(2,1)}, u32[]{:S(2)}) copy-start(bf16[1,32,640]{2,1,0:T(8,128)(2,1)} %param.9) | copy-start | bytes 122884
  1.4 35.4 %copy-start = (bf16[640,640]{1,0:T(8,128)(2,1)S(1)}, bf16[640,640]{1,0:T(8,128)(2,1)}, u32[]{:S(2)}) copy-start(bf16[640,640]{1,0:T(8,128)(2,1)} %wq.1) | copy-start | bytes 2457604
  1.4 35.4 %copy-start.6 = (bf16[1,32,640]{2,1,0:T(8,128)(2,1)S(1)}, bf16[1,32,640]{2,1,0:T(8,128)(2,1)}, u32[]{:S(2)}) copy-start(bf16[1,32,640]{2,1,0:T(8,128)(2,1)} %param.8) | copy-start | bytes 122884
  1.5 35.4 %copy-start.7 = (bf16[640,1024]{1,0:T(8,128)(2,1)S(1)}, bf16[640,1024]{1,0:T(8,128)(2,1)}, u32[]{:S(2)}) copy-start(bf16[640,1024]{1,0:T(8,128)(2,1)} %constant.2.clone.slices) | copy-start | bytes 3932164
  38.3 16.8 %copy-start.1 = (bf16[640,640]{1,0:T(8,128)(2,1)S(1)}, bf16[640,640]{1,0:T(8,128)(2,1)}, u32[]{:S(2)}) copy-start(bf16[640,640]{1,0:T(8,128)(2,1)} %weight.2) | copy-start | bytes 2457604
  38.3 19.5 %all-to-all-start = ((bf16[8,32,1024]{2,1,0:T(8,128)(2,1)}), bf16[8,32,1024]{2,1,0:T(8,128)(2,1)S(1)}, u32[]{:S(2)}, u32[]{:S(2)}) async-start(bf16[8,32,1024]{2,1,0:T(8,128)(2,1)} %get-tuple-element.12.after), calls=%async_computation | async-start | bytes 1048576 | tf_op jit(solution)/shard_map/all_to_all | solution.py:308
  45.1 11.0 %copy-start.2 = (bf16[640,640]{1,0:T(8,128)(2,1)S(1)}, bf16[640,640]{1,0:T(8,128)(2,1)}, u32[]{:S(2)}) copy-start(bf16[640,640]{1,0:T(8,128)(2,1)} %weight.3) | copy-start | bytes 2457604
  45.1 12.7 %collective-permute-start = (bf16[16,16,640]{2,1,0:T(8,128)(2,1)S(1)}, bf16[16,16,640]{2,1,0:T(8,128)(2,1)S(1)}, u32[]{:S(2)}, u32[]{:S(2)}) collective-permute-start(bf16[16,16,640]{2,1,0:T(8,128)(2,1)S(1)} %slice.4), channel_id=1, source_target_pairs={{0,1},{1,0},{2,3},{3,2},{4,5},{5,4},{6,7},{7,6},{8,9},{9,8},{10,11... | collective-permute-start | bytes 983048 | tf_op jit(solution)/shard_map/ppermute | solution.py:309
  57.8 19.8 %copy-start.3 = (bf16[640,640]{1,0:T(8,128)(2,1)S(1)}, bf16[640,640]{1,0:T(8,128)(2,1)}, u32[]{:S(2)}) copy-start(bf16[640,640]{1,0:T(8,128)(2,1)} %wo.1) | copy-start | bytes 2457604

commit v10 on v9

--- a/solution.py
+++ b/solution.py
@@ -19,7 +19,9 @@
 PAIRS = HEADS // 2
 QUERIES = GROUP * COLS
 KEYS = Z * COLS
-SEND = D + 3 * LANES
+SLICE = Z * OWN
+FREE = LANES - SLICE
+SEND = D + 2 * LANES
 BACK = D + 3 * LANES
 VMEM = 24 * 1024 * 1024
 PAYLOAD, PREPARE, PROJECT, ATTEND, FRESH, FINISH = 1, 2, 1, 3, 0.2, 2
@@ -34,16 +36,17 @@
     for j in range(GROUP):
         for z in range(Z):
             for c in range(OWN):
-                out[(z * GROUP + j) * OWN + c, LANES * j + 8 * z + c] = 1.0
+                out[(z * GROUP + j) * OWN + c, LANES * j + OWN * z + c] = 1.0
     return out.astype(ml_dtypes.bfloat16)
 
 
 def tap_matrix():
     row = lax.broadcasted_iota(jnp.int32, (3 * LANES, 2 * LANES), 0)
     col = lax.broadcasted_iota(jnp.int32, (3 * LANES, 2 * LANES), 1)
-    z, c = (row % LANES) // 8, row % 8
-    target = 16 * z + OWN * (row // LANES) + c
-    return jnp.where((c < OWN) & (col == target), 1.0, 0.0).astype(BF16)
+    lane = row % LANES
+    z, tap = col // 16, col % 16 - OWN * (row // LANES)
+    hit = (tap >= 0) & (tap < OWN) & (lane == OWN * z + tap) & (lane < SLICE)
+    return jnp.where(hit, 1.0, 0.0).astype(BF16)
 
 
 def layer_norm(values_in):
@@ -109,13 +112,18 @@
     three = jnp.concatenate(
         [silu(block[...].astype(F32)), silu(stale.astype(F32)), silu(halo)], axis=0
     )
-    cut = dot(three, slices[...]).astype(BF16)
-    for j in range(GROUP):
-        send[j, :, :D] = query
-        for part in range(3):
-            send[j, :, D + part * LANES : D + (part + 1) * LANES] = cut[
-                part * COLS : (part + 1) * COLS, j * LANES : (j + 1) * LANES
-            ]
+    cut = dot(three, slices[...])
+    lanes = lane_ids(COLS)
+    for to in range(GROUP):
+        at = slice(to * LANES, (to + 1) * LANES)
+        active, before, rim = (cut[part * COLS : (part + 1) * COLS, at] for part in range(3))
+        send[to, :, :D] = query
+        send[to, :, D : D + LANES] = jnp.where(
+            lanes < SLICE, active, pltpu.roll(rim, SLICE, 1)
+        ).astype(BF16)
+        send[to, :, D + LANES :] = jnp.where(
+            lanes < SLICE, before, pltpu.roll(rim, SLICE - FREE, 1)
+        ).astype(BF16)
 
 
 def project_kernel(gathered, block, weight, after, out, own):
@@ -150,9 +158,15 @@
     upper_half = jnp.where(zero_core, theirs, mine)
     weights = (lower_half[:, :CO], lower_half[:, CO:], upper_half[:, :CO])
     active = sent[:, :, D : D + LANES]
-    stale = sent[:, :, D + LANES : D + 2 * LANES]
-    upper = jnp.concatenate([sent[7:8, :, D + 2 * LANES :], stale[:7]], axis=0)
-    lower = jnp.concatenate([stale[1:], sent[0:1, :, D + 2 * LANES :]], axis=0)
+    stale = sent[:, :, D + LANES :]
+
+    def rim(member):
+        first = pltpu.roll(active[member].astype(F32), FREE, 1)
+        rest = pltpu.roll(stale[member].astype(F32), LANES - (SLICE - FREE), 1)
+        return jnp.where(lane_ids(COLS) < FREE, first, rest).astype(BF16)[None]
+
+    upper = jnp.concatenate([rim(GROUP - 1), stale[:7]], axis=0)
+    lower = jnp.concatenate([stale[1:], rim(0)], axis=0)
     column = lax.broadcasted_iota(jnp.int32, (QUERIES, LANES), 0) % COLS
     total = jnp.zeros((QUERIES, CO), F32)
     for dy, source in enumerate((upper, active, lower)):

time: 79.6 us -> 79.7 us (level)
  no operation moved by 1% of the time
where the time goes in v10:
time: 79.7 us; the launch traced here: 79.4 us
  blocking collectives  52.5 us (66%)
  starting transfers between devices  16.7 us (21%)
  Pallas kernels  8.58 us (11%)
  local copies, waits for them, and re-layouts  0.85 us (1%)
    all_gather x1, blocking collectives, local(): gathered = lax.all_gather(payload, 'z', axis=0)  35.1 us
    all_to_all x1, blocking collectives, local(): partial = lax.all_to_all(back, ('yh', 'x'), 0, 0, tiled=True)  17.4 us
    ppermute x1, starting transfers between devices, local(): other = lax.ppermute(gathered[:, COLS:, :], 'core', [(0, 1), (1, 0)])  9.92 us
    all_to_all x1, starting transfers between devices, local(): sent = lax.all_to_all(send, ('yh', 'x'), 0, 0, tiled=True)  6.78 us
    pallas_call x1, Pallas kernels, local(): pl.pallas_call(attend_kernel, out_shape=shape((GROUP, COLS, BACK)), in_sp...  2.52 us
    pallas_call x2, Pallas kernels, local(): pl.pallas_call(project_kernel, out_shape=(shape((KEYS, D)), shape((COLS,...  2.18 us
    pallas_call x1, Pallas kernels, local(): pl.pallas_call(finish_kernel, out_shape=(shape((COLS, D)), shape((COLS, C...  1.6 us
  transfers between devices with their start and end apart: 2, of which 0 were waited for; matrix products, arithmetic and copies ran while one was open for 0% of the time, Pallas kernels for 3%

profile of v10, /device:TPU:1, one launch (start us, length us, event | category | flops | bytes accessed | tf_op | source)
XLA Modules:
  0.0 79.4 jit_solution(907647806213611508)
XLA Ops:
  0.6 0.0 copy-start.4
  0.6 0.0 copy-start.5
  0.7 0.8 copy-done.4
  1.4 0.0 copy-done.5
  1.5 0.2 payload.1
  1.7 35.1 %all-gather = bf16[768,640]{1,0:T(8,128)(2,1)S(1)} all-gather(bf16[48,640]{1,0:T(8,128)(2,1)S(1)} %payload.1), channel_id=2, replica_groups=mesh['z'=16,'yh'=2,'x'=4,'yl'=2,'core'=2] {'z'}, dimensions={0}, use_global_device_ids=true | all-gather | bytes 1044480 | tf_op jit(solution)/shard_map/all_gather | solution.py:314
  36.8 0.0 copy-done
  36.8 0.0 copy-done.6
  36.8 0.0 copy-done.7
  36.9 1.5 %prepare.1 = (bf16[8,32,896]{2,1,0:T(8,128)(2,1)}, bf16[32,640]{1,0:T(8,128)(2,1)S(1)}) custom-call(bf16[32,640]{1,0:T(8,128)(2,1)S(1)} %bitcast.11, bf16[16,48,640]{2,1,0:T(8,128)(2,1)S(1)} %bitcast.5, bf16[640,640]{1,0:T(8,128)(2,1)S(1)} %copy-done, bf16[640,1024]{1,0:T(8,128)(2,1)S(1)} %copy-done.7), custom_call_target="tpu_custom_call" | custom-call | flops 2000000000 | tf_op jit(solution)/shard_map/prepare/pallas_call | solution.py:316
  38.3 6.8 %all-to-all-start = ((bf16[8,32,896]{2,1,0:T(8,128)(2,1)}), bf16[8,32,896]{2,1,0:T(8,128)(2,1)S(1)}, u32[]{:S(2)}, u32[]{:S(2)}) async-start(bf16[8,32,896]{2,1,0:T(8,128)(2,1)} %get-tuple-element.12.after), calls=%async_computation | async-start | bytes 917504 | tf_op jit(solution)/shard_map/all_to_all | solution.py:322
  45.1 0.0 copy-start.2
  45.1 9.9 %collective-permute-start = (bf16[16,16,640]{2,1,0:T(8,128)(2,1)S(1)}, bf16[16,16,640]{2,1,0:T(8,128)(2,1)S(1)}, u32[]{:S(2)}, u32[]{:S(2)}) collective-permute-start(bf16[16,16,640]{2,1,0:T(8,128)(2,1)S(1)} %slice.4), channel_id=1, source_target_pairs={{0,1},{1,0},{2,3},{3,2},{4,5},{5,4},{6,7},{7,6},{8,9},{9,8},{10,11... | collective-permute-start | bytes 983048 | tf_op jit(solution)/shard_map/ppermute | solution.py:323
  55.1 0.0 copy-done.1
  55.1 1.1 %keys.1 = (bf16[512,640]{1,0:T(8,128)(2,1)S(1)}, bf16[32,640]{1,0:T(8,128)(2,1)S(1)}) custom-call(bf16[16,48,640]{2,1,0:T(8,128)(2,1)S(1)} %bitcast.7, bf16[32,640]{1,0:T(8,128)(2,1)S(1)} %bitcast.12, bf16[640,640]{1,0:T(8,128)(2,1)S(1)} %copy-done.1, bf16[8,32,896]{2,1,0:T(8,128)(2,1)} %get-tuple-element.12.after), custom_call_target="tpu_custom_call" | custom-call | flops 1000000000 | tf_op jit(solution)/shard_map/keys/pallas_call | solution.py:328
  56.2 0.0 copy-done.2
  56.2 1.1 %values.1 = (bf16[512,640]{1,0:T(8,128)(2,1)S(1)}, bf16[32,640]{1,0:T(8,128)(2,1)S(1)}) custom-call(bf16[16,48,640]{2,1,0:T(8,128)(2,1)S(1)} %bitcast.8, bf16[32,640]{1,0:T(8,128)(2,1)S(1)} %bitcast.13, bf16[640,640]{1,0:T(8,128)(2,1)S(1)} %copy-done.2, bf16[512,640]{1,0:T(8,128)(2,1)S(1)} %get-tuple-element.13.after.all_keys), custom_call_target="tpu_custom_call" | custom-call | flops 1000000000 | tf_op jit(solution)/shard_map/values/pallas_call | solution.py:328
  57.3 0.6 fresh.1
  57.9 0.0 collective-permute-done.other
  57.9 0.0 all-to-all-done.sent
  57.9 0.0 copy-start.3
  57.9 2.5 %attend.1 = bf16[8,32,1024]{2,1,0:T(8,128)(2,1)S(1)} custom-call(bf16[8,32,896]{2,1,0:T(8,128)(2,1)S(1)} %all-to-all-done.sent, bf16[512,640]{1,0:T(8,128)(2,1)S(1)} %get-tuple-element.13.after.all_keys, bf16[512,640]{1,0:T(8,128)(2,1)S(1)} %get-tuple-element.14.all_values, bf16[16,48,640]{2,1,0:T(8,128)(2,1)S(1)} %bitcast.9, ...), custom_call_target="tpu_custom_call" | custom-call | flops 3000000000 | tf_op jit(solution)/shard_map/attend/pallas_call | solution.py:345
  60.4 17.4 %all_to_all.10.partial = bf16[8,32,1024]{2,1,0:T(8,128)(2,1)S(1)} all-to-all(bf16[8,32,1024]{2,1,0:T(8,128)(2,1)S(1)} %attend.1), channel_id=1, replica_groups=mesh['z'=16,'yh'=2,'x'=4,'yl'=2,'core'=2] {'yh','x'}, dimensions={0} | all-to-all | bytes 1048576 | tf_op jit(solution)/shard_map/all_to_all | solution.py:352
  77.8 1.6 %finish.1 = (bf16[32,640]{1,0:T(8,128)(2,1)}, bf16[32,320]{1,0:T(8,128)(2,1)}) custom-call(bf16[8,32,1024]{2,1,0:T(8,128)(2,1)S(1)} %all_to_all.10.partial, f32[32,640]{1,0:T(8,128)S(1)} %get-tuple-element.19.fresh, f32[32,128]{1,0:T(8,128)S(1)} %get-tuple-element.18.after.fresh_stats, bf16[640,640]{1,0:T(8,128)(2,1)S(1)} %copy-done.3), custom_call_target="tpu_custom_call" | custom-call | flops 2000000000 | tf_op jit(solution)/shard_map/finish/pallas_call | solution.py:354
  (7 shorter events, 0.0 us)
Async XLA Ops:
  0.6 0.8 %copy-start.4 = (bf16[9,5,320]{2,1,0:T(8,128)(2,1)S(1)}, bf16[9,5,320]{2,1,0:T(8,128)(2,1)}, u32[]{:S(2)}) copy-start(bf16[9,5,320]{2,1,0:T(8,128)(2,1)} %taps_hbm.1) | copy-start | bytes 86404
  0.6 0.8 %copy-start.5 = (bf16[1,32,640]{2,1,0:T(8,128)(2,1)S(1)}, bf16[1,32,640]{2,1,0:T(8,128)(2,1)}, u32[]{:S(2)}) copy-start(bf16[1,32,640]{2,1,0:T(8,128)(2,1)} %param.9) | copy-start | bytes 122884
  1.4 35.4 %copy-start = (bf16[640,640]{1,0:T(8,128)(2,1)S(1)}, bf16[640,640]{1,0:T(8,128)(2,1)}, u32[]{:S(2)}) copy-start(bf16[640,640]{1,0:T(8,128)(2,1)} %wq.1) | copy-start | bytes 2457604
  1.4 35.4 %copy-start.6 = (bf16[1,32,640]{2,1,0:T(8,128)(2,1)S(1)}, bf16[1,32,640]{2,1,0:T(8,128)(2,1)}, u32[]{:S(2)}) copy-start(bf16[1,32,640]{2,1,0:T(8,128)(2,1)} %param.8) | copy-start | bytes 122884
  1.5 35.4 %copy-start.7 = (bf16[640,1024]{1,0:T(8,128)(2,1)S(1)}, bf16[640,1024]{1,0:T(8,128)(2,1)}, u32[]{:S(2)}) copy-start(bf16[640,1024]{1,0:T(8,128)(2,1)} %constant.2.clone.slices) | copy-start | bytes 3932164
  38.3 16.8 %copy-start.1 = (bf16[640,640]{1,0:T(8,128)(2,1)S(1)}, bf16[640,640]{1,0:T(8,128)(2,1)}, u32[]{:S(2)}) copy-start(bf16[640,640]{1,0:T(8,128)(2,1)} %weight.2) | copy-start | bytes 2457604
  38.3 19.5 %all-to-all-start = ((bf16[8,32,896]{2,1,0:T(8,128)(2,1)}), bf16[8,32,896]{2,1,0:T(8,128)(2,1)S(1)}, u32[]{:S(2)}, u32[]{:S(2)}) async-start(bf16[8,32,896]{2,1,0:T(8,128)(2,1)} %get-tuple-element.12.after), calls=%async_computation | async-start | bytes 917504 | tf_op jit(solution)/shard_map/all_to_all | solution.py:322
  45.1 11.0 %copy-start.2 = (bf16[640,640]{1,0:T(8,128)(2,1)S(1)}, bf16[640,640]{1,0:T(8,128)(2,1)}, u32[]{:S(2)}) copy-start(bf16[640,640]{1,0:T(8,128)(2,1)} %weight.3) | copy-start | bytes 2457604
  45.1 12.7 %collective-permute-start = (bf16[16,16,640]{2,1,0:T(8,128)(2,1)S(1)}, bf16[16,16,640]{2,1,0:T(8,128)(2,1)S(1)}, u32[]{:S(2)}, u32[]{:S(2)}) collective-permute-start(bf16[16,16,640]{2,1,0:T(8,128)(2,1)S(1)} %slice.4), channel_id=1, source_target_pairs={{0,1},{1,0},{2,3},{3,2},{4,5},{5,4},{6,7},{7,6},{8,9},{9,8},{10,11... | collective-permute-start | bytes 983048 | tf_op jit(solution)/shard_map/ppermute | solution.py:323
  57.9 19.9 %copy-start.3 = (bf16[640,640]{1,0:T(8,128)(2,1)S(1)}, bf16[640,640]{1,0:T(8,128)(2,1)}, u32[]{:S(2)}) copy-start(bf16[640,640]{1,0:T(8,128)(2,1)} %wo.1) | copy-start | bytes 2457604
